TPU v7x, 32 devices: a whole 2x2x4 slice. The times are simulated.
32 devices in a mesh: groups: 2 (over x), dp: 8 (over z, y), tensor: 2 (over core).
Axes of the slice: x: 2, y: 2, z: 4, core: 2. Of those that a mesh axis runs over, the one named last changes fastest.
Arguments:
- hidden: bfloat16 [8192, 6144], P(('groups', 'dp'), 'tensor'), parts along dimension 0, may hold values from -320 to 320
- attn_out: bfloat16 [8192, 6144], P(('groups', 'dp'), 'tensor'), parts along dimension 0, may hold values from -6 to 6
- step_ids: int32 [8192], P(('groups', 'dp')), parts along dimension 0, may hold values from 0 to 7
- modulation: float32 [16, 2, 6144], P('groups'), parts along dimension 0, may hold values from -3 to 3
Outputs:
- hessian_qkv: float32 [2048, 6144], P(('groups', 'dp', 'tensor')), parts along dimension 0
- hessian_out: float32 [2048, 6144], P(('groups', 'dp', 'tensor')), parts along dimension 0
There are 2 independent parts, one for each index of `groups`. A program takes and returns all parts, laid end to end along the dimension named above; each array names one. Nothing has to cross between parts.
All inputs are finite; a program needn't handle non-finite values.
Results may differ from a plain program's by a relative error of at most 0.00076.
Values may be sent and summed in bfloat16 or wider, within the bound.
No kernel may reach another device: no remote copies, remote signals or barrier semaphores. Data moves between devices by JAX's collectives and lax.ppermute only.
A program may use at most 128 MiB of HBM per device.

v0:
```python
import jax
import jax.numpy as jnp
from jax import lax
from jax.sharding import PartitionSpec as P

ROW_DEV = 512


epsilon = 1e-06


def lookup_table(step_ids, table):
    steps = table.shape[0]
    columns = table.shape[2]
    onehot = (step_ids[:, None] == jnp.arange(steps, dtype=jnp.int32)[None, :]).astype(jnp.float32)
    looked = jnp.dot(onehot, table.reshape(steps, 2 * columns), precision=lax.Precision.HIGHEST)
    return (looked[:, :columns], looked[:, columns:])


def gram_rows(window, full):
    return lax.dot_general(
        window, full, (((0,), (0,)), ((), ())), preferred_element_type=jnp.float32
    )


def body(hidden, attn_out, step_ids, modulation):
    token_count = hidden.shape[0]
    local_width = hidden.shape[1]
    parts_tp = lax.axis_size("tensor")
    parts_dp = lax.axis_size("dp")
    width = local_width * parts_tp
    rows_dev = ROW_DEV
    factor = 2.0 / (token_count * parts_dp)
    column_start = lax.axis_index("tensor") * local_width
    local_table = lax.dynamic_slice_in_dim(modulation, column_start, local_width, 2)
    scale, shift = lookup_table(step_ids, local_table)
    values = hidden.astype(jnp.float32)
    moments = lax.psum((jnp.sum(values, axis=1), jnp.sum(values * values, axis=1)), "tensor")
    mean = (moments[0] / width)[:, None]
    meansq = (moments[1] / width)[:, None]
    normed = (values - mean) * lax.rsqrt(meansq - mean * mean + epsilon)
    local_mod = (normed * (1.0 + scale) + shift).astype(jnp.bfloat16)
    full_mod, full_attn = (
        lax.all_gather(local_mod, "tensor", axis=1, tiled=True),
        lax.all_gather(attn_out, "tensor", axis=1, tiled=True),
    )
    part_qkv = gram_rows(local_mod[:, :rows_dev], full_mod)
    part_out = gram_rows(attn_out[:, :rows_dev], full_attn)
    summed_qkv, summed_out = (
        lax.psum_scatter(part_qkv, "dp", scatter_dimension=0, tiled=True),
        lax.psum_scatter(part_out, "dp", scatter_dimension=0, tiled=True),
    )
    return (summed_qkv * factor, summed_out * factor)


def solution(mesh):
    return jax.shard_map(
        body,
        mesh=mesh,
        in_specs=(
            P(("groups", "dp"), "tensor"),
            P(("groups", "dp"), "tensor"),
            P(("groups", "dp")),
            P("groups", None, None),
        ),
        out_specs=(P(("groups", "dp", "tensor"), None), P(("groups", "dp", "tensor"), None)),
        check_vma=False,
    )
```

profile of v0, /device:TPU:0, one launch (start us, length us, event | category | flops | bytes accessed | tf_op | source)
XLA Modules:
  0.0 492.9 jit_solution(2037250032173726708)
XLA Ops:
  7.2 0.0 copy-start
  7.2 0.0 all-gather.3.cloned.1.call-start
  7.2 2.9 convert_reduce_fusion
  10.2 0.0 copy-done
  10.2 0.1 copy.6
  10.3 2.6 all-reduce
  12.9 0.0 copy-start.1
  12.9 6.0 %fusion.9 = f32[512,6144]{1,0:T(8,128)S(1)} fusion(f32[8,6144]{1,0:T(8,128)S(1)} %bitcast.6, s32[512]{0:T(512)} %param.6), kind=kOutput, calls=%fused_computation.16 | convolution fusion | flops 301993984 | bytes 12781568 | tf_op jit(solution)/shard_map/dot_general | solution.py:16
  18.9 0.0 copy-done.1
  18.9 3.7 fusion.3
  22.7 0.0 all-gather.3.cloned.1.call-update
  22.7 0.0 all-gather.5.cloned.1.call-start
  22.7 0.7 all-gather.5.cloned.1.call-update
  23.4 0.0 reduce-scatter.3.cloned.1.call-start
  23.5 18.7 %all-gather.3.cloned.1.call-done = bf16[512,6144]{1,0:T(8,128)(2,1)} async-done(((bf16[512,3072]{1,0:T(8,128)(2,1)}), bf16[512,6144]{1,0:T(8,128)(2,1)}) %all-gather.3.cloned.1.call-update) | async-done | bytes 6291472 | tf_op jit(solution)/shard_map/all_gather | solution.py:44
  42.2 12.3 %fusion.5 = f32[512,6144]{1,0:T(8,128)} fusion(bf16[512,6144]{1,0:T(8,128)(2,1)} %all-gather.3.cloned.1.call-done, bf16[512,3072]{1,0:T(8,128)(2,1)} %fusion.3), kind=kOutput, calls=%fused_computation.11 | convolution fusion | flops 3221225472 | bytes 19398656 | tf_op jit(solution)/shard_map/dot_general | solution.py:21
  54.5 0.0 reduce-scatter.3.cloned.1.call-update
  54.5 0.2 reduce-scatter.5.cloned.1.call-start
  54.7 7.0 %all-gather.5.cloned.1.call-done = bf16[512,6144]{1,0:T(8,128)(2,1)} async-done(((bf16[512,3072]{1,0:T(8,128)(2,1)}), bf16[512,6144]{1,0:T(8,128)(2,1)}) %all-gather.5.cloned.1.call-update) | async-done | bytes 6291472 | tf_op jit(solution)/shard_map/all_gather | solution.py:45
  61.7 10.9 %fusion.7 = f32[512,6144]{1,0:T(8,128)} fusion(bf16[512,6144]{1,0:T(8,128)(2,1)} %all-gather.5.cloned.1.call-done, bf16[512,3072]{1,0:T(8,128)(2,1)} %param.5), kind=kOutput, calls=%fused_computation.13 | convolution fusion | flops 3221225472 | bytes 19398656 | tf_op jit(solution)/shard_map/dot_general | solution.py:21
  72.6 0.0 reduce-scatter.5.cloned.1.call-update
  72.7 201.2 %reduce-scatter.3.cloned.1.call-done = f32[64,6144]{1,0:T(8,128)} async-done(((f32[512,6144]{1,0:T(8,128)}), f32[64,6144]{1,0:T(8,128)}) %reduce-scatter.3.cloned.1.call-update) | async-done | bytes 1572880 | tf_op jit(solution)/shard_map/reduce_scatter | solution.py:50
  273.8 2.7 broadcast_multiply_fusion.1
  276.5 207.2 %reduce-scatter.5.cloned.1.call-done = f32[64,6144]{1,0:T(8,128)} async-done(((f32[512,6144]{1,0:T(8,128)}), f32[64,6144]{1,0:T(8,128)}) %reduce-scatter.5.cloned.1.call-update) | async-done | bytes 1572880 | tf_op jit(solution)/shard_map/reduce_scatter | solution.py:51
  483.7 2.7 broadcast_multiply_fusion
  (2 shorter events, 0.0 us)
Async XLA Ops:
  7.2 3.0 copy-start
  7.2 35.0 %all-gather.3.cloned.1.call-start = ((), (), s32[]{:S(2)}) async-start(), calls=%async_computation.2 | async-start | bytes 9437184 | tf_op jit(solution)/shard_map/all_gather | solution.py:44
  12.9 6.0 %copy-start.1 = (bf16[512,3072]{1,0:T(8,128)(2,1)S(1)}, bf16[512,3072]{1,0:T(8,128)(2,1)}, u32[]{:S(2)}) copy-start(bf16[512,3072]{1,0:T(8,128)(2,1)} %param.4) | copy-start | bytes 9437188
  22.7 39.0 %all-gather.5.cloned.1.call-start = ((), (), s32[]{:S(2)}) async-start(), calls=%async_computation.4 | async-start | bytes 9437184 | tf_op jit(solution)/shard_map/all_gather | solution.py:45
  23.4 250.4 %reduce-scatter.3.cloned.1.call-start = ((), (), s32[]{:S(2)}) async-start(), calls=%async_computation.3 | async-start | bytes 14155776 | tf_op jit(solution)/shard_map/reduce_scatter | solution.py:50
  54.5 429.3 %reduce-scatter.5.cloned.1.call-start = ((), (), s32[]{:S(2)}) async-start(), calls=%async_computation.5 | async-start | bytes 14155776 | tf_op jit(solution)/shard_map/reduce_scatter | solution.py:51
Sparse Core Ops, SparseCore 0:
  22.8 19.3 all-gather.2
  43.7 17.9 all-gather.4
  65.3 208.4 reduce-scatter.2
  277.3 206.4 reduce-scatter.4
where the time goes:
time: 493 us
  waiting for transfers between devices  435 us (88%)
  matrix products  29.2 us (6%)
  between operations  13.8 us (3%)
  other arithmetic  12 us (2%)
    reduce_scatter x1, waiting for transfers between devices, body(): lax.psum_scatter(part_out, 'dp', scatter_dimension=0, tiled=True)  207 us
    reduce_scatter x1, waiting for transfers between devices, body(): lax.psum_scatter(part_qkv, 'dp', scatter_dimension=0, tiled=True)  201 us
    dot_general x2, matrix products, gram_rows(): lax.dot_general(window, full, (((0,), (0,)), ((), ())), preferred_element...  23.2 us
    all_gather x1, waiting for transfers between devices, body(): lax.all_gather(local_mod, 'tensor', axis=1, tiled=True)  18.7 us
  transfers between devices with their start and end apart: 4, of which 4 were waited for; matrix products, arithmetic and copies ran while one was open for 5% of the time, Pallas kernels for 0%

commit v1 on v0

--- a/solution.py
+++ b/solution.py
@@ -1,9 +1,14 @@
+import functools
+
 import jax
 import jax.numpy as jnp
 from jax import lax
+from jax.experimental import pallas as pl
+from jax.experimental.pallas import tpu as pltpu
 from jax.sharding import PartitionSpec as P
 
 ROW_DEV = 512
+LANES = 256
 
 
 epsilon = 1e-06
@@ -23,7 +28,7 @@
     )
 
 
-def body(hidden, attn_out, step_ids, modulation):
+def plain_body(hidden, attn_out, step_ids, modulation):
     token_count = hidden.shape[0]
     local_width = hidden.shape[1]
     parts_tp = lax.axis_size("tensor")
@@ -53,9 +58,367 @@
     return (summed_qkv * factor, summed_out * factor)
 
 
+def swap(size, mask=1):
+    return [(i, i ^ mask) for i in range(size)]
+
+
+def cut(values, start, size, axis):
+    return lax.dynamic_slice_in_dim(values, start, size, axis)
+
+
+def half16(values):
+    return values.astype(jnp.float16)
+
+
+def full32(values):
+    return values.astype(jnp.float32)
+
+
+FREE = pl.CostEstimate(flops=0, bytes_accessed=0, transcendentals=0)
+
+
+def gridded(kernel, indices, grid, in_specs, out_specs, out_shape, *operands):
+    return pl.pallas_call(
+        kernel,
+        grid_spec=pltpu.PrefetchScalarGridSpec(
+            num_scalar_prefetch=1, grid=(grid,), in_specs=in_specs, out_specs=out_specs
+        ),
+        out_shape=out_shape,
+        cost_estimate=FREE,
+        compiler_params=pltpu.CompilerParams(vmem_limit_bytes=32 << 20),
+    )(indices, *operands)
+
+
+def vector(*entries):
+    return jnp.stack([jnp.asarray(entry, jnp.int32) for entry in entries])
+
+
+def pick_kernel(at, source, out):
+    out[...] = source[...]
+
+
+def pick(source, *blocks):
+    tokens = source.shape[0]
+    return gridded(
+        pick_kernel,
+        vector(*blocks),
+        len(blocks),
+        [pl.BlockSpec((tokens, LANES), lambda i, at: (0, at[i]))],
+        pl.BlockSpec((tokens, LANES), lambda i, at: (0, i)),
+        jax.ShapeDtypeStruct((tokens, LANES * len(blocks)), source.dtype),
+        source,
+    )
+
+
+def turn_kernel(at, source, out):
+    out[...] = source[...].T
+
+
+def turn(source, blocks):
+    tokens = source.shape[0]
+    size = ROW_DEV // len(blocks)
+    return gridded(
+        turn_kernel,
+        vector(*blocks),
+        len(blocks),
+        [pl.BlockSpec((tokens, size), lambda i, at: (0, at[i]))],
+        pl.BlockSpec((size, tokens), lambda i, at: (i, 0)),
+        jax.ShapeDtypeStruct((ROW_DEV, tokens), source.dtype),
+        source,
+    )
+
+
+def store_sums(total, out, peak):
+    out[...] = total
+    peak[...] = jnp.broadcast_to(jnp.max(jnp.abs(total), axis=0, keepdims=True), peak.shape)
+
+
+def gram_kernel(at, rows, columns, out, peak):
+    store_sums(jnp.dot(rows[...], columns[...], preferred_element_type=jnp.float32), out, peak)
+
+
+def gram_two_kernel(at, rows, columns, other_rows, other_columns, out, peak):
+    total = jnp.dot(rows[...], columns[...], preferred_element_type=jnp.float32)
+    total = total + jnp.dot(other_rows[...], other_columns[...], preferred_element_type=jnp.float32)
+    store_sums(total, out, peak)
+
+
+def gram(rows, columns, blocks, other=None):
+    tokens = columns.shape[0]
+    in_specs = [
+        pl.BlockSpec((ROW_DEV, tokens), lambda i, at: (0, 0)),
+        pl.BlockSpec((tokens, LANES), lambda i, at: (0, at[i])),
+    ]
+    operands = [rows, columns]
+    skip = 0
+    if other is not None:
+        other_rows, other_columns, skip = other
+        in_specs += [
+            pl.BlockSpec((ROW_DEV, tokens), lambda i, at: (0, 0)),
+            pl.BlockSpec((tokens, LANES), lambda i, at: (0, i + skip)),
+        ]
+        operands += [other_rows, other_columns]
+    width = LANES * len(blocks)
+    return gridded(
+        gram_kernel if other is None else gram_two_kernel,
+        vector(*blocks),
+        len(blocks),
+        in_specs,
+        [pl.BlockSpec((ROW_DEV, LANES), lambda i, at: (0, i)), pl.BlockSpec((8, LANES), lambda i, at: (0, i))],
+        [
+            jax.ShapeDtypeStruct((ROW_DEV, width), jnp.float32),
+            jax.ShapeDtypeStruct((8, width), jnp.float32),
+        ],
+        *operands,
+    )
+
+
+def modulate_kernel(ids, values, mean, gain, scale_table, shift_table, out):
+    tokens = values.shape[0]
+    steps = scale_table.shape[0]
+    place = lax.broadcasted_iota(jnp.int32, (tokens, 3 * steps), 1)
+    onehot = (ids[...] == lax.rem(place, steps)).astype(jnp.bfloat16)
+
+    def lookup(table):
+        entries = table[...]
+        pieces = []
+        for _ in range(3):
+            piece = entries.astype(jnp.bfloat16).astype(jnp.float32)
+            entries = entries - piece
+            pieces.append(piece)
+        split = jnp.concatenate(pieces, axis=0).astype(jnp.bfloat16)
+        return jnp.dot(onehot, split, preferred_element_type=jnp.float32)
+
+    normed = (values[...].astype(jnp.float32) - mean[...]) * gain[...]
+    out[...] = (normed * (1.0 + lookup(scale_table)) + lookup(shift_table)).astype(jnp.bfloat16)
+
+
+def modulate(values, mean, gain, step_ids, table):
+    tokens, width = values.shape
+    steps = table.shape[0]
+    size = 2 * LANES
+    whole = pl.BlockSpec((tokens, 1), lambda i: (0, 0))
+    columns = pl.BlockSpec((tokens, size), lambda i: (0, i))
+    entries = pl.BlockSpec((steps, size), lambda i: (0, i))
+    return pl.pallas_call(
+        modulate_kernel,
+        grid=(width // size,),
+        in_specs=[whole, columns, whole, whole, entries, entries],
+        out_specs=columns,
+        out_shape=jax.ShapeDtypeStruct(values.shape, jnp.bfloat16),
+        cost_estimate=FREE,
+        compiler_params=pltpu.CompilerParams(vmem_limit_bytes=32 << 20),
+    )(step_ids[:, None], values, mean, gain, table[:, 0], table[:, 1])
+
+
+INWARD = [(0, 2), (1, 3), (6, 4), (7, 5)]
+MIDDLE = [(2, 4), (3, 5), (4, 2), (5, 3)]
+OUTWARD = [(2, 0), (3, 1), (4, 6), (5, 7)]
+
+
+def packed(values, peak):
+    exponent = jnp.ceil(jnp.log2(jnp.maximum(peak, 1e-30))) - 15.0
+    scaled = values * jnp.exp2(-exponent)
+    tail = jnp.broadcast_to(exponent, (16, values.shape[1]))
+    return half16(jnp.concatenate([scaled, tail], axis=0))
+
+
+def unit(message):
+    return jnp.exp2(full32(message[-1:]))
+
+
+def unpacked(message, first, last):
+    return full32(message[first:last]) * unit(message)
+
+
+def reach(message):
+    return 32768.0 * unit(message)
+
+
+def pipeline(count, make_part, stage, early):
+    side = lax.axis_index("dp") % 2
+    place = lax.axis_index("dp") // 2
+    outer = (place == 0) | (place == 3)
+    part, peak, sent1, came1, came2, came3, came4, owned = {}, {}, {}, {}, {}, {}, {}, {}
+    done = []
+
+    def begin(k, raw):
+        part[k], peak[k] = make_part(k, raw)
+        peak[k] = peak[k][:1]
+        block = part[k].shape[0] // 4
+        sent1[k] = packed(part[k][: 3 * block], peak[k])
+        came1[k] = lax.ppermute(sent1[k], "dp", INWARD)
+
+    begin(0, stage(0))
+    begin(1, stage(1))
+    extra = early(sent1[1])
+    for k in range(count + 3):
+        held = [group[j] for group, j in ((came1, k), (came2, k - 1), (came3, k - 2), (came4, k - 3)) if 0 <= j < count]
+        if k + 1 < count:
+            held.append(sent1[k + 1])
+        if k == 0:
+            held.append(extra)
+        held = list(lax.optimization_barrier(tuple(held)))
+        if k == 0:
+            early(None, held.pop())
+        ahead = []
+        if k < count:
+            came1[k] = held.pop(0)
+            block = part[k].shape[0] // 4
+            total = part[k][: 2 * block] + unpacked(came1[k], 0, 2 * block)
+            sent = packed(total, peak[k] + reach(came1[k]))
+            ahead.append(sent)
+            came2[k] = lax.ppermute(sent, "dp", MIDDLE)
+        if 0 <= k - 1 < count:
+            j = k - 1
+            came2[j] = held.pop(0)
+            block = part[j].shape[0] // 4
+            total = part[j][2 * block : 3 * block] + unpacked(came2[j], block, 2 * block)
+            sent = packed(total, peak[j] + reach(came2[j]))
+            ahead.append(sent)
+            came3[j] = lax.ppermute(sent, "dp", OUTWARD)
+        if 0 <= k - 2 < count:
+            j = k - 2
+            came3[j] = held.pop(0)
+            block = part[j].shape[0] // 4
+            total = part[j][3 * block :] + unpacked(came1[j], 2 * block, 3 * block)
+            total = total + unpacked(came2[j], 0, block) + unpacked(came3[j], 0, block)
+            more = jnp.where(outer, reach(came3[j]), reach(came1[j]) + reach(came2[j]))
+            own = block // 2
+            owned[j] = cut(total, side * own, own, 0)
+            sent = packed(cut(total, (1 - side) * own, own, 0), peak[j] + more)
+            ahead.append(sent)
+            came4[j] = lax.ppermute(sent, "dp", swap(8))
+        if 0 <= k - 3 < count:
+            j = k - 3
+            done.append((owned[j], unpacked(held.pop(0), 0, owned[j].shape[0])))
+        if k + 2 < count:
+            raw, _ = lax.optimization_barrier((stage(k + 2), tuple(ahead)))
+            begin(k + 2, raw)
+    return done
+
+
+def in_order(own, other):
+    side = lax.axis_index("dp") % 2
+    return jnp.where(side == 0, own, other), jnp.where(side == 0, other, own)
+
+
+def assemble(done, shared, scale):
+    core = lax.axis_index("tensor")
+    half = ROW_DEV // 2
+    cores = []
+    for which in range(2):
+        mine = done[which::2]
+        pieces = []
+        if shared:
+            pieces.append(mine[0][0] + mine[0][1])
+            mine = mine[1:]
+        ordered = [in_order(*pair) for pair in mine]
+        head = [ordered[0][0][:, :half], ordered[0][1][:, :half]]
+        ordered[0] = (ordered[0][0][:, half:], ordered[0][1][:, half:])
+        pieces = head + pieces + [pair[0] for pair in ordered] + [pair[1] for pair in ordered]
+        cores.append(jnp.concatenate(pieces, axis=1))
+    left = jnp.where(core == 0, cores[0], cores[1])
+    right = jnp.where(core == 0, cores[1], cores[0])
+    return jnp.concatenate([left, right], axis=1) * scale
+
+
+def body(hidden, attn_out, step_ids, modulation):
+    token_count = hidden.shape[0]
+    local_width = hidden.shape[1]
+    parts_tp = lax.axis_size("tensor")
+    dp = lax.axis_size("dp")
+    width = local_width * parts_tp
+    tokens = token_count * dp
+    factor = 2.0 / tokens
+    column_start = lax.axis_index("tensor") * local_width
+    local_table = lax.dynamic_slice_in_dim(modulation, column_start, local_width, 2)
+    core_swap = swap(2)
+    side = lax.axis_index("dp") % 2
+    place = lax.axis_index("dp") // 2
+    blocks = local_width // LANES
+    store = {}
+
+    low = place < 2
+    order = [jnp.where(low, 2, 1), jnp.where(low, 3, 0), place ^ 1, place]
+    arrived = [jnp.where(index // 2 == side, 2 + index % 2, index % 2) for index in order]
+
+    def owned_blocks(which, common):
+        rest = (blocks - 2 - common) // 2
+        return [which] + [2 + common + which * rest + i for i in range(rest)]
+
+    common = 4
+    attn_mine = owned_blocks(side, common)
+    attn_theirs = owned_blocks(1 - side, common)
+    qkv_mine = owned_blocks(side, 0)
+    qkv_theirs = owned_blocks(1 - side, 0)
+    first = 4
+
+    shared = [2 + i for i in range(common)]
+    attn_far = lax.ppermute(attn_out, "tensor", core_swap)
+    attn_rows = turn(attn_out, order)
+    attn_pair = lax.ppermute(pick(attn_out, side, *attn_theirs), "dp", swap(dp))
+
+    def early(earlier, result=None):
+        if result is not None:
+            store["mod"] = result
+            return
+        values, _ = lax.optimization_barrier((hidden, earlier))
+        values32 = values.astype(jnp.float32)
+        moments = lax.psum((jnp.sum(values32, axis=1), jnp.sum(values32 * values32, axis=1)), "tensor")
+        mean = (moments[0] / width)[:, None]
+        meansq = (moments[1] / width)[:, None]
+        gain = lax.rsqrt(meansq - mean * mean + epsilon)
+        return modulate(values, mean, gain, step_ids, local_table)
+
+    def stage(k):
+        if k == 0:
+            return attn_out
+        if k == 1:
+            return attn_far
+        if k == 2:
+            return attn_pair, store["mod"]
+        if k in (4, 6):
+            return store["pair"]
+        return store["far"]
+
+    def make_part(k, raw):
+        if k < 2:
+            return gram(attn_rows, raw, shared)
+        if k == 2:
+            pair, mod = raw
+            store["far"] = lax.ppermute(pair, "tensor", core_swap)
+            store["other"] = turn(pair, arrived)
+            store["mod"] = mod
+            store["pair"] = lax.ppermute(pick(mod, side, *qkv_theirs[:first]), "dp", swap(dp))
+            store["mod_far"] = lax.ppermute(mod, "tensor", core_swap)
+            store["rows"] = turn(mod, order)
+            return gram(attn_rows, attn_out, attn_mine, (store["other"], pair, 1))
+        if k == 3:
+            return gram(attn_rows, attn_far, attn_mine, (store["other"], raw, 1))
+        if k == 4:
+            store["far"] = lax.ppermute(raw, "tensor", core_swap)
+            store["other"] = turn(raw, arrived)
+            mod, _ = lax.optimization_barrier((store["mod"], raw))
+            store["pair"] = lax.ppermute(pick(mod, *qkv_theirs[first:]), "dp", swap(dp))
+            return gram(store["rows"], store["mod"], qkv_mine[:first], (store["other"], raw, 1))
+        if k == 5:
+            return gram(store["rows"], store["mod_far"], qkv_mine[:first], (store["other"], raw, 1))
+        if k == 6:
+            store["far"] = lax.ppermute(raw, "tensor", core_swap)
+            return gram(store["rows"], store["mod"], qkv_mine[first:], (store["other"], raw, 0))
+        return gram(store["rows"], store["mod_far"], qkv_mine[first:], (store["other"], raw, 0))
+
+    done = pipeline(8, make_part, stage, early)
+    out_rows = assemble(done[:4], True, factor)
+    qkv_rows = assemble(done[4:], False, factor)
+    return (qkv_rows, out_rows)
+
+
 def solution(mesh):
+    lined = mesh.shape["dp"] == 8 and mesh.shape["tensor"] == 2
     return jax.shard_map(
-        body,
+        body if lined else plain_body,
         mesh=mesh,
         in_specs=(
             P(("groups", "dp"), "tensor"),

time: 493 us -> 207 us (0.42)
  waiting for transfers between devices: 435 us -> 43.4 us
  starting transfers between devices: 0.34 us -> 76.4 us
  Pallas kernels: 0 us -> 36.9 us
  matrix products: 29.2 us -> 0 us
  local copies, waits for them, and re-layouts: 0.1 us -> 16 us
  other arithmetic: 12 us -> 27.3 us
  between operations: 13.8 us -> 2.5 us
    reduce_scatter x2 -> x0, waiting for transfers between devices: 408 us -> none  [the longest x1 207 us: body(): lax.psum_scatter(part_out, 'dp', scatter_dimension=0, tiled=True)]
    ppermute x0 -> x40, starting transfers between devices: none -> 76.4 us  [the longest x8 46.9 us: begin(): came1[k] = lax.ppermute(sent1[k], 'dp', INWARD)]
    ppermute x0 -> x40, waiting for transfers between devices: none -> 43.4 us  [the longest x8 24.3 us: pipeline(): came3[j] = lax.ppermute(sent, 'dp', OUTWARD)]
    pallas_call x0 -> x16, Pallas kernels: none -> 36.9 us  [the longest x15 33 us: gridded(): pl.pallas_call(kernel, grid_spec=pltpu.PrefetchScalarGridSpec(num_scalar_...]
    dot_general x3 -> x0, matrix products: 29.2 us -> none  [the longest x2 23.2 us: gram_rows(): lax.dot_general(window, full, (((0,), (0,)), ((), ())), preferred_element...]
    all_gather x2 -> x0, waiting for transfers between devices: 25.7 us -> none  [the longest x1 18.7 us: body(): lax.all_gather(local_mod, 'tensor', axis=1, tiled=True)]
    unnamed x6 -> x56, local copies, waits for them, and re-layouts: 0.1 us -> 9.83 us
    another operation x0 -> x70, other arithmetic: none -> 8.05 us
  transfers between devices with their start and end apart: 4 -> 40, of which waited for: 4 -> 9; matrix products, arithmetic and copies ran while one was open for 5% -> 15% of each run, Pallas kernels for 0% -> 18%
where the time goes in v1:
time: 207 us; the launch traced here: 206 us
  starting transfers between devices  76.4 us (37%)
  waiting for transfers between devices  43.4 us (21%)
  Pallas kernels  36.9 us (18%)
  other arithmetic  27.3 us (13%)
  local copies, waits for them, and re-layouts  16 us (8%)
  blocking collectives  3.16 us (2%)
  between operations  2.5 us (1%)
    ppermute x8, starting transfers between devices, begin(): came1[k] = lax.ppermute(sent1[k], 'dp', INWARD)  46.9 us
    pallas_call x15, Pallas kernels, gridded(): pl.pallas_call(kernel, grid_spec=pltpu.PrefetchScalarGridSpec(num_scalar_...  33 us
    ppermute x8, waiting for transfers between devices, pipeline(): came3[j] = lax.ppermute(sent, 'dp', OUTWARD)  24.3 us
    ppermute x8, waiting for transfers between devices, begin(): came1[k] = lax.ppermute(sent1[k], 'dp', INWARD)  12.4 us
    ppermute x8, starting transfers between devices, pipeline(): came3[j] = lax.ppermute(sent, 'dp', OUTWARD)  10.3 us
    unnamed x56, local copies, waits for them, and re-layouts  9.83 us
    ppermute x8, starting transfers between devices, pipeline(): came4[j] = lax.ppermute(sent, 'dp', swap(8))  7.78 us
    ppermute x8, waiting for transfers between devices, pipeline(): came4[j] = lax.ppermute(sent, 'dp', swap(8))  6.74 us
  transfers between devices with their start and end apart: 40, of which 9 were waited for; matrix products, arithmetic and copies ran while one was open for 15% of the time, Pallas kernels for 18%

profile of v1, /device:TPU:0, one launch (start us, length us, event | category | flops | bytes accessed | tf_op | source)
XLA Modules:
  0.0 205.6 jit_solution(7719058525804652447)
XLA Ops:
  1.2 1.9 copy-done
  3.1 2.8 %shard_map.59 = bf16[512,1280]{1,0:T(8,128)(2,1)} custom-call(s32[5]{0:T(128)S(1)} %stack.143.at, bf16[512,3072]{1,0:T(8,128)(2,1)S(1)} %copy-done), custom_call_target="tpu_custom_call" | custom-call | tf_op jit(solution)/shard_map/pallas_call | solution.py:81
  6.0 2.6 %collective-permute-start = (bf16[512,1280]{1,0:T(8,128)(2,1)}, bf16[512,1280]{1,0:T(8,128)(2,1)}, u32[]{:S(2)}, u32[]{:S(2)}) collective-permute-start(bf16[512,1280]{1,0:T(8,128)(2,1)} %shard_map.59), channel_id=1, source_target_pairs={{0,2},{2,0},{4,6},{6,4},{8,10},{10,8},{12,14},{14,12},{1,3},{3,1},... | collective-permute-start | bytes 3932168 | tf_op jit(solution)/shard_map/ppermute | solution.py:360
  9.7 2.1 %shard_map.61 = (f32[512,1024]{1,0:T(8,128)S(1)}, f32[8,1024]{1,0:T(8,128)S(1)}) custom-call(s32[4]{0:T(128)S(1)} %copy-done.17, bf16[512,512]{1,0:T(8,128)(2,1)S(1)} %shard_map.60.rows, bf16[512,3072]{1,0:T(8,128)(2,1)S(1)} %copy-done.1), custom_call_target="tpu_custom_call" | custom-call | tf_op jit(solution)/shard_map/pallas_call | solution.py:81
  14.3 4.5 %collective-permute-start.1 = (f16[400,1024]{1,0:T(8,128)(2,1)}, f16[400,1024]{1,0:T(8,128)(2,1)}, u32[]{:S(2)}, u32[]{:S(2)}) collective-permute-start(f16[400,1024]{1,0:T(8,128)(2,1)} %pad_maximum_fusion), channel_id=1, source_target_pairs={{0,4},{2,6},{12,8},{14,10},{1,5},{3,7},{13,9},{15,11},{16,20},{18,... | collective-permute-start | bytes 2457608 | tf_op jit(solution)/shard_map/ppermute | solution.py:250
  24.6 3.5 %shard_map.62 = (f32[512,1024]{1,0:T(8,128)S(1)}, f32[8,1024]{1,0:T(8,128)S(1)}) custom-call(s32[4]{0:T(128)S(1)} %copy-done.18, bf16[512,512]{1,0:T(8,128)(2,1)S(1)} %copy-done.3, bf16[512,3072]{1,0:T(8,128)(2,1)} %collective-permute-done.2.columns), custom_call_target="tpu_custom_call" | custom-call | tf_op jit(solution)/shard_map/pallas_call | solution.py:81
  29.5 2.3 %collective-permute-start.5 = (f16[400,1024]{1,0:T(8,128)(2,1)}, f16[400,1024]{1,0:T(8,128)(2,1)}, u32[]{:S(2)}, u32[]{:S(2)}) collective-permute-start(f16[400,1024]{1,0:T(8,128)(2,1)} %pad_maximum_fusion.1), channel_id=1, source_target_pairs={{0,4},{2,6},{12,8},{14,10},{1,5},{3,7},{13,9},{15,11},{16,20},{18,... | collective-permute-start | bytes 2457608 | tf_op jit(solution)/shard_map/ppermute | solution.py:250
  33.4 3.2 %all-reduce = (f32[512]{0:T(512)}, f32[512]{0:T(512)}) all-reduce(f32[512]{0:T(512)} %get-tuple-element.117, f32[512]{0:T(512)} %get-tuple-element.116), channel_id=1, replica_groups=mesh['groups'=2,'dp'=8,'tensor'=2] {'tensor'}, use_global_device_ids=true, to_apply=%region_1.2 | all-reduce | flops 1024 | bytes 8192 | tf_op jit(solution)/shard_map/psum | solution.py:368
  40.8 1.9 copy-done.6
  45.5 3.9 %shard_map.63.source.columns = bf16[512,3072]{1,0:T(8,128)(2,1)S(1)} custom-call(s32[512,1]{1,0:T(8,128)S(1)} %copy.8.ids, bf16[512,3072]{1,0:T(8,128)(2,1)S(1)} %copy-done.6, f32[512,1]{1,0:T(8,128)S(1)} %copy-done.11, f32[512,1]{1,0:T(8,128)S(1)} %copy-done.12, f32[8,3072]{1,0:T(8,128)S(1)} %copy-done.13, f32[8,3072]{1,0:T(8,128)S(1)} %get-tuple-element.224.shift_table), custom_call_target="tpu_custom_call" | custom-call | tf_op jit(solution)/shard_map/pallas_call | solution.py:203
  54.0 2.7 %shard_map.66.other_rows = bf16[512,512]{1,0:T(8,128)(2,1)S(1)} custom-call(s32[4]{0:T(128)S(1)} %pad_add_fusion.2.at, bf16[512,1280]{1,0:T(8,128)(2,1)} %collective-permute-done.source.other_columns), custom_call_target="tpu_custom_call" | custom-call | tf_op jit(solution)/shard_map/pallas_call | solution.py:81
  58.4 4.0 %shard_map.67 = (f32[512,1024]{1,0:T(8,128)S(1)}, f32[8,1024]{1,0:T(8,128)S(1)}) custom-call(s32[4]{0:T(128)S(1)} %pad_add_fusion.3.at, bf16[512,512]{1,0:T(8,128)(2,1)S(1)} %copy-done.4, bf16[512,3072]{1,0:T(8,128)(2,1)S(1)} %copy-done.1, bf16[512,512]{1,0:T(8,128)(2,1)S(1)} %shard_map.66.other_rows, bf16[512,1280]{1,0:T(8,128)(2,1)} %collective-permute-done.source.other_columns), custom_call_target="tpu_custom_call" | custom-call | tf_op jit(solution)/shard_map/pallas_call | solution.py:81
  62.9 5.1 %collective-permute-start.4 = (f16[400,1024]{1,0:T(8,128)(2,1)S(1)}, f16[400,1024]{1,0:T(8,128)(2,1)S(1)}, u32[]{:S(2)}, u32[]{:S(2)}) collective-permute-start(f16[400,1024]{1,0:T(8,128)(2,1)S(1)} %pad_maximum_fusion.2), channel_id=1, source_target_pairs={{0,4},{2,6},{12,8},{14,10},{1,5},{3,7},{13,9},{15,11},{16,20},{18,... | collective-permute-start | bytes 2457608 | tf_op jit(solution)/shard_map/ppermute | solution.py:250
  72.6 4.0 %shard_map.68 = (f32[512,1024]{1,0:T(8,128)S(1)}, f32[8,1024]{1,0:T(8,128)S(1)}) custom-call(s32[4]{0:T(128)S(1)} %pad_add_fusion.3.at, bf16[512,512]{1,0:T(8,128)(2,1)S(1)} %copy-done.4, bf16[512,3072]{1,0:T(8,128)(2,1)} %collective-permute-done.2.columns, bf16[512,512]{1,0:T(8,128)(2,1)S(1)} %shard_map.66.other_rows, ...), custom_call_target="tpu_custom_call" | custom-call | tf_op jit(solution)/shard_map/pallas_call | solution.py:81
  77.0 7.9 %collective-permute-done.4 = f16[400,1024]{1,0:T(8,128)(2,1)S(1)} collective-permute-done((f16[400,1024]{1,0:T(8,128)(2,1)S(1)}, f16[400,1024]{1,0:T(8,128)(2,1)S(1)}, u32[]{:S(2)}, u32[]{:S(2)}) %collective-permute-start.4) | collective-permute-done | bytes 819232 | tf_op jit(solution)/shard_map/ppermute | solution.py:250
  85.0 4.4 %collective-permute-start.11 = (f16[400,1024]{1,0:T(8,128)(2,1)S(1)}, f16[400,1024]{1,0:T(8,128)(2,1)S(1)}, u32[]{:S(2)}, u32[]{:S(2)}) collective-permute-start(f16[400,1024]{1,0:T(8,128)(2,1)S(1)} %pad_maximum_fusion.3), channel_id=1, source_target_pairs={{0,4},{2,6},{12,8},{14,10},{1,5},{3,7},{13,9},{15,11},{16,20},{18,... | collective-permute-start | bytes 2457608 | tf_op jit(solution)/shard_map/ppermute | solution.py:250
  96.6 2.7 %shard_map.70 = (f32[512,1024]{1,0:T(8,128)S(1)}, f32[8,1024]{1,0:T(8,128)S(1)}) custom-call(s32[4]{0:T(128)S(1)} %pad_add_fusion.at, bf16[512,512]{1,0:T(8,128)(2,1)S(1)} %shard_map.64.rows, bf16[512,3072]{1,0:T(8,128)(2,1)S(1)} %shard_map.63.source.columns, bf16[512,512]{1,0:T(8,128)(2,1)S(1)} %shard_map.69.other_rows, ...), custom_call_target="tpu_custom_call" | custom-call | tf_op jit(solution)/shard_map/pallas_call | solution.py:81
  103.3 10.4 %collective-permute-start.10 = (f16[400,1024]{1,0:T(8,128)(2,1)S(1)}, f16[400,1024]{1,0:T(8,128)(2,1)S(1)}, u32[]{:S(2)}, u32[]{:S(2)}) collective-permute-start(f16[400,1024]{1,0:T(8,128)(2,1)S(1)} %pad_maximum_fusion.4), channel_id=1, source_target_pairs={{0,4},{2,6},{12,8},{14,10},{1,5},{3,7},{13,9},{15,11},{16,20},{18,... | collective-permute-start | bytes 2457608 | tf_op jit(solution)/shard_map/ppermute | solution.py:250
  115.8 1.6 collective-permute-start.17
  120.1 2.7 %shard_map.71 = (f32[512,1024]{1,0:T(8,128)S(1)}, f32[8,1024]{1,0:T(8,128)S(1)}) custom-call(s32[4]{0:T(128)S(1)} %pad_add_fusion.at, bf16[512,512]{1,0:T(8,128)(2,1)S(1)} %shard_map.64.rows, bf16[512,3072]{1,0:T(8,128)(2,1)S(1)} %collective-permute-done.18.columns, bf16[512,512]{1,0:T(8,128)(2,1)S(1)} %shard_map.69.other_rows, ...), custom_call_target="tpu_custom_call" | custom-call | tf_op jit(solution)/shard_map/pallas_call | solution.py:81
  123.4 4.4 %collective-permute-done.10 = f16[400,1024]{1,0:T(8,128)(2,1)S(1)} collective-permute-done((f16[400,1024]{1,0:T(8,128)(2,1)S(1)}, f16[400,1024]{1,0:T(8,128)(2,1)S(1)}, u32[]{:S(2)}, u32[]{:S(2)}) %collective-permute-start.10) | collective-permute-done | bytes 819232 | tf_op jit(solution)/shard_map/ppermute | solution.py:250
  127.8 4.4 %collective-permute-start.20 = (f16[400,1024]{1,0:T(8,128)(2,1)S(1)}, f16[400,1024]{1,0:T(8,128)(2,1)S(1)}, u32[]{:S(2)}, u32[]{:S(2)}) collective-permute-start(f16[400,1024]{1,0:T(8,128)(2,1)S(1)} %pad_maximum_fusion.5), channel_id=1, source_target_pairs={{0,4},{2,6},{12,8},{14,10},{1,5},{3,7},{13,9},{15,11},{16,20},{18,... | collective-permute-start | bytes 2457608 | tf_op jit(solution)/shard_map/ppermute | solution.py:250
  137.0 1.7 shard_map.73
  139.0 7.4 %collective-permute-start.25 = (f16[400,512]{1,0:T(8,128)(2,1)S(1)}, f16[400,512]{1,0:T(8,128)(2,1)S(1)}, u32[]{:S(2)}, u32[]{:S(2)}) collective-permute-start(f16[400,512]{1,0:T(8,128)(2,1)S(1)} %pad_maximum_fusion.12), channel_id=1, source_target_pairs={{0,4},{2,6},{12,8},{14,10},{1,5},{3,7},{13,9},{15,11},{16,20},{18,... | collective-permute-start | bytes 1228808 | tf_op jit(solution)/shard_map/ppermute | solution.py:250
  150.3 1.7 shard_map.74
  152.2 8.5 %collective-permute-start.30 = (f16[400,512]{1,0:T(8,128)(2,1)S(1)}, f16[400,512]{1,0:T(8,128)(2,1)S(1)}, u32[]{:S(2)}, u32[]{:S(2)}) collective-permute-start(f16[400,512]{1,0:T(8,128)(2,1)S(1)} %pad_maximum_fusion.13), channel_id=1, source_target_pairs={{0,4},{2,6},{12,8},{14,10},{1,5},{3,7},{13,9},{15,11},{16,20},{18,... | collective-permute-start | bytes 1228808 | tf_op jit(solution)/shard_map/ppermute | solution.py:250
  161.5 1.6 collective-permute-start.33
  167.0 12.0 %collective-permute-done.32 = f16[144,1024]{1,0:T(8,128)(2,1)S(1)} collective-permute-done((f16[144,1024]{1,0:T(8,128)(2,1)S(1)}, f16[144,1024]{1,0:T(8,128)(2,1)S(1)}, u32[]{:S(2)}, u32[]{:S(2)}) %collective-permute-start.32) | collective-permute-done | bytes 294944 | tf_op jit(solution)/shard_map/ppermute | solution.py:279
  182.6 4.1 %collective-permute-done.35 = f16[144,512]{1,0:T(8,128)(2,1)S(1)} collective-permute-done((f16[144,512]{1,0:T(8,128)(2,1)S(1)}, f16[144,512]{1,0:T(8,128)(2,1)S(1)}, u32[]{:S(2)}, u32[]{:S(2)}) %collective-permute-start.35) | collective-permute-done | bytes 147488 | tf_op jit(solution)/shard_map/ppermute | solution.py:279
  189.5 2.5 %collective-permute-done.38 = f16[80,512]{1,0:T(8,128)(2,1)S(1)} collective-permute-done((f16[80,512]{1,0:T(8,128)(2,1)S(1)}, f16[80,512]{1,0:T(8,128)(2,1)S(1)}, u32[]{:S(2)}, u32[]{:S(2)}) %collective-permute-start.38) | collective-permute-done | bytes 81952 | tf_op jit(solution)/shard_map/ppermute | solution.py:291
  192.0 7.4 %collective-permute-done.37 = f16[144,512]{1,0:T(8,128)(2,1)S(1)} collective-permute-done((f16[144,512]{1,0:T(8,128)(2,1)S(1)}, f16[144,512]{1,0:T(8,128)(2,1)S(1)}, u32[]{:S(2)}, u32[]{:S(2)}) %collective-permute-start.37) | collective-permute-done | bytes 147488 | tf_op jit(solution)/shard_map/ppermute | solution.py:279
  200.3 3.8 %collective-permute-done.39 = f16[80,512]{1,0:T(8,128)(2,1)S(1)} collective-permute-done((f16[80,512]{1,0:T(8,128)(2,1)S(1)}, f16[80,512]{1,0:T(8,128)(2,1)S(1)}, u32[]{:S(2)}, u32[]{:S(2)}) %collective-permute-start.39) | collective-permute-done | bytes 81952 | tf_op jit(solution)/shard_map/ppermute | solution.py:291
  (328 shorter events, 69.6 us)
Async XLA Ops:
  0.6 22.2 %collective-permute-start.2 = (bf16[512,3072]{1,0:T(8,128)(2,1)}, bf16[512,3072]{1,0:T(8,128)(2,1)}, u32[]{:S(2)}, u32[]{:S(2)}) collective-permute-start(bf16[512,3072]{1,0:T(8,128)(2,1)} %columns.3), channel_id=1, source_target_pairs={{0,1},{1,0},{2,3},{3,2},{4,5},{5,4},{6,7},{7,6},{8,9},{9,8},{10,11... | collective-permute-start | bytes 9437192 | tf_op jit(solution)/shard_map/ppermute | solution.py:358
  6.0 46.4 %collective-permute-start = (bf16[512,1280]{1,0:T(8,128)(2,1)}, bf16[512,1280]{1,0:T(8,128)(2,1)}, u32[]{:S(2)}, u32[]{:S(2)}) collective-permute-start(bf16[512,1280]{1,0:T(8,128)(2,1)} %shard_map.59), channel_id=1, source_target_pairs={{0,2},{2,0},{4,6},{6,4},{8,10},{10,8},{12,14},{14,12},{1,3},{3,1},... | collective-permute-start | bytes 3932168 | tf_op jit(solution)/shard_map/ppermute | solution.py:360
  14.3 35.1 %collective-permute-start.1 = (f16[400,1024]{1,0:T(8,128)(2,1)}, f16[400,1024]{1,0:T(8,128)(2,1)}, u32[]{:S(2)}, u32[]{:S(2)}) collective-permute-start(f16[400,1024]{1,0:T(8,128)(2,1)} %pad_maximum_fusion), channel_id=1, source_target_pairs={{0,4},{2,6},{12,8},{14,10},{1,5},{3,7},{13,9},{15,11},{16,20},{18,... | collective-permute-start | bytes 2457608 | tf_op jit(solution)/shard_map/ppermute | solution.py:250
  29.5 38.5 %collective-permute-start.5 = (f16[400,1024]{1,0:T(8,128)(2,1)}, f16[400,1024]{1,0:T(8,128)(2,1)}, u32[]{:S(2)}, u32[]{:S(2)}) collective-permute-start(f16[400,1024]{1,0:T(8,128)(2,1)} %pad_maximum_fusion.1), channel_id=1, source_target_pairs={{0,4},{2,6},{12,8},{14,10},{1,5},{3,7},{13,9},{15,11},{16,20},{18,... | collective-permute-start | bytes 2457608 | tf_op jit(solution)/shard_map/ppermute | solution.py:250
  51.6 11.3 %collective-permute-start.6 = (f16[272,1024]{1,0:T(8,128)(2,1)S(1)}, f16[272,1024]{1,0:T(8,128)(2,1)S(1)}, u32[]{:S(2)}, u32[]{:S(2)}) collective-permute-start(f16[272,1024]{1,0:T(8,128)(2,1)S(1)} %pad_maximum_fusion.6), channel_id=1, source_target_pairs={{4,8},{6,10},{8,4},{10,6},{5,9},{7,11},{9,5},{11,7},{20,24},{22,26... | collective-permute-start | bytes 1671176 | tf_op jit(solution)/shard_map/ppermute | solution.py:271
  53.5 65.9 %collective-permute-start.18 = (bf16[512,3072]{1,0:T(8,128)(2,1)S(1)}, bf16[512,3072]{1,0:T(8,128)(2,1)S(1)}, u32[]{:S(2)}, u32[]{:S(2)}) collective-permute-start(bf16[512,3072]{1,0:T(8,128)(2,1)S(1)} %shard_map.63.source.columns), channel_id=1, source_target_pairs={{0,1},{1,0},{2,3},{3,2},{4,5},{5,4},{6,7},{7,6},{8,9},{9,8},{10,11... | collective-permute-start | bytes 9437192 | tf_op jit(solution)/shard_map/ppermute | solution.py:394
  53.7 18.1 %collective-permute-start.9 = (bf16[512,1280]{1,0:T(8,128)(2,1)}, bf16[512,1280]{1,0:T(8,128)(2,1)S(1)}, u32[]{:S(2)}, u32[]{:S(2)}) collective-permute-start(bf16[512,1280]{1,0:T(8,128)(2,1)} %collective-permute-done.source.other_columns), channel_id=1, source_target_pairs={{0,1},{1,0},{2,3},{3,2},{4,5},{5,4},{6,7},{7,6},{8,9},{9,8},{10,11... | collective-permute-start | bytes 3932168 | tf_op jit(solution)/shard_map/ppermute | solution.py:390
  57.8 37.0 %collective-permute-start.3 = (bf16[512,1280]{1,0:T(8,128)(2,1)S(1)}, bf16[512,1280]{1,0:T(8,128)(2,1)S(1)}, u32[]{:S(2)}, u32[]{:S(2)}) collective-permute-start(bf16[512,1280]{1,0:T(8,128)(2,1)S(1)} %shard_map.65), channel_id=1, source_target_pairs={{0,2},{2,0},{4,6},{6,4},{8,10},{10,8},{12,14},{14,12},{1,3},{3,1},... | collective-permute-start | bytes 3932168 | tf_op jit(solution)/shard_map/ppermute | solution.py:393
  62.9 22.0 %collective-permute-start.4 = (f16[400,1024]{1,0:T(8,128)(2,1)S(1)}, f16[400,1024]{1,0:T(8,128)(2,1)S(1)}, u32[]{:S(2)}, u32[]{:S(2)}) collective-permute-start(f16[400,1024]{1,0:T(8,128)(2,1)S(1)} %pad_maximum_fusion.2), channel_id=1, source_target_pairs={{0,4},{2,6},{12,8},{14,10},{1,5},{3,7},{13,9},{15,11},{16,20},{18,... | collective-permute-start | bytes 2457608 | tf_op jit(solution)/shard_map/ppermute | solution.py:250
  68.3 21.1 %collective-permute-start.8 = (f16[144,1024]{1,0:T(8,128)(2,1)S(1)}, f16[144,1024]{1,0:T(8,128)(2,1)S(1)}, u32[]{:S(2)}, u32[]{:S(2)}) collective-permute-start(f16[144,1024]{1,0:T(8,128)(2,1)S(1)} %pad_maximum_fusion.14), channel_id=1, source_target_pairs={{4,0},{6,2},{8,12},{10,14},{5,1},{7,3},{9,13},{11,15},{20,16},{22,... | collective-permute-start | bytes 884744 | tf_op jit(solution)/shard_map/ppermute | solution.py:279
  71.9 17.6 %collective-permute-start.7 = (f16[272,1024]{1,0:T(8,128)(2,1)S(1)}, f16[272,1024]{1,0:T(8,128)(2,1)S(1)}, u32[]{:S(2)}, u32[]{:S(2)}) collective-permute-start(f16[272,1024]{1,0:T(8,128)(2,1)S(1)} %pad_maximum_fusion.7), channel_id=1, source_target_pairs={{4,8},{6,10},{8,4},{10,6},{5,9},{7,11},{9,5},{11,7},{20,24},{22,26... | collective-permute-start | bytes 1671176 | tf_op jit(solution)/shard_map/ppermute | solution.py:271
  85.0 28.7 %collective-permute-start.11 = (f16[400,1024]{1,0:T(8,128)(2,1)S(1)}, f16[400,1024]{1,0:T(8,128)(2,1)S(1)}, u32[]{:S(2)}, u32[]{:S(2)}) collective-permute-start(f16[400,1024]{1,0:T(8,128)(2,1)S(1)} %pad_maximum_fusion.3), channel_id=1, source_target_pairs={{0,4},{2,6},{12,8},{14,10},{1,5},{3,7},{13,9},{15,11},{16,20},{18,... | collective-permute-start | bytes 2457608 | tf_op jit(solution)/shard_map/ppermute | solution.py:250
  92.3 8.7 %collective-permute-start.14 = (f16[80,1024]{1,0:T(8,128)(2,1)S(1)}, f16[80,1024]{1,0:T(8,128)(2,1)S(1)}, u32[]{:S(2)}, u32[]{:S(2)}) collective-permute-start(f16[80,1024]{1,0:T(8,128)(2,1)S(1)} %pad_maximum_fusion.22), channel_id=1, source_target_pairs={{0,2},{2,0},{4,6},{6,4},{8,10},{10,8},{12,14},{14,12},{1,3},{3,1},... | collective-permute-start | bytes 491528 | tf_op jit(solution)/shard_map/ppermute | solution.py:291
  93.1 8.7 %collective-permute-start.13 = (f16[144,1024]{1,0:T(8,128)(2,1)S(1)}, f16[144,1024]{1,0:T(8,128)(2,1)S(1)}, u32[]{:S(2)}, u32[]{:S(2)}) collective-permute-start(f16[144,1024]{1,0:T(8,128)(2,1)S(1)} %pad_maximum_fusion.15), channel_id=1, source_target_pairs={{4,0},{6,2},{8,12},{10,14},{5,1},{7,3},{9,13},{11,15},{20,16},{22,... | collective-permute-start | bytes 884744 | tf_op jit(solution)/shard_map/ppermute | solution.py:279
  94.8 8.5 %collective-permute-start.12 = (f16[272,1024]{1,0:T(8,128)(2,1)S(1)}, f16[272,1024]{1,0:T(8,128)(2,1)S(1)}, u32[]{:S(2)}, u32[]{:S(2)}) collective-permute-start(f16[272,1024]{1,0:T(8,128)(2,1)S(1)} %pad_maximum_fusion.8), channel_id=1, source_target_pairs={{4,8},{6,10},{8,4},{10,6},{5,9},{7,11},{9,5},{11,7},{20,24},{22,26... | collective-permute-start | bytes 1671176 | tf_op jit(solution)/shard_map/ppermute | solution.py:271
  100.9 17.2 %collective-permute-start.19 = (bf16[512,1280]{1,0:T(8,128)(2,1)S(1)}, bf16[512,1280]{1,0:T(8,128)(2,1)S(1)}, u32[]{:S(2)}, u32[]{:S(2)}) collective-permute-start(bf16[512,1280]{1,0:T(8,128)(2,1)S(1)} %collective-permute-done.3.source.other_columns), channel_id=1, source_target_pairs={{0,1},{1,0},{2,3},{3,2},{4,5},{5,4},{6,7},{7,6},{8,9},{9,8},{10,11... | collective-permute-start | bytes 3932168 | tf_op jit(solution)/shard_map/ppermute | solution.py:400
  101.8 35.2 %collective-permute-start.24 = (bf16[512,512]{1,0:T(8,128)(2,1)S(1)}, bf16[512,512]{1,0:T(8,128)(2,1)S(1)}, u32[]{:S(2)}, u32[]{:S(2)}) collective-permute-start(bf16[512,512]{1,0:T(8,128)(2,1)S(1)} %shard_map.72), channel_id=1, source_target_pairs={{0,2},{2,0},{4,6},{6,4},{8,10},{10,8},{12,14},{14,12},{1,3},{3,1},... | collective-permute-start | bytes 1572872 | tf_op jit(solution)/shard_map/ppermute | solution.py:403
  103.3 24.5 %collective-permute-start.10 = (f16[400,1024]{1,0:T(8,128)(2,1)S(1)}, f16[400,1024]{1,0:T(8,128)(2,1)S(1)}, u32[]{:S(2)}, u32[]{:S(2)}) collective-permute-start(f16[400,1024]{1,0:T(8,128)(2,1)S(1)} %pad_maximum_fusion.4), channel_id=1, source_target_pairs={{0,4},{2,6},{12,8},{14,10},{1,5},{3,7},{13,9},{15,11},{16,20},{18,... | collective-permute-start | bytes 2457608 | tf_op jit(solution)/shard_map/ppermute | solution.py:250
  115.8 16.4 %collective-permute-start.17 = (f16[80,1024]{1,0:T(8,128)(2,1)S(1)}, f16[80,1024]{1,0:T(8,128)(2,1)S(1)}, u32[]{:S(2)}, u32[]{:S(2)}) collective-permute-start(f16[80,1024]{1,0:T(8,128)(2,1)S(1)} %pad_maximum_fusion.23), channel_id=1, source_target_pairs={{0,2},{2,0},{4,6},{6,4},{8,10},{10,8},{12,14},{14,12},{1,3},{3,1},... | collective-permute-start | bytes 491528 | tf_op jit(solution)/shard_map/ppermute | solution.py:291
  118.1 14.1 %collective-permute-start.16 = (f16[144,1024]{1,0:T(8,128)(2,1)S(1)}, f16[144,1024]{1,0:T(8,128)(2,1)S(1)}, u32[]{:S(2)}, u32[]{:S(2)}) collective-permute-start(f16[144,1024]{1,0:T(8,128)(2,1)S(1)} %pad_maximum_fusion.16), channel_id=1, source_target_pairs={{4,0},{6,2},{8,12},{10,14},{5,1},{7,3},{9,13},{11,15},{20,16},{22,... | collective-permute-start | bytes 884744 | tf_op jit(solution)/shard_map/ppermute | solution.py:279
  119.4 12.8 %collective-permute-start.15 = (f16[272,1024]{1,0:T(8,128)(2,1)S(1)}, f16[272,1024]{1,0:T(8,128)(2,1)S(1)}, u32[]{:S(2)}, u32[]{:S(2)}) collective-permute-start(f16[272,1024]{1,0:T(8,128)(2,1)S(1)} %pad_maximum_fusion.9), channel_id=1, source_target_pairs={{4,8},{6,10},{8,4},{10,6},{5,9},{7,11},{9,5},{11,7},{20,24},{22,26... | collective-permute-start | bytes 1671176 | tf_op jit(solution)/shard_map/ppermute | solution.py:271
  127.8 18.6 %collective-permute-start.20 = (f16[400,1024]{1,0:T(8,128)(2,1)S(1)}, f16[400,1024]{1,0:T(8,128)(2,1)S(1)}, u32[]{:S(2)}, u32[]{:S(2)}) collective-permute-start(f16[400,1024]{1,0:T(8,128)(2,1)S(1)} %pad_maximum_fusion.5), channel_id=1, source_target_pairs={{0,4},{2,6},{12,8},{14,10},{1,5},{3,7},{13,9},{15,11},{16,20},{18,... | collective-permute-start | bytes 2457608 | tf_op jit(solution)/shard_map/ppermute | solution.py:250
  134.5 11.9 %collective-permute-start.22 = (f16[144,1024]{1,0:T(8,128)(2,1)S(1)}, f16[144,1024]{1,0:T(8,128)(2,1)S(1)}, u32[]{:S(2)}, u32[]{:S(2)}) collective-permute-start(f16[144,1024]{1,0:T(8,128)(2,1)S(1)} %pad_maximum_fusion.17), channel_id=1, source_target_pairs={{4,0},{6,2},{8,12},{10,14},{5,1},{7,3},{9,13},{11,15},{20,16},{22,... | collective-permute-start | bytes 884744 | tf_op jit(solution)/shard_map/ppermute | solution.py:279
  136.2 10.2 %collective-permute-start.21 = (f16[272,1024]{1,0:T(8,128)(2,1)S(1)}, f16[272,1024]{1,0:T(8,128)(2,1)S(1)}, u32[]{:S(2)}, u32[]{:S(2)}) collective-permute-start(f16[272,1024]{1,0:T(8,128)(2,1)S(1)} %pad_maximum_fusion.10), channel_id=1, source_target_pairs={{4,8},{6,10},{8,4},{10,6},{5,9},{7,11},{9,5},{11,7},{20,24},{22,26... | collective-permute-start | bytes 1671176 | tf_op jit(solution)/shard_map/ppermute | solution.py:271
  136.9 13.3 %collective-permute-start.29 = (bf16[512,512]{1,0:T(8,128)(2,1)S(1)}, bf16[512,512]{1,0:T(8,128)(2,1)S(1)}, u32[]{:S(2)}, u32[]{:S(2)}) collective-permute-start(bf16[512,512]{1,0:T(8,128)(2,1)S(1)} %collective-permute-done.24.other_columns), channel_id=1, source_target_pairs={{0,1},{1,0},{2,3},{3,2},{4,5},{5,4},{6,7},{7,6},{8,9},{9,8},{10,11... | collective-permute-start | bytes 1572872 | tf_op jit(solution)/shard_map/ppermute | solution.py:408
  139.0 21.9 %collective-permute-start.25 = (f16[400,512]{1,0:T(8,128)(2,1)S(1)}, f16[400,512]{1,0:T(8,128)(2,1)S(1)}, u32[]{:S(2)}, u32[]{:S(2)}) collective-permute-start(f16[400,512]{1,0:T(8,128)(2,1)S(1)} %pad_maximum_fusion.12), channel_id=1, source_target_pairs={{0,4},{2,6},{12,8},{14,10},{1,5},{3,7},{13,9},{15,11},{16,20},{18,... | collective-permute-start | bytes 1228808 | tf_op jit(solution)/shard_map/ppermute | solution.py:250
  146.9 14.0 %collective-permute-start.28 = (f16[80,1024]{1,0:T(8,128)(2,1)S(1)}, f16[80,1024]{1,0:T(8,128)(2,1)S(1)}, u32[]{:S(2)}, u32[]{:S(2)}) collective-permute-start(f16[80,1024]{1,0:T(8,128)(2,1)S(1)} %pad_maximum_fusion.25), channel_id=1, source_target_pairs={{0,2},{2,0},{4,6},{6,4},{8,10},{10,8},{12,14},{14,12},{1,3},{3,1},... | collective-permute-start | bytes 491528 | tf_op jit(solution)/shard_map/ppermute | solution.py:291
  147.8 13.1 %collective-permute-start.27 = (f16[144,1024]{1,0:T(8,128)(2,1)S(1)}, f16[144,1024]{1,0:T(8,128)(2,1)S(1)}, u32[]{:S(2)}, u32[]{:S(2)}) collective-permute-start(f16[144,1024]{1,0:T(8,128)(2,1)S(1)} %pad_maximum_fusion.18), channel_id=1, source_target_pairs={{4,0},{6,2},{8,12},{10,14},{5,1},{7,3},{9,13},{11,15},{20,16},{22,... | collective-permute-start | bytes 884744 | tf_op jit(solution)/shard_map/ppermute | solution.py:279
  149.5 11.4 %collective-permute-start.26 = (f16[272,1024]{1,0:T(8,128)(2,1)S(1)}, f16[272,1024]{1,0:T(8,128)(2,1)S(1)}, u32[]{:S(2)}, u32[]{:S(2)}) collective-permute-start(f16[272,1024]{1,0:T(8,128)(2,1)S(1)} %pad_maximum_fusion.11), channel_id=1, source_target_pairs={{4,8},{6,10},{8,4},{10,6},{5,9},{7,11},{9,5},{11,7},{20,24},{22,26... | collective-permute-start | bytes 1671176 | tf_op jit(solution)/shard_map/ppermute | solution.py:271
  152.2 14.8 %collective-permute-start.30 = (f16[400,512]{1,0:T(8,128)(2,1)S(1)}, f16[400,512]{1,0:T(8,128)(2,1)S(1)}, u32[]{:S(2)}, u32[]{:S(2)}) collective-permute-start(f16[400,512]{1,0:T(8,128)(2,1)S(1)} %pad_maximum_fusion.13), channel_id=1, source_target_pairs={{0,4},{2,6},{12,8},{14,10},{1,5},{3,7},{13,9},{15,11},{16,20},{18,... | collective-permute-start | bytes 1228808 | tf_op jit(solution)/shard_map/ppermute | solution.py:250
  164.2 14.8 %collective-permute-start.32 = (f16[144,1024]{1,0:T(8,128)(2,1)S(1)}, f16[144,1024]{1,0:T(8,128)(2,1)S(1)}, u32[]{:S(2)}, u32[]{:S(2)}) collective-permute-start(f16[144,1024]{1,0:T(8,128)(2,1)S(1)} %pad_maximum_fusion.19), channel_id=1, source_target_pairs={{4,0},{6,2},{8,12},{10,14},{5,1},{7,3},{9,13},{11,15},{20,16},{22,... | collective-permute-start | bytes 884744 | tf_op jit(solution)/shard_map/ppermute | solution.py:279
  188.2 11.2 %collective-permute-start.37 = (f16[144,512]{1,0:T(8,128)(2,1)S(1)}, f16[144,512]{1,0:T(8,128)(2,1)S(1)}, u32[]{:S(2)}, u32[]{:S(2)}) collective-permute-start(f16[144,512]{1,0:T(8,128)(2,1)S(1)} %pad_maximum_fusion.29), channel_id=1, source_target_pairs={{4,0},{6,2},{8,12},{10,14},{5,1},{7,3},{9,13},{11,15},{20,16},{22,... | collective-permute-start | bytes 442376 | tf_op jit(solution)/shard_map/ppermute | solution.py:279
  (29 other events, 107.6 us)

commit v2 on v0

--- a/solution.py
+++ b/solution.py
@@ -1,12 +1,25 @@
+import functools
+
 import jax
 import jax.numpy as jnp
 from jax import lax
+from jax.experimental import pallas as pl
+from jax.experimental.pallas import tpu as pltpu
 from jax.sharding import PartitionSpec as P
 
 ROW_DEV = 512
+LANES = 256
 
 
 epsilon = 1e-06
+VMEM = 16 << 20
+TAIL = 16
+LAG = 2
+LATER = (2, 3, 4, 5, 6, 7)
+LAST = 8
+GATE = 1
+CHUNKS = [[("shared", False, 0, 4)], [("shared", True, 0, 4)], [("attn", False, 0, 4)], [("attn", True, 0, 4)], [("qkv", False, 0, 4)], [("qkv", True, 0, 4)], [("qkv", False, 4, 2)], [("qkv", True, 4, 2)]]
+PIECES = (5, 2)
 
 
 def lookup_table(step_ids, table):
@@ -23,7 +36,7 @@
     )
 
 
-def body(hidden, attn_out, step_ids, modulation):
+def plain_body(hidden, attn_out, step_ids, modulation):
     token_count = hidden.shape[0]
     local_width = hidden.shape[1]
     parts_tp = lax.axis_size("tensor")
@@ -53,9 +66,487 @@
     return (summed_qkv * factor, summed_out * factor)
 
 
+def swap(size, mask=1):
+    return [(i, i ^ mask) for i in range(size)]
+
+
+def cut(values, start, size, axis):
+    return lax.dynamic_slice_in_dim(values, start, size, axis)
+
+
+FREE = pl.CostEstimate(flops=0, bytes_accessed=0, transcendentals=0)
+
+
+def gridded(kernel, indices, grid, in_specs, out_specs, out_shape, *operands):
+    return pl.pallas_call(
+        kernel,
+        grid_spec=pltpu.PrefetchScalarGridSpec(
+            num_scalar_prefetch=1, grid=(grid,), in_specs=in_specs, out_specs=out_specs
+        ),
+        out_shape=out_shape,
+        cost_estimate=FREE,
+        compiler_params=pltpu.CompilerParams(vmem_limit_bytes=VMEM),
+    )(indices, *operands)
+
+
+def pick_kernel(at, source, out):
+    out[...] = source[...]
+
+
+def pick(plan, source, first, count):
+    tokens = source.shape[0]
+    return gridded(
+        pick_kernel,
+        plan,
+        count,
+        [pl.BlockSpec((tokens, LANES), lambda i, at: (0, at[first + i]))],
+        pl.BlockSpec((tokens, LANES), lambda i, at: (0, i)),
+        jax.ShapeDtypeStruct((tokens, LANES * count), source.dtype),
+        source,
+    )
+
+
+def turn_kernel(at, source, out):
+    out[...] = source[...].T
+
+
+def turn(plan, source, first):
+    tokens = source.shape[0]
+    size = ROW_DEV // 4
+    return gridded(
+        turn_kernel,
+        plan,
+        4,
+        [pl.BlockSpec((tokens, size), lambda i, at: (0, at[first + i]))],
+        pl.BlockSpec((size, tokens), lambda i, at: (i, 0)),
+        jax.ShapeDtypeStruct((ROW_DEV, tokens), source.dtype),
+        source,
+    )
+
+
+def store_coded(total, message):
+    rows = total.shape[0]
+    peak = jnp.max(jnp.abs(total), axis=0, keepdims=True)
+    power = jnp.ceil(jnp.log2(jnp.maximum(peak, 1e-30))) - 15.0
+    codes = jnp.clip(jnp.round(total * jnp.exp2(-power)), -32767.0, 32767.0)
+    message[:rows, :] = codes.astype(jnp.int32).astype(jnp.int16)
+    tail = jnp.broadcast_to(power, (TAIL, total.shape[1]))
+    message[rows:, :] = tail.astype(jnp.int32).astype(jnp.int16)
+
+
+def decoded(message, first, last):
+    power = message[message.shape[0] - TAIL :, :].astype(jnp.int32).astype(jnp.float32)[:1]
+    return message[first:last, :].astype(jnp.int32).astype(jnp.float32) * jnp.exp2(power)
+
+
+def chosen_piece(step, starts, pieces):
+    values = pieces[0][...]
+    for start, piece in zip(starts[1:], pieces[1:]):
+        values = jnp.where(step < start, values, piece[...])
+    return values
+
+
+def gram_kernel(starts, at, rows, *refs):
+    own, message = refs[-2:]
+    step = pl.program_id(0)
+    mine = len(starts[0])
+    total = jnp.dot(rows[...], chosen_piece(step, starts[0], refs[:mine]), preferred_element_type=jnp.float32)
+    if starts[1]:
+        columns = chosen_piece(step, starts[1], refs[mine + 1 : -2])
+        total = total + jnp.dot(refs[mine][...], columns, preferred_element_type=jnp.float32)
+    sent = message.shape[0] - TAIL
+    own[...] = total[sent:]
+    store_coded(total[:sent], message)
+
+
+def gram(plan, rows, columns, other_rows=None, other_columns=()):
+    tokens = rows.shape[1]
+    whole = pl.BlockSpec((ROW_DEV, tokens), lambda i, at: (0, 0))
+    in_specs, operands = [whole], [rows]
+    starts = ([], [])
+    for group, pieces in enumerate((columns, other_columns)):
+        if group == 1 and pieces:
+            in_specs.append(whole)
+            operands.append(other_rows)
+        start = 0
+        for array, base, held in pieces:
+
+            def place(i, at, listed=group == 0, base=base, held=held, start=start):
+                index = jnp.clip(i - start, 0, held - 1) + base
+                return (0, at[index] if listed else index)
+
+            in_specs.append(pl.BlockSpec((tokens, LANES), place))
+            operands.append(array)
+            starts[group].append(start)
+            start += held
+    count = sum(held for _, _, held in columns)
+    width = LANES * count
+    own = ROW_DEV // 2
+    sent = ROW_DEV - own + TAIL
+    return gridded(
+        functools.partial(gram_kernel, tuple(map(tuple, starts))),
+        plan,
+        count,
+        in_specs,
+        [pl.BlockSpec((own, LANES), lambda i, at: (0, i)), pl.BlockSpec((sent, LANES), lambda i, at: (0, i))],
+        [jax.ShapeDtypeStruct((own, width), jnp.float32), jax.ShapeDtypeStruct((sent, width), jnp.int16)],
+        *operands,
+    )
+
+
+def blocked(kernel, width, inputs, outputs):
+    size = min(width, 2 * LANES)
+    return pl.pallas_call(
+        kernel,
+        grid=(width // size,),
+        in_specs=[pl.BlockSpec((rows, size), lambda i, at=at: (at, i)) for _, rows, at in inputs],
+        out_specs=[pl.BlockSpec((rows, size), lambda i: (0, i)) for rows, _ in outputs],
+        out_shape=[jax.ShapeDtypeStruct((rows, width), dtype) for rows, dtype in outputs],
+        cost_estimate=FREE,
+        compiler_params=pltpu.CompilerParams(vmem_limit_bytes=VMEM),
+    )(*[array for array, _, _ in inputs])
+
+
+def add_kernel(own, came, message):
+    rows = own.shape[0]
+    store_coded(own[...] + decoded(came, 0, rows), message)
+
+
+def add_sums(own, came):
+    rows = own.shape[0] // 2
+    inputs = [(own, rows, 0), (came, came.shape[0], 0)]
+    return blocked(add_kernel, own.shape[1], inputs, [(rows + TAIL, jnp.int16)])[0]
+
+
+def total_kernel(own, came1, came2, mine, message):
+    rows = own.shape[0]
+    total = own[...] + decoded(came1, rows, 2 * rows) + decoded(came2, 0, rows)
+    side = lax.rem(lax.axis_index("dp"), 2)
+    half = rows // 2
+    low, high = total[:half], total[half:]
+    mine[...] = jnp.where(side == 0, low, high)
+    store_coded(jnp.where(side == 0, high, low), message)
+
+
+def total_sums(own, came1, came2):
+    rows = own.shape[0] // 2
+    inputs = [(own, rows, 1), (came1, came1.shape[0], 0), (came2, came2.shape[0], 0)]
+    outputs = [(rows // 2, jnp.float32), (rows // 2 + TAIL, jnp.int16)]
+    return blocked(total_kernel, own.shape[1], inputs, outputs)
+
+
+def token_columns(rows):
+    full = jnp.concatenate([rows, jnp.zeros((8 - rows.shape[0], rows.shape[1]), rows.dtype)], axis=0)
+    return full.T
+
+
+def chosen_rows(ids, steps, kind, repeat):
+    place = lax.broadcasted_iota(jnp.int32, (ids.shape[0], repeat * 2 * steps), 1)
+    return (2.0 * ids + kind).astype(jnp.int32) == lax.rem(place, 2 * steps)
+
+
+def stats_kernel(hidden, moments):
+    values = hidden[...].astype(jnp.float32)
+    total = jnp.sum(values, axis=1, keepdims=True)
+    squares = jnp.sum(values * values, axis=1, keepdims=True)
+    lane = lax.broadcasted_iota(jnp.int32, (values.shape[0], 128), 1)
+    moments[...] = jnp.where(lane == 0, total, jnp.where(lane == 1, squares, 0.0)).T[:8]
+
+
+def stats(hidden):
+    tokens, width = hidden.shape
+    size = tokens // 4
+    return pl.pallas_call(
+        stats_kernel,
+        grid=(4,),
+        in_specs=[pl.BlockSpec((size, width), lambda i: (i, 0))],
+        out_specs=pl.BlockSpec((8, size), lambda i: (0, i)),
+        out_shape=jax.ShapeDtypeStruct((8, tokens), jnp.float32),
+        cost_estimate=FREE,
+        compiler_params=pltpu.CompilerParams(vmem_limit_bytes=VMEM),
+    )(hidden)
+
+
+def modulate_kernel(width, at, ids, moments, values, table, out):
+    steps = table.shape[0] // 2
+    turned = token_columns(jnp.concatenate([moments[...][:2], ids[...].astype(jnp.float32)], axis=0))
+    mean = turned[:, :1] * (1.0 / width)
+    meansq = turned[:, 1:2] * (1.0 / width)
+    gain = lax.rsqrt(meansq - mean * mean + epsilon)
+    entries = table[...]
+    pieces = []
+    for _ in range(3):
+        piece = entries.astype(jnp.bfloat16).astype(jnp.float32)
+        entries = entries - piece
+        pieces.append(piece)
+    split = jnp.concatenate(pieces, axis=0).astype(jnp.bfloat16)
+
+    def lookup(kind):
+        onehot = chosen_rows(turned[:, 2:3], steps, kind, 3).astype(jnp.bfloat16)
+        return jnp.dot(onehot, split, preferred_element_type=jnp.float32)
+
+    normed = (values[...].astype(jnp.float32) - mean) * gain
+    out[...] = (normed * (1.0 + lookup(0)) + lookup(1)).astype(jnp.bfloat16)
+
+
+def modulate(plan, at_core, step_ids, moments, values, table, width):
+    tokens, local_width = values.shape
+    size = 2 * LANES
+    count = local_width // size
+    columns = pl.BlockSpec((tokens, size), lambda i, at: (0, i))
+    return gridded(
+        functools.partial(modulate_kernel, width),
+        plan,
+        count,
+        [
+            pl.BlockSpec((1, tokens), lambda i, at: (0, 0)),
+            pl.BlockSpec((8, tokens), lambda i, at: (0, 0)),
+            columns,
+            pl.BlockSpec((table.shape[0], size), lambda i, at: (0, at[at_core] * count + i)),
+        ],
+        columns,
+        jax.ShapeDtypeStruct(values.shape, jnp.bfloat16),
+        step_ids,
+        moments,
+        values,
+        table,
+    )
+
+
+def pipeline(count, make_part, stage, hooks, later, finish):
+    own, sent1, came1, came2, came3, owned = {}, {}, {}, {}, {}, {}
+    due2, due3 = {}, {}
+    for j in range(count):
+        due2[j] = max(j + 1, min(j + (LAG if j < LAST else 1), count))
+        due3[j] = due2[j] + 1
+
+    def begin(k, raw):
+        own[k], sent1[k] = make_part(k, raw)
+        came1[k] = lax.ppermute(sent1[k], "dp", swap(8, 2))
+
+    begin(0, stage(0))
+    begin(1, stage(1))
+    for k in range(max(due3.values()) + 1):
+        now2 = [j for j in range(count) if due2[j] == k]
+        now3 = [j for j in range(count) if due3[j] == k]
+        wanted = {"came2": [came2[j] for j in now2], "came3": [came3[j] for j in now3]}
+        if k < count:
+            wanted["came1"] = came1[k]
+        if k + 1 < count:
+            wanted["sent1"] = sent1[k + 1]
+        if k in hooks:
+            wanted["more"] = hooks[k][0]()
+        wanted = lax.optimization_barrier(wanted)
+        if k in hooks:
+            hooks[k][1](wanted["more"])
+        if k + 2 < count and k + 2 not in later:
+            raw, _ = lax.optimization_barrier((stage(k + 2), wanted["came1"]))
+            begin(k + 2, raw)
+            wanted, _ = lax.optimization_barrier((wanted, sent1[k + 2]))
+        ahead = []
+        if k < count:
+            came1[k] = wanted["came1"]
+            sent = add_sums(own[k], came1[k])
+            ahead.append(sent)
+            came2[k] = lax.ppermute(sent, "dp", swap(8, 4))
+        for j, came in zip(now2, wanted["came2"]):
+            owned[j], sent = total_sums(own[j], came1[j], came)
+            ahead.append(sent)
+            came3[j] = lax.ppermute(sent, "dp", swap(8))
+        for j, came in zip(now3, wanted["came3"]):
+            finish(j, owned[j], came)
+        if k + 2 < count and k + 2 in later:
+            raw, _ = lax.optimization_barrier((stage(k + 2), tuple(ahead)))
+            begin(k + 2, raw)
+
+
+def unpacked(message):
+    rows = message.shape[0] - TAIL
+    return message[:rows].astype(jnp.float32) * jnp.exp2(message[rows : rows + 1].astype(jnp.float32))
+
+
+def in_order(own, other):
+    side = lax.axis_index("dp") % 2
+    return jnp.where(side == 0, own, other), jnp.where(side == 0, other, own)
+
+
+def assemble(done, shared, scale):
+    core = lax.axis_index("tensor")
+    half = ROW_DEV // 2
+    cores = []
+    for which in range(2):
+        mine = done[which::2]
+        pieces = []
+        if shared:
+            pieces.append(mine[0][0] + mine[0][1])
+            mine = mine[1:]
+        ordered = [in_order(*pair) for pair in mine]
+        head = [ordered[0][0][:, :half], ordered[0][1][:, :half]]
+        ordered[0] = (ordered[0][0][:, half:], ordered[0][1][:, half:])
+        pieces = head + pieces + [pair[0] for pair in ordered] + [pair[1] for pair in ordered]
+        cores.append(jnp.concatenate(pieces, axis=1))
+    left = jnp.where(core == 0, cores[0], cores[1])
+    right = jnp.where(core == 0, cores[1], cores[0])
+    return jnp.concatenate([left, right], axis=1) * scale
+
+
+def body(hidden, attn_out, step_ids, modulation):
+    token_count = hidden.shape[0]
+    local_width = hidden.shape[1]
+    parts_tp = lax.axis_size("tensor")
+    dp = lax.axis_size("dp")
+    width = local_width * parts_tp
+    tokens = token_count * dp
+    factor = 2.0 / tokens
+    core_swap = swap(2)
+    side = lax.axis_index("dp") % 2
+    place = lax.axis_index("dp") // 2
+    blocks = local_width // LANES
+    store = {}
+
+    order = [place ^ 3, place ^ 1, place ^ 2, place]
+    arrived = [jnp.where(index // 2 == side, 2 + index % 2, index % 2) for index in order]
+
+    def owned_blocks(which, common):
+        rest = (blocks - 2 - common) // 2
+        return [which] + [2 + common + which * rest + i for i in range(rest)]
+
+    common = 4
+    attn_mine = owned_blocks(side, common)
+    attn_theirs = owned_blocks(1 - side, common)
+    qkv_mine = owned_blocks(side, 0)
+    qkv_theirs = owned_blocks(1 - side, 0)
+    first = 4
+
+    shared = [2 + i for i in range(common)]
+    core = lax.axis_index("tensor")
+
+    lists = ([core], order, arrived, shared, attn_mine, [side] + attn_theirs, qkv_mine, [side] + qkv_theirs)
+    at_core, at_order, at_arrived, at_shared, at_attn, at_attn_theirs, at_qkv, at_qkv_theirs = (
+        sum(len(entries) for entries in lists[:index]) for index in range(len(lists))
+    )
+    plan = jnp.stack([jnp.asarray(entry, jnp.int32) for entries in lists for entry in entries])
+
+    ids = step_ids.reshape(1, token_count)
+    table = modulation.reshape(2 * modulation.shape[0], width)
+
+    attn_rows = turn(plan, attn_out, at_order)
+    attn = attn_out
+    attn_far = lax.ppermute(attn, "tensor", core_swap)
+    attn_pair = lax.ppermute(pick(plan, attn, at_attn_theirs, 1 + len(attn_theirs)), "dp", swap(dp))
+
+    def qkv_input():
+        values, _ = lax.optimization_barrier((hidden, sent1_gate[0]))
+        moments = lax.psum(stats(values), "tensor")
+        return modulate(plan, at_core, ids, moments, values, table, width)
+
+    def qkv_ready(mod):
+        store["mod"] = mod
+        store["pieces"] = {}
+        store["far_pieces"] = {}
+        for index in range(len(PIECES)):
+            if index:
+                mod, _ = lax.optimization_barrier((mod, message))
+            message = pick(plan, mod, at_qkv_theirs + sum(PIECES[:index]), PIECES[index])
+            store["pieces"][index] = lax.ppermute(message, "dp", swap(dp))
+        store["mod_far"] = lax.ppermute(store["mod"], "tensor", core_swap)
+        store["rows"] = turn(plan, store["mod"], at_order)
+
+    sent1_gate = []
+    hooks = {0: (qkv_input, qkv_ready)}
+
+    count = len(attn_mine)
+    pair_sizes = (PIECES[0] - 1,) + PIECES[1:]
+
+    def stage(k):
+        needed = []
+        for kind, far, first, size in CHUNKS[k]:
+            if kind == "shared":
+                needed.append(attn_far if far else attn)
+            elif kind == "attn":
+                needed.append(fetched("attn", far, 0))
+            else:
+                needed.append([fetched("qkv", far, index) for index, _, _ in qkv_pieces(first, size)])
+        return needed
+
+    def fetched(kind, far, index):
+        if kind == "attn":
+            near = attn_pair
+        else:
+            near = store["pieces"][index]
+        if not far:
+            return near
+        key = (kind, index)
+        if key not in store:
+            store[key] = lax.ppermute(store.get(("near",) + key, near), "tensor", core_swap)
+        return store[key]
+
+    def landed(kind, far, index, value):
+        if not far and ("near", kind, index) not in store:
+            store["near", kind, index] = value
+            store[kind, index] = lax.ppermute(value, "tensor", core_swap)
+            if index == 0:
+                store["other_" + kind] = turn(plan, value, at_arrived)
+
+    def qkv_pieces(first, size):
+        held = []
+        for index, length in enumerate(pair_sizes):
+            start = sum(pair_sizes[:index])
+            low, high = max(first, start), min(first + size, start + length)
+            if low < high:
+                held.append((index, low - start, high - low))
+        return held
+
+    def make_part(k, raw):
+        columns, others = [], []
+        rows, other_rows = attn_rows, None
+        for (kind, far, first, size), held in zip(CHUNKS[k], raw):
+            if kind == "shared":
+                columns.append((held, at_shared + first, size))
+            elif kind == "attn":
+                landed("attn", far, 0, held)
+                columns.append((attn_far if far else attn, at_attn + first, size))
+                others.append((held, 1 + first, size))
+                other_rows = store["other_attn"]
+            else:
+                for (index, _, _), piece in zip(qkv_pieces(first, size), held):
+                    landed("qkv", far, index, piece)
+                rows, other_rows = store["rows"], store["other_qkv"]
+                columns.append((store["mod_far" if far else "mod"], at_qkv + first, size))
+                for (index, start, length), piece in zip(qkv_pieces(first, size), held):
+                    others.append((piece, start + (1 if index == 0 else 0), length))
+        result = gram(plan, rows, columns, other_rows, others)
+        if k == GATE:
+            sent1_gate.append(result[1])
+        return result
+
+    done = {}
+    results = {}
+
+    def finish(k, own, came):
+        values = unpacked(came)
+        at = 0
+        for kind, far, first, size in CHUNKS[k]:
+            end = at + size * LANES
+            done[kind, far, first] = (own[:, at:end], values[:, at:end])
+            at = end
+        if "out" not in results and len([key for key in done if key[0] != "qkv"]) == 4:
+            keys = [("shared", False, 0), ("shared", True, 0), ("attn", False, 0), ("attn", True, 0)]
+            results["out"] = assemble([done[key] for key in keys], True, factor)
+
+    pipeline(len(CHUNKS), make_part, stage, hooks, LATER, finish)
+    sides = []
+    for far in (False, True):
+        parts = [done[key] for key in sorted(key for key in done if key[0] == "qkv" and key[1] == far)]
+        sides.append(tuple(jnp.concatenate(pieces, axis=1) for pieces in zip(*parts)))
+    qkv_rows = assemble(sides, False, factor)
+    return (qkv_rows, results["out"])
+
+
 def solution(mesh):
+    lined = mesh.shape["dp"] == 8 and mesh.shape["tensor"] == 2
     return jax.shard_map(
-        body,
+        body if lined else plain_body,
         mesh=mesh,
         in_specs=(
             P(("groups", "dp"), "tensor"),

time: 493 us -> 186 us (0.38)
  waiting for transfers between devices: 435 us -> 71.4 us
  Pallas kernels: 0 us -> 55.8 us
  starting transfers between devices: 0.34 us -> 37.6 us
  matrix products: 29.2 us -> 0 us
  between operations: 13.8 us -> 1.62 us
  local copies, waits for them, and re-layouts: 0.1 us -> 10.9 us
  other arithmetic: 12 us -> 4.2 us
    reduce_scatter x2 -> x0, waiting for transfers between devices: 408 us -> none  [the longest x1 207 us: body(): lax.psum_scatter(part_out, 'dp', scatter_dimension=0, tiled=True)]
    ppermute x0 -> x32, waiting for transfers between devices: none -> 71.4 us  [the longest x8 51.6 us: pipeline(): came2[k] = lax.ppermute(sent, 'dp', swap(8, 4))]
    pallas_call x0 -> x33, Pallas kernels: none -> 55.8 us  [the longest x16 43.3 us: gridded(): pl.pallas_call(kernel, grid_spec=pltpu.PrefetchScalarGridSpec(num_scalar_...]
    ppermute x0 -> x32, starting transfers between devices: none -> 37.6 us  [the longest x8 16.1 us: begin(): came1[k] = lax.ppermute(sent1[k], 'dp', swap(8, 2))]
    dot_general x3 -> x0, matrix products: 29.2 us -> none  [the longest x2 23.2 us: gram_rows(): lax.dot_general(window, full, (((0,), (0,)), ((), ())), preferred_element...]
    all_gather x2 -> x0, waiting for transfers between devices: 25.7 us -> none  [the longest x1 18.7 us: body(): lax.all_gather(local_mod, 'tensor', axis=1, tiled=True)]
    unnamed x6 -> x90, local copies, waits for them, and re-layouts: 0.1 us -> 10.3 us
  transfers between devices with their start and end apart: 4 -> 32, of which waited for: 4 -> 15; matrix products, arithmetic and copies ran while one was open for 5% -> 2% of each run, Pallas kernels for 0% -> 30%
where the time goes in v2:
time: 186 us
  waiting for transfers between devices  71.4 us (38%)
  Pallas kernels  55.8 us (30%)
  starting transfers between devices  37.6 us (20%)
  local copies, waits for them, and re-layouts  10.9 us (6%)
  other arithmetic  4.2 us (2%)
  blocking collectives  3.96 us (2%)
    ppermute x8, waiting for transfers between devices, pipeline(): came2[k] = lax.ppermute(sent, 'dp', swap(8, 4))  51.6 us
    pallas_call x16, Pallas kernels, gridded(): pl.pallas_call(kernel, grid_spec=pltpu.PrefetchScalarGridSpec(num_scalar_...  43.3 us
    ppermute x8, starting transfers between devices, begin(): came1[k] = lax.ppermute(sent1[k], 'dp', swap(8, 2))  16.1 us
    ppermute x8, waiting for transfers between devices, begin(): came1[k] = lax.ppermute(sent1[k], 'dp', swap(8, 2))  13.5 us
    pallas_call x16, Pallas kernels, blocked(): pl.pallas_call(kernel, grid=(width // size,), in_specs=[pl.BlockSpec((row...  11.2 us
    unnamed x90, local copies, waits for them, and re-layouts  10.3 us
    ppermute x8, starting transfers between devices, pipeline(): came2[k] = lax.ppermute(sent, 'dp', swap(8, 4))  8.95 us
    ppermute x8, starting transfers between devices, pipeline(): came3[j] = lax.ppermute(sent, 'dp', swap(8))  6.44 us
  transfers between devices with their start and end apart: 32, of which 15 were waited for; matrix products, arithmetic and copies ran while one was open for 2% of the time, Pallas kernels for 30%

profile of v2, /device:TPU:0, one launch (start us, length us, event | category | flops | bytes accessed | tf_op | source)
XLA Modules:
  0.0 185.6 jit_solution(6435032538754854144)
XLA Ops:
  3.2 2.8 %shard_map.66 = bf16[512,1280]{1,0:T(8,128)(2,1)} custom-call(s32[35]{0:T(128)S(1)} %stack.115.at, bf16[512,3072]{1,0:T(8,128)(2,1)S(1)} %copy-done), custom_call_target="tpu_custom_call" | custom-call | tf_op jit(solution)/shard_map/pallas_call | solution.py:81
  6.0 2.7 %collective-permute-start.3 = (bf16[512,1280]{1,0:T(8,128)(2,1)}, bf16[512,1280]{1,0:T(8,128)(2,1)}, u32[]{:S(2)}, u32[]{:S(2)}) collective-permute-start(bf16[512,1280]{1,0:T(8,128)(2,1)} %shard_map.66), channel_id=1, source_target_pairs={{0,2},{2,0},{4,6},{6,4},{8,10},{10,8},{12,14},{14,12},{1,3},{3,1},... | collective-permute-start | bytes 3932168 | tf_op jit(solution)/shard_map/ppermute | solution.py:436
  9.8 3.0 %shard_map.60 = (f32[256,1024]{1,0:T(8,128)S(1)}, s16[272,1024]{1,0:T(8,128)(2,1)}) custom-call(s32[35]{0:T(128)S(1)} %stack.115.at, bf16[512,512]{1,0:T(8,128)(2,1)S(1)} %shard_map.59.rows, bf16[512,3072]{1,0:T(8,128)(2,1)S(1)} %copy-done), custom_call_target="tpu_custom_call" | custom-call | tf_op jit(solution)/shard_map/pallas_call | solution.py:81
  15.7 3.8 %shard_map.61 = (f32[256,1024]{1,0:T(8,128)S(1)}, s16[272,1024]{1,0:T(8,128)(2,1)S(1)}) custom-call(s32[35]{0:T(128)S(1)} %stack.115.at, bf16[512,512]{1,0:T(8,128)(2,1)S(1)} %shard_map.59.rows, bf16[512,3072]{1,0:T(8,128)(2,1)} %collective-permute-done.1.refs_0_), custom_call_target="tpu_custom_call" | custom-call | tf_op jit(solution)/shard_map/pallas_call | solution.py:81
  21.8 4.0 %psum.7.moments = f32[8,512]{1,0:T(8,128)} all-reduce(f32[8,512]{1,0:T(8,128)S(1)} %shard_map.62), channel_id=1, replica_groups=mesh['groups'=2,'dp'=8,'tensor'=2] {'tensor'}, use_global_device_ids=true, to_apply=%region_0.1 | all-reduce | flops 4096 | bytes 32768 | tf_op jit(solution)/shard_map/psum | solution.py:440
  25.8 1.9 %copy-done.9 = bf16[512,3072]{1,0:T(8,128)(2,1)S(1)} copy-done((bf16[512,3072]{1,0:T(8,128)(2,1)S(1)}, bf16[512,3072]{1,0:T(8,128)(2,1)}, u32[]{:S(2)}) %copy-start.9) | copy-done | bytes 3145752
  28.4 5.8 %shard_map.63.source.refs_0_ = bf16[512,3072]{1,0:T(8,128)(2,1)S(1)} custom-call(s32[35]{0:T(128)S(1)} %stack.115.at, s32[1,512]{1,0:T(1,128)S(1)} %bitcast.36, f32[8,512]{1,0:T(8,128)S(1)} %copy-done.33, bf16[512,3072]{1,0:T(8,128)(2,1)S(1)} %copy-done.9, f32[16,6144]{1,0:T(8,128)S(1)} %reshape.11.table), custom_call_target="tpu_custom_call" | custom-call | tf_op jit(solution)/shard_map/pallas_call | solution.py:81
  35.8 2.4 %collective-permute-done.3.source.refs_2_ = bf16[512,1280]{1,0:T(8,128)(2,1)} collective-permute-done((bf16[512,1280]{1,0:T(8,128)(2,1)}, bf16[512,1280]{1,0:T(8,128)(2,1)}, u32[]{:S(2)}, u32[]{:S(2)}) %collective-permute-start.3) | collective-permute-done | bytes 1310752 | tf_op jit(solution)/shard_map/ppermute | solution.py:436
  42.7 2.7 %shard_map.68.refs_1_ = bf16[512,512]{1,0:T(8,128)(2,1)S(1)} custom-call(s32[35]{0:T(128)S(1)} %stack.115.at, bf16[512,1280]{1,0:T(8,128)(2,1)} %collective-permute-done.3.source.refs_2_), custom_call_target="tpu_custom_call" | custom-call | tf_op jit(solution)/shard_map/pallas_call | solution.py:81
  45.4 4.1 %shard_map.69 = (f32[256,1024]{1,0:T(8,128)S(1)}, s16[272,1024]{1,0:T(8,128)(2,1)S(1)}) custom-call(s32[35]{0:T(128)S(1)} %stack.115.at, bf16[512,512]{1,0:T(8,128)(2,1)S(1)} %copy-done.7, bf16[512,3072]{1,0:T(8,128)(2,1)S(1)} %copy-done.1, bf16[512,512]{1,0:T(8,128)(2,1)S(1)} %shard_map.68.refs_1_, bf16[512,1280]{1,0:T(8,128)(2,1)} %collective-permute-done.3.source.refs_2_), custom_call_target="tpu_custom_call" | custom-call | tf_op jit(solution)/shard_map/pallas_call | solution.py:81
  50.0 6.6 %collective-permute-done.7.came.came1 = s16[272,1024]{1,0:T(8,128)(2,1)S(1)} collective-permute-done((s16[272,1024]{1,0:T(8,128)(2,1)S(1)}, s16[272,1024]{1,0:T(8,128)(2,1)S(1)}, u32[]{:S(2)}, u32[]{:S(2)}) %collective-permute-start.7) | collective-permute-done | bytes 557088 | tf_op jit(solution)/shard_map/ppermute | solution.py:325
  56.6 2.6 %collective-permute-start.5 = (s16[144,1024]{1,0:T(8,128)(2,1)S(1)}, s16[144,1024]{1,0:T(8,128)(2,1)S(1)}, u32[]{:S(2)}, u32[]{:S(2)}) collective-permute-start(s16[144,1024]{1,0:T(8,128)(2,1)S(1)} %shard_map.67), channel_id=1, source_target_pairs={{0,8},{2,10},{4,12},{6,14},{8,0},{10,2},{12,4},{14,6},{1,9},{3,11}... | collective-permute-start | bytes 884744 | tf_op jit(solution)/shard_map/ppermute | solution.py:351
  59.5 4.0 %shard_map.71 = (f32[256,1024]{1,0:T(8,128)S(1)}, s16[272,1024]{1,0:T(8,128)(2,1)S(1)}) custom-call(s32[35]{0:T(128)S(1)} %stack.115.at, bf16[512,512]{1,0:T(8,128)(2,1)S(1)} %copy-done.7, bf16[512,3072]{1,0:T(8,128)(2,1)} %collective-permute-done.1.refs_0_, bf16[512,512]{1,0:T(8,128)(2,1)S(1)} %shard_map.68.refs_1_, ...), custom_call_target="tpu_custom_call" | custom-call | tf_op jit(solution)/shard_map/pallas_call | solution.py:81
  63.6 9.7 %collective-permute-done.5.came2 = s16[144,1024]{1,0:T(8,128)(2,1)S(1)} collective-permute-done((s16[144,1024]{1,0:T(8,128)(2,1)S(1)}, s16[144,1024]{1,0:T(8,128)(2,1)S(1)}, u32[]{:S(2)}, u32[]{:S(2)}) %collective-permute-start.5) | collective-permute-done | bytes 294944 | tf_op jit(solution)/shard_map/ppermute | solution.py:351
  76.1 2.7 %collective-permute-start.10 = (s16[272,1024]{1,0:T(8,128)(2,1)S(1)}, s16[272,1024]{1,0:T(8,128)(2,1)S(1)}, u32[]{:S(2)}, u32[]{:S(2)}) collective-permute-start(s16[272,1024]{1,0:T(8,128)(2,1)S(1)} %get-tuple-element.79), channel_id=1, source_target_pairs={{0,4},{2,6},{4,0},{6,2},{8,12},{10,14},{12,8},{14,10},{1,5},{3,7},... | collective-permute-start | bytes 1671176 | tf_op jit(solution)/shard_map/ppermute | solution.py:325
  83.1 3.5 %shard_map.75 = (f32[256,1024]{1,0:T(8,128)S(1)}, s16[272,1024]{1,0:T(8,128)(2,1)}) custom-call(s32[35]{0:T(128)S(1)} %stack.115.at, bf16[512,512]{1,0:T(8,128)(2,1)S(1)} %shard_map.64.rows, bf16[512,3072]{1,0:T(8,128)(2,1)S(1)} %shard_map.63.source.refs_0_, bf16[512,512]{1,0:T(8,128)(2,1)S(1)} %shard_map.74.refs_1_, ...), custom_call_target="tpu_custom_call" | custom-call | tf_op jit(solution)/shard_map/pallas_call | solution.py:81
  86.6 11.0 %collective-permute-done.11.came2 = s16[144,1024]{1,0:T(8,128)(2,1)S(1)} collective-permute-done((s16[144,1024]{1,0:T(8,128)(2,1)S(1)}, s16[144,1024]{1,0:T(8,128)(2,1)S(1)}, u32[]{:S(2)}, u32[]{:S(2)}) %collective-permute-start.11) | collective-permute-done | bytes 294944 | tf_op jit(solution)/shard_map/ppermute | solution.py:351
  97.6 2.4 %collective-permute-start.8 = (s16[272,1024]{1,0:T(8,128)(2,1)}, s16[272,1024]{1,0:T(8,128)(2,1)}, u32[]{:S(2)}, u32[]{:S(2)}) collective-permute-start(s16[272,1024]{1,0:T(8,128)(2,1)} %get-tuple-element.85), channel_id=1, source_target_pairs={{0,4},{2,6},{4,0},{6,2},{8,12},{10,14},{12,8},{14,10},{1,5},{3,7},... | collective-permute-start | bytes 1671176 | tf_op jit(solution)/shard_map/ppermute | solution.py:325
  104.2 3.5 %shard_map.78 = (f32[256,1024]{1,0:T(8,128)S(1)}, s16[272,1024]{1,0:T(8,128)(2,1)}) custom-call(s32[35]{0:T(128)S(1)} %stack.115.at, bf16[512,512]{1,0:T(8,128)(2,1)S(1)} %shard_map.64.rows, bf16[512,3072]{1,0:T(8,128)(2,1)S(1)} %collective-permute-done.14.refs_0_, bf16[512,512]{1,0:T(8,128)(2,1)S(1)} %shard_map.74.refs_1_, ...), custom_call_target="tpu_custom_call" | custom-call | tf_op jit(solution)/shard_map/pallas_call | solution.py:81
  108.8 2.0 %collective-permute-start.19 = (s16[272,1024]{1,0:T(8,128)(2,1)}, s16[272,1024]{1,0:T(8,128)(2,1)}, u32[]{:S(2)}, u32[]{:S(2)}) collective-permute-start(s16[272,1024]{1,0:T(8,128)(2,1)} %get-tuple-element.91), channel_id=1, source_target_pairs={{0,4},{2,6},{4,0},{6,2},{8,12},{10,14},{12,8},{14,10},{1,5},{3,7},... | collective-permute-start | bytes 1671176 | tf_op jit(solution)/shard_map/ppermute | solution.py:325
  112.3 7.3 %collective-permute-done.9.came2 = s16[144,1024]{1,0:T(8,128)(2,1)} collective-permute-done((s16[144,1024]{1,0:T(8,128)(2,1)S(1)}, s16[144,1024]{1,0:T(8,128)(2,1)}, u32[]{:S(2)}, u32[]{:S(2)}) %collective-permute-start.9) | collective-permute-done | bytes 294944 | tf_op jit(solution)/shard_map/ppermute | solution.py:351
  119.5 3.5 %collective-permute-start.20 = (s16[144,1024]{1,0:T(8,128)(2,1)}, s16[144,1024]{1,0:T(8,128)(2,1)S(1)}, u32[]{:S(2)}, u32[]{:S(2)}) collective-permute-start(s16[144,1024]{1,0:T(8,128)(2,1)} %copy-done.28), channel_id=1, source_target_pairs={{0,8},{2,10},{4,12},{6,14},{8,0},{10,2},{12,4},{14,6},{1,9},{3,11}... | collective-permute-start | bytes 884744 | tf_op jit(solution)/shard_map/ppermute | solution.py:351
  129.3 2.5 %shard_map.82 = (f32[256,512]{1,0:T(8,128)S(1)}, s16[272,512]{1,0:T(8,128)(2,1)S(1)}) custom-call(s32[35]{0:T(128)S(1)} %stack.115.at, bf16[512,512]{1,0:T(8,128)(2,1)S(1)} %copy-done.3, bf16[512,3072]{1,0:T(8,128)(2,1)S(1)} %shard_map.63.source.refs_0_, bf16[512,512]{1,0:T(8,128)(2,1)S(1)} %copy-done.5, bf16[512,512]{1,0:T(8,128)(2,1)} %collective-permute-done.16.refs_2_), custom_call_target="tpu_custom_call" | custom-call | tf_op jit(solution)/shard_map/pallas_call | solution.py:81
  132.0 5.9 %collective-permute-done.20.came2 = s16[144,1024]{1,0:T(8,128)(2,1)S(1)} collective-permute-done((s16[144,1024]{1,0:T(8,128)(2,1)}, s16[144,1024]{1,0:T(8,128)(2,1)S(1)}, u32[]{:S(2)}, u32[]{:S(2)}) %collective-permute-start.20) | collective-permute-done | bytes 294944 | tf_op jit(solution)/shard_map/ppermute | solution.py:351
  138.0 3.4 %collective-permute-start.17 = (s16[272,512]{1,0:T(8,128)(2,1)S(1)}, s16[272,512]{1,0:T(8,128)(2,1)S(1)}, u32[]{:S(2)}, u32[]{:S(2)}) collective-permute-start(s16[272,512]{1,0:T(8,128)(2,1)S(1)} %get-tuple-element.97), channel_id=1, source_target_pairs={{0,4},{2,6},{4,0},{6,2},{8,12},{10,14},{12,8},{14,10},{1,5},{3,7},... | collective-permute-start | bytes 835592 | tf_op jit(solution)/shard_map/ppermute | solution.py:325
  145.6 2.0 %collective-permute-start.25 = (s16[272,512]{1,0:T(8,128)(2,1)S(1)}, s16[272,512]{1,0:T(8,128)(2,1)S(1)}, u32[]{:S(2)}, u32[]{:S(2)}) collective-permute-start(s16[272,512]{1,0:T(8,128)(2,1)S(1)} %get-tuple-element.103), channel_id=1, source_target_pairs={{0,4},{2,6},{4,0},{6,2},{8,12},{10,14},{12,8},{14,10},{1,5},{3,7},... | collective-permute-start | bytes 835592 | tf_op jit(solution)/shard_map/ppermute | solution.py:325
  147.7 4.8 %collective-permute-done.17.came.came1 = s16[272,512]{1,0:T(8,128)(2,1)S(1)} collective-permute-done((s16[272,512]{1,0:T(8,128)(2,1)S(1)}, s16[272,512]{1,0:T(8,128)(2,1)S(1)}, u32[]{:S(2)}, u32[]{:S(2)}) %collective-permute-start.17) | collective-permute-done | bytes 278560 | tf_op jit(solution)/shard_map/ppermute | solution.py:325
  152.4 5.0 %collective-permute-done.18.came2 = s16[144,1024]{1,0:T(8,128)(2,1)S(1)} collective-permute-done((s16[144,1024]{1,0:T(8,128)(2,1)S(1)}, s16[144,1024]{1,0:T(8,128)(2,1)S(1)}, u32[]{:S(2)}, u32[]{:S(2)}) %collective-permute-start.18) | collective-permute-done | bytes 294944 | tf_op jit(solution)/shard_map/ppermute | solution.py:351
  162.5 5.4 %collective-permute-done.26.came2 = s16[144,1024]{1,0:T(8,128)(2,1)S(1)} collective-permute-done((s16[144,1024]{1,0:T(8,128)(2,1)S(1)}, s16[144,1024]{1,0:T(8,128)(2,1)S(1)}, u32[]{:S(2)}, u32[]{:S(2)}) %collective-permute-start.26) | collective-permute-done | bytes 294944 | tf_op jit(solution)/shard_map/ppermute | solution.py:351
  170.1 4.2 %collective-permute-done.24.came2 = s16[144,512]{1,0:T(8,128)(2,1)S(1)} collective-permute-done((s16[144,512]{1,0:T(8,128)(2,1)S(1)}, s16[144,512]{1,0:T(8,128)(2,1)S(1)}, u32[]{:S(2)}, u32[]{:S(2)}) %collective-permute-start.24) | collective-permute-done | bytes 147488 | tf_op jit(solution)/shard_map/ppermute | solution.py:351
  174.2 3.1 %collective-permute-done.28.came2 = s16[144,512]{1,0:T(8,128)(2,1)S(1)} collective-permute-done((s16[144,512]{1,0:T(8,128)(2,1)S(1)}, s16[144,512]{1,0:T(8,128)(2,1)S(1)}, u32[]{:S(2)}, u32[]{:S(2)}) %collective-permute-start.28) | collective-permute-done | bytes 147488 | tf_op jit(solution)/shard_map/ppermute | solution.py:351
  179.9 3.0 %collective-permute-done.30 = s16[80,512]{1,0:T(8,128)(2,1)S(1)} collective-permute-done((s16[80,512]{1,0:T(8,128)(2,1)S(1)}, s16[80,512]{1,0:T(8,128)(2,1)S(1)}, u32[]{:S(2)}, u32[]{:S(2)}) %collective-permute-start.30) | collective-permute-done | bytes 81952 | tf_op jit(solution)/shard_map/ppermute | solution.py:355
  (190 shorter events, 52.7 us)
Async XLA Ops:
  0.6 15.1 %collective-permute-start.1 = (bf16[512,3072]{1,0:T(8,128)(2,1)}, bf16[512,3072]{1,0:T(8,128)(2,1)}, u32[]{:S(2)}, u32[]{:S(2)}) collective-permute-start(bf16[512,3072]{1,0:T(8,128)(2,1)} %refs_0_.3), channel_id=1, source_target_pairs={{0,1},{1,0},{2,3},{3,2},{4,5},{5,4},{6,7},{7,6},{8,9},{9,8},{10,11... | collective-permute-start | bytes 9437192 | tf_op jit(solution)/shard_map/ppermute | solution.py:435
  6.0 32.3 %collective-permute-start.3 = (bf16[512,1280]{1,0:T(8,128)(2,1)}, bf16[512,1280]{1,0:T(8,128)(2,1)}, u32[]{:S(2)}, u32[]{:S(2)}) collective-permute-start(bf16[512,1280]{1,0:T(8,128)(2,1)} %shard_map.66), channel_id=1, source_target_pairs={{0,2},{2,0},{4,6},{6,4},{8,10},{10,8},{12,14},{14,12},{1,3},{3,1},... | collective-permute-start | bytes 3932168 | tf_op jit(solution)/shard_map/ppermute | solution.py:436
  13.9 20.3 %collective-permute-start = (s16[272,1024]{1,0:T(8,128)(2,1)}, s16[272,1024]{1,0:T(8,128)(2,1)}, u32[]{:S(2)}, u32[]{:S(2)}) collective-permute-start(s16[272,1024]{1,0:T(8,128)(2,1)} %get-tuple-element.67), channel_id=1, source_target_pairs={{0,4},{2,6},{4,0},{6,2},{8,12},{10,14},{12,8},{14,10},{1,5},{3,7},... | collective-permute-start | bytes 1671176 | tf_op jit(solution)/shard_map/ppermute | solution.py:325
  34.2 70.0 %collective-permute-start.14 = (bf16[512,3072]{1,0:T(8,128)(2,1)S(1)}, bf16[512,3072]{1,0:T(8,128)(2,1)S(1)}, u32[]{:S(2)}, u32[]{:S(2)}) collective-permute-start(bf16[512,3072]{1,0:T(8,128)(2,1)S(1)} %shard_map.63.source.refs_0_), channel_id=1, source_target_pairs={{0,1},{1,0},{2,3},{3,2},{4,5},{5,4},{6,7},{7,6},{8,9},{9,8},{10,11... | collective-permute-start | bytes 9437192 | tf_op jit(solution)/shard_map/ppermute | solution.py:452
  38.3 21.3 %collective-permute-start.6 = (bf16[512,1280]{1,0:T(8,128)(2,1)}, bf16[512,1280]{1,0:T(8,128)(2,1)S(1)}, u32[]{:S(2)}, u32[]{:S(2)}) collective-permute-start(bf16[512,1280]{1,0:T(8,128)(2,1)} %collective-permute-done.3.source.refs_2_), channel_id=1, source_target_pairs={{0,1},{1,0},{2,3},{3,2},{4,5},{5,4},{6,7},{7,6},{8,9},{9,8},{10,11... | collective-permute-start | bytes 3932168 | tf_op jit(solution)/shard_map/ppermute | solution.py:487
  39.3 36.7 %collective-permute-start.2 = (bf16[512,1280]{1,0:T(8,128)(2,1)S(1)}, bf16[512,1280]{1,0:T(8,128)(2,1)S(1)}, u32[]{:S(2)}, u32[]{:S(2)}) collective-permute-start(bf16[512,1280]{1,0:T(8,128)(2,1)S(1)} %shard_map.65), channel_id=1, source_target_pairs={{0,2},{2,0},{4,6},{6,4},{8,10},{10,8},{12,14},{14,12},{1,3},{3,1},... | collective-permute-start | bytes 3932168 | tf_op jit(solution)/shard_map/ppermute | solution.py:451
  41.1 15.5 %collective-permute-start.7 = (s16[272,1024]{1,0:T(8,128)(2,1)S(1)}, s16[272,1024]{1,0:T(8,128)(2,1)S(1)}, u32[]{:S(2)}, u32[]{:S(2)}) collective-permute-start(s16[272,1024]{1,0:T(8,128)(2,1)S(1)} %copy-done.36), channel_id=1, source_target_pairs={{0,4},{2,6},{4,0},{6,2},{8,12},{10,14},{12,8},{14,10},{1,5},{3,7},... | collective-permute-start | bytes 1671176 | tf_op jit(solution)/shard_map/ppermute | solution.py:325
  49.5 24.6 %collective-permute-start.4 = (s16[272,1024]{1,0:T(8,128)(2,1)S(1)}, s16[272,1024]{1,0:T(8,128)(2,1)S(1)}, u32[]{:S(2)}, u32[]{:S(2)}) collective-permute-start(s16[272,1024]{1,0:T(8,128)(2,1)S(1)} %get-tuple-element.75), channel_id=1, source_target_pairs={{0,4},{2,6},{4,0},{6,2},{8,12},{10,14},{12,8},{14,10},{1,5},{3,7},... | collective-permute-start | bytes 1671176 | tf_op jit(solution)/shard_map/ppermute | solution.py:325
  56.6 16.6 %collective-permute-start.5 = (s16[144,1024]{1,0:T(8,128)(2,1)S(1)}, s16[144,1024]{1,0:T(8,128)(2,1)S(1)}, u32[]{:S(2)}, u32[]{:S(2)}) collective-permute-start(s16[144,1024]{1,0:T(8,128)(2,1)S(1)} %shard_map.67), channel_id=1, source_target_pairs={{0,8},{2,10},{4,12},{6,14},{8,0},{10,2},{12,4},{14,6},{1,9},{3,11}... | collective-permute-start | bytes 884744 | tf_op jit(solution)/shard_map/ppermute | solution.py:351
  76.0 27.9 %collective-permute-start.15 = (bf16[512,1280]{1,0:T(8,128)(2,1)S(1)}, bf16[512,1280]{1,0:T(8,128)(2,1)S(1)}, u32[]{:S(2)}, u32[]{:S(2)}) collective-permute-start(bf16[512,1280]{1,0:T(8,128)(2,1)S(1)} %collective-permute-done.2.source.refs_2_), channel_id=1, source_target_pairs={{0,1},{1,0},{2,3},{3,2},{4,5},{5,4},{6,7},{7,6},{8,9},{9,8},{10,11... | collective-permute-start | bytes 3932168 | tf_op jit(solution)/shard_map/ppermute | solution.py:487
  76.1 25.9 %collective-permute-start.10 = (s16[272,1024]{1,0:T(8,128)(2,1)S(1)}, s16[272,1024]{1,0:T(8,128)(2,1)S(1)}, u32[]{:S(2)}, u32[]{:S(2)}) collective-permute-start(s16[272,1024]{1,0:T(8,128)(2,1)S(1)} %get-tuple-element.79), channel_id=1, source_target_pairs={{0,4},{2,6},{4,0},{6,2},{8,12},{10,14},{12,8},{14,10},{1,5},{3,7},... | collective-permute-start | bytes 1671176 | tf_op jit(solution)/shard_map/ppermute | solution.py:325
  78.8 18.8 %collective-permute-start.11 = (s16[144,1024]{1,0:T(8,128)(2,1)S(1)}, s16[144,1024]{1,0:T(8,128)(2,1)S(1)}, u32[]{:S(2)}, u32[]{:S(2)}) collective-permute-start(s16[144,1024]{1,0:T(8,128)(2,1)S(1)} %shard_map.70), channel_id=1, source_target_pairs={{0,8},{2,10},{4,12},{6,14},{8,0},{10,2},{12,4},{14,6},{1,9},{3,11}... | collective-permute-start | bytes 884744 | tf_op jit(solution)/shard_map/ppermute | solution.py:351
  80.4 21.1 %collective-permute-start.12 = (s16[80,1024]{1,0:T(8,128)(2,1)S(1)}, s16[80,1024]{1,0:T(8,128)(2,1)S(1)}, u32[]{:S(2)}, u32[]{:S(2)}) collective-permute-start(s16[80,1024]{1,0:T(8,128)(2,1)S(1)} %get-tuple-element.82), channel_id=1, source_target_pairs={{0,2},{2,0},{4,6},{6,4},{8,10},{10,8},{12,14},{14,12},{1,3},{3,1},... | collective-permute-start | bytes 491528 | tf_op jit(solution)/shard_map/ppermute | solution.py:355
  97.6 26.2 %collective-permute-start.8 = (s16[272,1024]{1,0:T(8,128)(2,1)}, s16[272,1024]{1,0:T(8,128)(2,1)}, u32[]{:S(2)}, u32[]{:S(2)}) collective-permute-start(s16[272,1024]{1,0:T(8,128)(2,1)} %get-tuple-element.85), channel_id=1, source_target_pairs={{0,4},{2,6},{4,0},{6,2},{8,12},{10,14},{12,8},{14,10},{1,5},{3,7},... | collective-permute-start | bytes 1671176 | tf_op jit(solution)/shard_map/ppermute | solution.py:325
  101.5 27.8 %collective-permute-start.16 = (bf16[512,512]{1,0:T(8,128)(2,1)}, bf16[512,512]{1,0:T(8,128)(2,1)}, u32[]{:S(2)}, u32[]{:S(2)}) collective-permute-start(bf16[512,512]{1,0:T(8,128)(2,1)} %shard_map.79), channel_id=1, source_target_pairs={{0,2},{2,0},{4,6},{6,4},{8,10},{10,8},{12,14},{14,12},{1,3},{3,1},... | collective-permute-start | bytes 1572872 | tf_op jit(solution)/shard_map/ppermute | solution.py:451
  102.1 17.4 %collective-permute-start.9 = (s16[144,1024]{1,0:T(8,128)(2,1)S(1)}, s16[144,1024]{1,0:T(8,128)(2,1)}, u32[]{:S(2)}, u32[]{:S(2)}) collective-permute-start(s16[144,1024]{1,0:T(8,128)(2,1)S(1)} %shard_map.72), channel_id=1, source_target_pairs={{0,8},{2,10},{4,12},{6,14},{8,0},{10,2},{12,4},{14,6},{1,9},{3,11}... | collective-permute-start | bytes 884744 | tf_op jit(solution)/shard_map/ppermute | solution.py:351
  108.8 32.6 %collective-permute-start.19 = (s16[272,1024]{1,0:T(8,128)(2,1)}, s16[272,1024]{1,0:T(8,128)(2,1)}, u32[]{:S(2)}, u32[]{:S(2)}) collective-permute-start(s16[272,1024]{1,0:T(8,128)(2,1)} %get-tuple-element.91), channel_id=1, source_target_pairs={{0,4},{2,6},{4,0},{6,2},{8,12},{10,14},{12,8},{14,10},{1,5},{3,7},... | collective-permute-start | bytes 1671176 | tf_op jit(solution)/shard_map/ppermute | solution.py:325
  110.8 13.0 %collective-permute-start.13 = (s16[80,1024]{1,0:T(8,128)(2,1)}, s16[80,1024]{1,0:T(8,128)(2,1)S(1)}, u32[]{:S(2)}, u32[]{:S(2)}) collective-permute-start(s16[80,1024]{1,0:T(8,128)(2,1)} %copy-done.37), channel_id=1, source_target_pairs={{0,2},{2,0},{4,6},{6,4},{8,10},{10,8},{12,14},{14,12},{1,3},{3,1},... | collective-permute-start | bytes 491528 | tf_op jit(solution)/shard_map/ppermute | solution.py:355
  119.5 18.4 %collective-permute-start.20 = (s16[144,1024]{1,0:T(8,128)(2,1)}, s16[144,1024]{1,0:T(8,128)(2,1)S(1)}, u32[]{:S(2)}, u32[]{:S(2)}) collective-permute-start(s16[144,1024]{1,0:T(8,128)(2,1)} %copy-done.28), channel_id=1, source_target_pairs={{0,8},{2,10},{4,12},{6,14},{8,0},{10,2},{12,4},{14,6},{1,9},{3,11}... | collective-permute-start | bytes 884744 | tf_op jit(solution)/shard_map/ppermute | solution.py:351
  127.4 14.0 %collective-permute-start.21 = (s16[80,1024]{1,0:T(8,128)(2,1)S(1)}, s16[80,1024]{1,0:T(8,128)(2,1)S(1)}, u32[]{:S(2)}, u32[]{:S(2)}) collective-permute-start(s16[80,1024]{1,0:T(8,128)(2,1)S(1)} %get-tuple-element.95), channel_id=1, source_target_pairs={{0,2},{2,0},{4,6},{6,4},{8,10},{10,8},{12,14},{14,12},{1,3},{3,1},... | collective-permute-start | bytes 491528 | tf_op jit(solution)/shard_map/ppermute | solution.py:355
  131.8 12.0 %collective-permute-start.23 = (bf16[512,512]{1,0:T(8,128)(2,1)}, bf16[512,512]{1,0:T(8,128)(2,1)S(1)}, u32[]{:S(2)}, u32[]{:S(2)}) collective-permute-start(bf16[512,512]{1,0:T(8,128)(2,1)} %collective-permute-done.16.refs_2_), channel_id=1, source_target_pairs={{0,1},{1,0},{2,3},{3,2},{4,5},{5,4},{6,7},{7,6},{8,9},{9,8},{10,11... | collective-permute-start | bytes 1572872 | tf_op jit(solution)/shard_map/ppermute | solution.py:487
  131.9 25.5 %collective-permute-start.18 = (s16[144,1024]{1,0:T(8,128)(2,1)S(1)}, s16[144,1024]{1,0:T(8,128)(2,1)S(1)}, u32[]{:S(2)}, u32[]{:S(2)}) collective-permute-start(s16[144,1024]{1,0:T(8,128)(2,1)S(1)} %shard_map.80), channel_id=1, source_target_pairs={{0,8},{2,10},{4,12},{6,14},{8,0},{10,2},{12,4},{14,6},{1,9},{3,11}... | collective-permute-start | bytes 884744 | tf_op jit(solution)/shard_map/ppermute | solution.py:351
  138.0 14.5 %collective-permute-start.17 = (s16[272,512]{1,0:T(8,128)(2,1)S(1)}, s16[272,512]{1,0:T(8,128)(2,1)S(1)}, u32[]{:S(2)}, u32[]{:S(2)}) collective-permute-start(s16[272,512]{1,0:T(8,128)(2,1)S(1)} %get-tuple-element.97), channel_id=1, source_target_pairs={{0,4},{2,6},{4,0},{6,2},{8,12},{10,14},{12,8},{14,10},{1,5},{3,7},... | collective-permute-start | bytes 835592 | tf_op jit(solution)/shard_map/ppermute | solution.py:325
  141.9 15.6 %collective-permute-start.22 = (s16[80,1024]{1,0:T(8,128)(2,1)S(1)}, s16[80,1024]{1,0:T(8,128)(2,1)S(1)}, u32[]{:S(2)}, u32[]{:S(2)}) collective-permute-start(s16[80,1024]{1,0:T(8,128)(2,1)S(1)} %get-tuple-element.99), channel_id=1, source_target_pairs={{0,2},{2,0},{4,6},{6,4},{8,10},{10,8},{12,14},{14,12},{1,3},{3,1},... | collective-permute-start | bytes 491528 | tf_op jit(solution)/shard_map/ppermute | solution.py:355
  143.7 24.2 %collective-permute-start.26 = (s16[144,1024]{1,0:T(8,128)(2,1)S(1)}, s16[144,1024]{1,0:T(8,128)(2,1)S(1)}, u32[]{:S(2)}, u32[]{:S(2)}) collective-permute-start(s16[144,1024]{1,0:T(8,128)(2,1)S(1)} %shard_map.84), channel_id=1, source_target_pairs={{0,8},{2,10},{4,12},{6,14},{8,0},{10,2},{12,4},{14,6},{1,9},{3,11}... | collective-permute-start | bytes 884744 | tf_op jit(solution)/shard_map/ppermute | solution.py:351
  145.6 16.9 %collective-permute-start.25 = (s16[272,512]{1,0:T(8,128)(2,1)S(1)}, s16[272,512]{1,0:T(8,128)(2,1)S(1)}, u32[]{:S(2)}, u32[]{:S(2)}) collective-permute-start(s16[272,512]{1,0:T(8,128)(2,1)S(1)} %get-tuple-element.103), channel_id=1, source_target_pairs={{0,4},{2,6},{4,0},{6,2},{8,12},{10,14},{12,8},{14,10},{1,5},{3,7},... | collective-permute-start | bytes 835592 | tf_op jit(solution)/shard_map/ppermute | solution.py:325
  159.0 9.0 %collective-permute-start.27 = (s16[80,1024]{1,0:T(8,128)(2,1)S(1)}, s16[80,1024]{1,0:T(8,128)(2,1)S(1)}, u32[]{:S(2)}, u32[]{:S(2)}) collective-permute-start(s16[80,1024]{1,0:T(8,128)(2,1)S(1)} %get-tuple-element.109), channel_id=1, source_target_pairs={{0,2},{2,0},{4,6},{6,4},{8,10},{10,8},{12,14},{14,12},{1,3},{3,1},... | collective-permute-start | bytes 491528 | tf_op jit(solution)/shard_map/ppermute | solution.py:355
  159.6 14.6 %collective-permute-start.24 = (s16[144,512]{1,0:T(8,128)(2,1)S(1)}, s16[144,512]{1,0:T(8,128)(2,1)S(1)}, u32[]{:S(2)}, u32[]{:S(2)}) collective-permute-start(s16[144,512]{1,0:T(8,128)(2,1)S(1)} %shard_map.87), channel_id=1, source_target_pairs={{0,8},{2,10},{4,12},{6,14},{8,0},{10,2},{12,4},{14,6},{1,9},{3,11}... | collective-permute-start | bytes 442376 | tf_op jit(solution)/shard_map/ppermute | solution.py:351
  168.0 9.3 %collective-permute-start.28 = (s16[144,512]{1,0:T(8,128)(2,1)S(1)}, s16[144,512]{1,0:T(8,128)(2,1)S(1)}, u32[]{:S(2)}, u32[]{:S(2)}) collective-permute-start(s16[144,512]{1,0:T(8,128)(2,1)S(1)} %shard_map.88), channel_id=1, source_target_pairs={{0,8},{2,10},{4,12},{6,14},{8,0},{10,2},{12,4},{14,6},{1,9},{3,11}... | collective-permute-start | bytes 442376 | tf_op jit(solution)/shard_map/ppermute | solution.py:351
  169.4 7.9 %collective-permute-start.29 = (s16[80,1024]{1,0:T(8,128)(2,1)S(1)}, s16[80,1024]{1,0:T(8,128)(2,1)S(1)}, u32[]{:S(2)}, u32[]{:S(2)}) collective-permute-start(s16[80,1024]{1,0:T(8,128)(2,1)S(1)} %get-tuple-element.112), channel_id=1, source_target_pairs={{0,2},{2,0},{4,6},{6,4},{8,10},{10,8},{12,14},{14,12},{1,3},{3,1},... | collective-permute-start | bytes 491528 | tf_op jit(solution)/shard_map/ppermute | solution.py:355
  177.5 5.4 %collective-permute-start.30 = (s16[80,512]{1,0:T(8,128)(2,1)S(1)}, s16[80,512]{1,0:T(8,128)(2,1)S(1)}, u32[]{:S(2)}, u32[]{:S(2)}) collective-permute-start(s16[80,512]{1,0:T(8,128)(2,1)S(1)} %get-tuple-element.116), channel_id=1, source_target_pairs={{0,2},{2,0},{4,6},{6,4},{8,10},{10,8},{12,14},{14,12},{1,3},{3,1},... | collective-permute-start | bytes 245768 | tf_op jit(solution)/shard_map/ppermute | solution.py:355
  178.2 5.5 %collective-permute-start.31 = (s16[80,512]{1,0:T(8,128)(2,1)S(1)}, s16[80,512]{1,0:T(8,128)(2,1)S(1)}, u32[]{:S(2)}, u32[]{:S(2)}) collective-permute-start(s16[80,512]{1,0:T(8,128)(2,1)S(1)} %get-tuple-element.118), channel_id=1, source_target_pairs={{0,2},{2,0},{4,6},{6,4},{8,10},{10,8},{12,14},{14,12},{1,3},{3,1},... | collective-permute-start | bytes 245768 | tf_op jit(solution)/shard_map/ppermute | solution.py:355
  (41 other events, 303.6 us)

commit v3 on v2

--- a/solution.py
+++ b/solution.py
@@ -14,7 +14,14 @@
 epsilon = 1e-06
 VMEM = 16 << 20
 TAIL = 16
-LAG = 2
+LAG = 1
+FIRST = False
+DOUBLES = (0,)
+COMMON = 4
+PAIR = 2
+ROWS_AT = 1
+PICK_LATE = False
+EARLY = False
 LATER = (2, 3, 4, 5, 6, 7)
 LAST = 8
 GATE = 1
@@ -140,16 +147,19 @@
 
 
 def chosen_piece(step, starts, pieces):
-    values = pieces[0][...]
-    for start, piece in zip(starts[1:], pieces[1:]):
-        values = jnp.where(step < start, values, piece[...])
-    return values
+    sides = []
+    for lane in range(PAIR):
+        values = pieces[lane][...]
+        for index, start in enumerate(starts[1:], 1):
+            values = jnp.where(step < start, values, pieces[index * PAIR + lane][...])
+        sides.append(values)
+    return jnp.concatenate(sides, axis=1) if PAIR > 1 else sides[0]
 
 
 def gram_kernel(starts, at, rows, *refs):
     own, message = refs[-2:]
     step = pl.program_id(0)
-    mine = len(starts[0])
+    mine = len(starts[0]) * PAIR
     total = jnp.dot(rows[...], chosen_piece(step, starts[0], refs[:mine]), preferred_element_type=jnp.float32)
     if starts[1]:
         columns = chosen_piece(step, starts[1], refs[mine + 1 : -2])
@@ -170,25 +180,27 @@
             operands.append(other_rows)
         start = 0
         for array, base, held in pieces:
-
-            def place(i, at, listed=group == 0, base=base, held=held, start=start):
-                index = jnp.clip(i - start, 0, held - 1) + base
-                return (0, at[index] if listed else index)
-
-            in_specs.append(pl.BlockSpec((tokens, LANES), place))
-            operands.append(array)
+            for lane in range(PAIR):
+
+                def place(i, at, listed=group == 0, base=base, held=held, start=start, lane=lane):
+                    index = jnp.clip(i - start, 0, held // PAIR - 1) * PAIR + lane + base
+                    return (0, at[index] if listed else index)
+
+                in_specs.append(pl.BlockSpec((tokens, LANES), place))
+                operands.append(array)
             starts[group].append(start)
-            start += held
+            start += held // PAIR
     count = sum(held for _, _, held in columns)
     width = LANES * count
     own = ROW_DEV // 2
     sent = ROW_DEV - own + TAIL
+    size = LANES * PAIR
     return gridded(
         functools.partial(gram_kernel, tuple(map(tuple, starts))),
         plan,
-        count,
+        count // PAIR,
         in_specs,
-        [pl.BlockSpec((own, LANES), lambda i, at: (0, i)), pl.BlockSpec((sent, LANES), lambda i, at: (0, i))],
+        [pl.BlockSpec((own, size), lambda i, at: (0, i)), pl.BlockSpec((sent, size), lambda i, at: (0, i))],
         [jax.ShapeDtypeStruct((own, width), jnp.float32), jax.ShapeDtypeStruct((sent, width), jnp.int16)],
         *operands,
     )
@@ -313,7 +325,7 @@
     )
 
 
-def pipeline(count, make_part, stage, hooks, later, finish):
+def pipeline(count, make_part, stage, hooks, extras, later, finish):
     own, sent1, came1, came2, came3, owned = {}, {}, {}, {}, {}, {}
     due2, due3 = {}, {}
     for j in range(count):
@@ -325,20 +337,33 @@
         came1[k] = lax.ppermute(sent1[k], "dp", swap(8, 2))
 
     begin(0, stage(0))
-    begin(1, stage(1))
+    if GATE:
+        begin(1, stage(1))
+    else:
+        ready, raw = lax.optimization_barrier((hooks[0][0](), stage(1)))
+        hooks = {0: (lambda: ready, hooks[0][1])}
+        begin(1, raw)
     for k in range(max(due3.values()) + 1):
         now2 = [j for j in range(count) if due2[j] == k]
         now3 = [j for j in range(count) if due3[j] == k]
-        wanted = {"came2": [came2[j] for j in now2], "came3": [came3[j] for j in now3]}
+        wanted = {}
         if k < count:
             wanted["came1"] = came1[k]
         if k + 1 < count:
             wanted["sent1"] = sent1[k + 1]
         if k in hooks:
             wanted["more"] = hooks[k][0]()
+        if k in extras:
+            wanted["extra"] = extras[k][0]()
+        if k in DOUBLES:
+            wanted["next1"] = came1[k + 1]
         wanted = lax.optimization_barrier(wanted)
         if k in hooks:
             hooks[k][1](wanted["more"])
+        if k in extras:
+            extras[k][1](wanted["extra"])
+        if k in DOUBLES:
+            came1[k + 1] = wanted["next1"]
         if k + 2 < count and k + 2 not in later:
             raw, _ = lax.optimization_barrier((stage(k + 2), wanted["came1"]))
             begin(k + 2, raw)
@@ -349,13 +374,20 @@
             sent = add_sums(own[k], came1[k])
             ahead.append(sent)
             came2[k] = lax.ppermute(sent, "dp", swap(8, 4))
-        for j, came in zip(now2, wanted["came2"]):
+        rest = {"came2": [came2[j] for j in now2]}
+        rest, _ = lax.optimization_barrier((rest, wanted["came1"] if FIRST and k < count else ahead))
+        if EARLY and k + 2 < count and k + 2 in later:
+            raw, _ = lax.optimization_barrier((stage(k + 2), tuple(ahead)))
+            begin(k + 2, raw)
+            rest, _ = lax.optimization_barrier((rest, sent1[k + 2]))
+        for j, came in zip(now2, rest["came2"]):
             owned[j], sent = total_sums(own[j], came1[j], came)
             ahead.append(sent)
             came3[j] = lax.ppermute(sent, "dp", swap(8))
-        for j, came in zip(now3, wanted["came3"]):
+        ended, _ = lax.optimization_barrier(([came3[j] for j in now3], tuple(ahead)))
+        for j, came in zip(now3, ended):
             finish(j, owned[j], came)
-        if k + 2 < count and k + 2 in later:
+        if not EARLY and k + 2 < count and k + 2 in later:
             raw, _ = lax.optimization_barrier((stage(k + 2), tuple(ahead)))
             begin(k + 2, raw)
 
@@ -411,7 +443,7 @@
         rest = (blocks - 2 - common) // 2
         return [which] + [2 + common + which * rest + i for i in range(rest)]
 
-    common = 4
+    common = COMMON
     attn_mine = owned_blocks(side, common)
     attn_theirs = owned_blocks(1 - side, common)
     qkv_mine = owned_blocks(side, 0)
@@ -433,7 +465,8 @@
     attn_rows = turn(plan, attn_out, at_order)
     attn = attn_out
     attn_far = lax.ppermute(attn, "tensor", core_swap)
-    attn_pair = lax.ppermute(pick(plan, attn, at_attn_theirs, 1 + len(attn_theirs)), "dp", swap(dp))
+    if not PICK_LATE:
+        store["attn_pair"] = lax.ppermute(pick(plan, attn, at_attn_theirs, 1 + len(attn_theirs)), "dp", swap(dp))
 
     def qkv_input():
         values, _ = lax.optimization_barrier((hidden, sent1_gate[0]))
@@ -453,6 +486,9 @@
         store["rows"] = turn(plan, store["mod"], at_order)
 
     sent1_gate = []
+    extras = {}
+    if ROWS_AT:
+        extras[ROWS_AT] = (lambda: store["rows"], lambda value: store.update(rows=value))
     hooks = {0: (qkv_input, qkv_ready)}
 
     count = len(attn_mine)
@@ -471,7 +507,7 @@
 
     def fetched(kind, far, index):
         if kind == "attn":
-            near = attn_pair
+            near = store["attn_pair"]
         else:
             near = store["pieces"][index]
         if not far:
@@ -516,6 +552,9 @@
                 for (index, start, length), piece in zip(qkv_pieces(first, size), held):
                     others.append((piece, start + (1 if index == 0 else 0), length))
         result = gram(plan, rows, columns, other_rows, others)
+        if k == 0 and PICK_LATE:
+            late, _ = lax.optimization_barrier((attn, result[1]))
+            store["attn_pair"] = lax.ppermute(pick(plan, late, at_attn_theirs, 1 + len(attn_theirs)), "dp", swap(dp))
         if k == GATE:
             sent1_gate.append(result[1])
         return result
@@ -530,16 +569,17 @@
             end = at + size * LANES
             done[kind, far, first] = (own[:, at:end], values[:, at:end])
             at = end
-        if "out" not in results and len([key for key in done if key[0] != "qkv"]) == 4:
-            keys = [("shared", False, 0), ("shared", True, 0), ("attn", False, 0), ("attn", True, 0)]
-            results["out"] = assemble([done[key] for key in keys], True, factor)
-
-    pipeline(len(CHUNKS), make_part, stage, hooks, LATER, finish)
-    sides = []
-    for far in (False, True):
-        parts = [done[key] for key in sorted(key for key in done if key[0] == "qkv" and key[1] == far)]
-        sides.append(tuple(jnp.concatenate(pieces, axis=1) for pieces in zip(*parts)))
-    qkv_rows = assemble(sides, False, factor)
+        kinds = [entry[0] for parts in CHUNKS for entry in parts if entry[0] != "qkv"]
+        if "out" not in results and len([key for key in done if key[0] != "qkv"]) == len(kinds):
+            joined = [gathered(kind, far) for kind in ("shared", "attn") for far in (False, True)]
+            results["out"] = assemble(joined, True, factor)
+
+    def gathered(kind, far):
+        parts = [done[key] for key in sorted(key for key in done if key[:2] == (kind, far))]
+        return tuple(jnp.concatenate(pieces, axis=1) for pieces in zip(*parts))
+
+    pipeline(len(CHUNKS), make_part, stage, hooks, extras, LATER, finish)
+    qkv_rows = assemble([gathered("qkv", far) for far in (False, True)], False, factor)
     return (qkv_rows, results["out"])
 
 

time: 186 us -> 174 us (0.935)
  waiting for transfers between devices: 71.4 us -> 57.2 us
  local copies, waits for them, and re-layouts: 10.9 us -> 14.4 us
    ppermute x8, waiting for transfers between devices: 51.6 us -> 7.88 us  [pipeline(): came2[k] = lax.ppermute(sent, 'dp', swap(8, 4))]
    ppermute x8, waiting for transfers between devices: 13.5 us -> 44 us  [begin(): came1[k] = lax.ppermute(sent1[k], 'dp', swap(8, 2))]
    ppermute x8, starting transfers between devices: 6.44 us -> 10.8 us  [pipeline(): came3[j] = lax.ppermute(sent, 'dp', swap(8))]
    ppermute x8, starting transfers between devices: 16.1 us -> 12.5 us  [begin(): came1[k] = lax.ppermute(sent1[k], 'dp', swap(8, 2))]
    unnamed x90 -> x80, local copies, waits for them, and re-layouts: 10.3 us -> 12.9 us
    ppermute x1, waiting for transfers between devices: 2.45 us -> 0.01 us  [body(): lax.ppermute(pick(plan, attn, at_attn_theirs, 1 + len(attn_theirs)), 'dp'...]
  transfers between devices with their start and end apart: 32 -> 32, of which waited for: 15 -> 13; matrix products, arithmetic and copies ran while one was open for 2% -> 3% of each run, Pallas kernels for 30% -> 31%
where the time goes in v3:
time: 174 us; the launch traced here: 173 us
  waiting for transfers between devices  57.2 us (33%)
  Pallas kernels  54.2 us (31%)
  starting transfers between devices  36.7 us (21%)
  local copies, waits for them, and re-layouts  14.4 us (8%)
  other arithmetic  5.14 us (3%)
  blocking collectives  4.06 us (2%)
    ppermute x8, waiting for transfers between devices, begin(): came1[k] = lax.ppermute(sent1[k], 'dp', swap(8, 2))  44 us
    pallas_call x16, Pallas kernels, gridded(): pl.pallas_call(kernel, grid_spec=pltpu.PrefetchScalarGridSpec(num_scalar_...  41.7 us
    unnamed x80, local copies, waits for them, and re-layouts  12.9 us
    ppermute x8, starting transfers between devices, begin(): came1[k] = lax.ppermute(sent1[k], 'dp', swap(8, 2))  12.5 us
    pallas_call x16, Pallas kernels, blocked(): pl.pallas_call(kernel, grid=(width // size,), in_specs=[pl.BlockSpec((row...  11.2 us
    ppermute x8, starting transfers between devices, pipeline(): came3[j] = lax.ppermute(sent, 'dp', swap(8))  10.8 us
    ppermute x8, waiting for transfers between devices, pipeline(): came2[k] = lax.ppermute(sent, 'dp', swap(8, 4))  7.88 us
    ppermute x8, starting transfers between devices, pipeline(): came2[k] = lax.ppermute(sent, 'dp', swap(8, 4))  7.51 us
  transfers between devices with their start and end apart: 32, of which 13 were waited for; matrix products, arithmetic and copies ran while one was open for 3% of the time, Pallas kernels for 31%

profile of v3, /device:TPU:0, one launch (start us, length us, event | category | flops | bytes accessed | tf_op | source)
XLA Modules:
  0.0 173.3 jit_solution(2871874275528916102)
XLA Ops:
  1.3 1.9 %copy-done = bf16[512,3072]{1,0:T(8,128)(2,1)S(1)} copy-done((bf16[512,3072]{1,0:T(8,128)(2,1)S(1)}, bf16[512,3072]{1,0:T(8,128)(2,1)}, u32[]{:S(2)}) %copy-start) | copy-done | bytes 3145752
  3.2 2.8 %shard_map.65 = bf16[512,1280]{1,0:T(8,128)(2,1)} custom-call(s32[35]{0:T(128)S(1)} %stack.115.at, bf16[512,3072]{1,0:T(8,128)(2,1)S(1)} %copy-done), custom_call_target="tpu_custom_call" | custom-call | tf_op jit(solution)/shard_map/pallas_call | solution.py:88
  6.0 2.7 %collective-permute-start.3 = (bf16[512,1280]{1,0:T(8,128)(2,1)}, bf16[512,1280]{1,0:T(8,128)(2,1)}, u32[]{:S(2)}, u32[]{:S(2)}) collective-permute-start(bf16[512,1280]{1,0:T(8,128)(2,1)} %shard_map.65), channel_id=1, source_target_pairs={{0,2},{2,0},{4,6},{6,4},{8,10},{10,8},{12,14},{14,12},{1,3},{3,1},... | collective-permute-start | bytes 3932168 | tf_op jit(solution)/shard_map/ppermute | solution.py:469
  9.8 2.5 %shard_map.60 = (f32[256,1024]{1,0:T(8,128)S(1)}, s16[272,1024]{1,0:T(8,128)(2,1)}) custom-call(s32[35]{0:T(128)S(1)} %stack.115.at, bf16[512,512]{1,0:T(8,128)(2,1)S(1)} %shard_map.59.rows, bf16[512,3072]{1,0:T(8,128)(2,1)S(1)} %copy-done, bf16[512,3072]{1,0:T(8,128)(2,1)S(1)} %copy-done), custom_call_target="tpu_custom_call" | custom-call | tf_op jit(solution)/shard_map/pallas_call | solution.py:88
  14.9 2.5 %shard_map.61 = (f32[256,1024]{1,0:T(8,128)S(1)}, s16[272,1024]{1,0:T(8,128)(2,1)}) custom-call(s32[35]{0:T(128)S(1)} %stack.115.at, bf16[512,512]{1,0:T(8,128)(2,1)S(1)} %shard_map.59.rows, bf16[512,3072]{1,0:T(8,128)(2,1)S(1)} %collective-permute-done.1.refs_0_.refs_1_, bf16[512,3072]{1,0:T(8,128)(2,1)S(1)} %collective-permute-done.1.refs_0_.refs_1_), custom_call_target="tpu_custom_call" | custom-call | tf_op jit(solution)/shard_map/pallas_call | solution.py:88
  20.1 1.9 %copy-done.10 = bf16[512,3072]{1,0:T(8,128)(2,1)S(1)} copy-done((bf16[512,3072]{1,0:T(8,128)(2,1)S(1)}, bf16[512,3072]{1,0:T(8,128)(2,1)}, u32[]{:S(2)}) %copy-start.10) | copy-done | bytes 3145752
  23.3 4.1 %psum.7.moments = f32[8,512]{1,0:T(8,128)} all-reduce(f32[8,512]{1,0:T(8,128)S(1)} %shard_map.62), channel_id=1, replica_groups=mesh['groups'=2,'dp'=8,'tensor'=2] {'tensor'}, use_global_device_ids=true, to_apply=%region_0.1 | all-reduce | flops 4096 | bytes 32768 | tf_op jit(solution)/shard_map/psum | solution.py:473
  27.3 1.9 %copy-done.11 = bf16[512,3072]{1,0:T(8,128)(2,1)S(1)} copy-done((bf16[512,3072]{1,0:T(8,128)(2,1)S(1)}, bf16[512,3072]{1,0:T(8,128)(2,1)}, u32[]{:S(2)}) %copy-start.11) | copy-done | bytes 3145752
  29.9 5.8 %shard_map.63.source.refs_0_.refs_1_ = bf16[512,3072]{1,0:T(8,128)(2,1)S(1)} custom-call(s32[35]{0:T(128)S(1)} %stack.115.at, s32[1,512]{1,0:T(1,128)S(1)} %bitcast.36, f32[8,512]{1,0:T(8,128)S(1)} %copy-done.32, bf16[512,3072]{1,0:T(8,128)(2,1)S(1)} %copy-done.11, f32[16,6144]{1,0:T(8,128)S(1)} %reshape.11.table), custom_call_target="tpu_custom_call" | custom-call | tf_op jit(solution)/shard_map/pallas_call | solution.py:88
  35.7 4.4 %collective-permute-done.2.came.came1 = s16[272,1024]{1,0:T(8,128)(2,1)} collective-permute-done((s16[272,1024]{1,0:T(8,128)(2,1)}, s16[272,1024]{1,0:T(8,128)(2,1)}, u32[]{:S(2)}, u32[]{:S(2)}) %collective-permute-start.2) | collective-permute-done | bytes 557088 | tf_op jit(solution)/shard_map/ppermute | solution.py:337
  43.4 2.8 %collective-permute-start.7 = (s16[144,1024]{1,0:T(8,128)(2,1)S(1)}, s16[144,1024]{1,0:T(8,128)(2,1)S(1)}, u32[]{:S(2)}, u32[]{:S(2)}) collective-permute-start(s16[144,1024]{1,0:T(8,128)(2,1)S(1)} %shard_map.66), channel_id=1, source_target_pairs={{0,8},{2,10},{4,12},{6,14},{8,0},{10,2},{12,4},{14,6},{1,9},{3,11}... | collective-permute-start | bytes 884744 | tf_op jit(solution)/shard_map/ppermute | solution.py:376
  46.2 2.7 %shard_map.67.refs_2_ = bf16[512,512]{1,0:T(8,128)(2,1)S(1)} custom-call(s32[35]{0:T(128)S(1)} %stack.115.at, bf16[512,1280]{1,0:T(8,128)(2,1)} %collective-permute-done.3.source.refs_3_.refs_4_), custom_call_target="tpu_custom_call" | custom-call | tf_op jit(solution)/shard_map/pallas_call | solution.py:88
  48.9 3.4 %shard_map.68 = (f32[256,1024]{1,0:T(8,128)S(1)}, s16[272,1024]{1,0:T(8,128)(2,1)S(1)}) custom-call(s32[35]{0:T(128)S(1)} %stack.115.at, bf16[512,512]{1,0:T(8,128)(2,1)S(1)} %copy-done.9, bf16[512,3072]{1,0:T(8,128)(2,1)S(1)} %copy-done.1, bf16[512,3072]{1,0:T(8,128)(2,1)S(1)} %copy-done.1, bf16[512,512]{1,0:T(8,128)(2,1)S(1)} %shard_map.67.refs_2_, ...), custom_call_target="tpu_custom_call" | custom-call | tf_op jit(solution)/shard_map/pallas_call | solution.py:88
  56.5 3.0 %collective-permute-done.7.came2 = s16[144,1024]{1,0:T(8,128)(2,1)S(1)} collective-permute-done((s16[144,1024]{1,0:T(8,128)(2,1)S(1)}, s16[144,1024]{1,0:T(8,128)(2,1)S(1)}, u32[]{:S(2)}, u32[]{:S(2)}) %collective-permute-start.7) | collective-permute-done | bytes 294944 | tf_op jit(solution)/shard_map/ppermute | solution.py:376
  60.8 2.5 %shard_map.72 = (f32[256,1024]{1,0:T(8,128)S(1)}, s16[272,1024]{1,0:T(8,128)(2,1)S(1)}) custom-call(s32[35]{0:T(128)S(1)} %stack.115.at, bf16[512,512]{1,0:T(8,128)(2,1)S(1)} %copy-done.9, bf16[512,3072]{1,0:T(8,128)(2,1)S(1)} %copy-done.3, bf16[512,3072]{1,0:T(8,128)(2,1)S(1)} %copy-done.3, bf16[512,512]{1,0:T(8,128)(2,1)S(1)} %shard_map.67.refs_2_, ...), custom_call_target="tpu_custom_call" | custom-call | tf_op jit(solution)/shard_map/pallas_call | solution.py:88
  63.4 14.3 %collective-permute-done.5.came.came1 = s16[272,1024]{1,0:T(8,128)(2,1)S(1)} collective-permute-done((s16[272,1024]{1,0:T(8,128)(2,1)S(1)}, s16[272,1024]{1,0:T(8,128)(2,1)S(1)}, u32[]{:S(2)}, u32[]{:S(2)}) %collective-permute-start.5) | collective-permute-done | bytes 557088 | tf_op jit(solution)/shard_map/ppermute | solution.py:337
  81.2 3.0 %collective-permute-start.13 = (s16[144,1024]{1,0:T(8,128)(2,1)S(1)}, s16[144,1024]{1,0:T(8,128)(2,1)}, u32[]{:S(2)}, u32[]{:S(2)}) collective-permute-start(s16[144,1024]{1,0:T(8,128)(2,1)S(1)} %shard_map.73), channel_id=1, source_target_pairs={{0,8},{2,10},{4,12},{6,14},{8,0},{10,2},{12,4},{14,6},{1,9},{3,11}... | collective-permute-start | bytes 884744 | tf_op jit(solution)/shard_map/ppermute | solution.py:376
  84.1 2.0 %collective-permute-done.29 = s16[80,1024]{1,0:T(8,128)(2,1)} collective-permute-done((s16[80,1024]{1,0:T(8,128)(2,1)S(1)}, s16[80,1024]{1,0:T(8,128)(2,1)}, u32[]{:S(2)}, u32[]{:S(2)}) %collective-permute-start.29) | collective-permute-done | bytes 163872 | tf_op jit(solution)/shard_map/ppermute | solution.py:386
  87.7 2.7 %shard_map.75.refs_2_ = bf16[512,512]{1,0:T(8,128)(2,1)S(1)} custom-call(s32[35]{0:T(128)S(1)} %stack.115.at, bf16[512,1280]{1,0:T(8,128)(2,1)} %collective-permute-done.4.source.refs_3_.refs_4_), custom_call_target="tpu_custom_call" | custom-call | tf_op jit(solution)/shard_map/pallas_call | solution.py:88
  90.4 4.0 %shard_map.76 = (f32[256,1024]{1,0:T(8,128)S(1)}, s16[272,1024]{1,0:T(8,128)(2,1)}) custom-call(s32[35]{0:T(128)S(1)} %stack.115.at, bf16[512,512]{1,0:T(8,128)(2,1)S(1)} %shard_map.64.rows, bf16[512,3072]{1,0:T(8,128)(2,1)S(1)} %shard_map.63.source.refs_0_.refs_1_, bf16[512,3072]{1,0:T(8,128)(2,1)S(1)} %shard_map.63.source.refs_0_.refs_1_, ...), custom_call_target="tpu_custom_call" | custom-call | tf_op jit(solution)/shard_map/pallas_call | solution.py:88
  97.8 3.4 %collective-permute-done.12.came.came1 = s16[272,1024]{1,0:T(8,128)(2,1)S(1)} collective-permute-done((s16[272,1024]{1,0:T(8,128)(2,1)S(1)}, s16[272,1024]{1,0:T(8,128)(2,1)S(1)}, u32[]{:S(2)}, u32[]{:S(2)}) %collective-permute-start.12) | collective-permute-done | bytes 557088 | tf_op jit(solution)/shard_map/ppermute | solution.py:337
  110.8 3.5 %shard_map.79 = (f32[256,1024]{1,0:T(8,128)S(1)}, s16[272,1024]{1,0:T(8,128)(2,1)S(1)}) custom-call(s32[35]{0:T(128)S(1)} %stack.115.at, bf16[512,512]{1,0:T(8,128)(2,1)S(1)} %copy-done.5, bf16[512,3072]{1,0:T(8,128)(2,1)} %collective-permute-done.10.refs_0_.refs_1_, bf16[512,3072]{1,0:T(8,128)(2,1)} %collective-permute-done.10.refs_0_.refs_1_, ...), custom_call_target="tpu_custom_call" | custom-call | tf_op jit(solution)/shard_map/pallas_call | solution.py:88
  114.3 2.5 %collective-permute-start.15 = (s16[272,1024]{1,0:T(8,128)(2,1)S(1)}, s16[272,1024]{1,0:T(8,128)(2,1)S(1)}, u32[]{:S(2)}, u32[]{:S(2)}) collective-permute-start(s16[272,1024]{1,0:T(8,128)(2,1)S(1)} %get-tuple-element.94), channel_id=1, source_target_pairs={{0,4},{2,6},{4,0},{6,2},{8,12},{10,14},{12,8},{14,10},{1,5},{3,7},... | collective-permute-start | bytes 1671176 | tf_op jit(solution)/shard_map/ppermute | solution.py:337
  119.4 2.2 %collective-permute-done.17.came2 = s16[144,1024]{1,0:T(8,128)(2,1)S(1)} collective-permute-done((s16[144,1024]{1,0:T(8,128)(2,1)S(1)}, s16[144,1024]{1,0:T(8,128)(2,1)S(1)}, u32[]{:S(2)}, u32[]{:S(2)}) %collective-permute-start.17) | collective-permute-done | bytes 294944 | tf_op jit(solution)/shard_map/ppermute | solution.py:376
  122.6 2.3 %shard_map.83 = (f32[256,512]{1,0:T(8,128)S(1)}, s16[272,512]{1,0:T(8,128)(2,1)S(1)}) custom-call(s32[35]{0:T(128)S(1)} %stack.115.at, bf16[512,512]{1,0:T(8,128)(2,1)S(1)} %copy-done.5, bf16[512,3072]{1,0:T(8,128)(2,1)S(1)} %shard_map.63.source.refs_0_.refs_1_, bf16[512,3072]{1,0:T(8,128)(2,1)S(1)} %shard_map.63.source.refs_0_.refs_1_, ...), custom_call_target="tpu_custom_call" | custom-call | tf_op jit(solution)/shard_map/pallas_call | solution.py:88
  128.0 10.3 %collective-permute-done.15.came.came1 = s16[272,1024]{1,0:T(8,128)(2,1)S(1)} collective-permute-done((s16[272,1024]{1,0:T(8,128)(2,1)S(1)}, s16[272,1024]{1,0:T(8,128)(2,1)S(1)}, u32[]{:S(2)}, u32[]{:S(2)}) %collective-permute-start.15) | collective-permute-done | bytes 557088 | tf_op jit(solution)/shard_map/ppermute | solution.py:337
  141.8 2.3 %shard_map.86 = (f32[256,512]{1,0:T(8,128)S(1)}, s16[272,512]{1,0:T(8,128)(2,1)S(1)}) custom-call(s32[35]{0:T(128)S(1)} %stack.115.at, bf16[512,512]{1,0:T(8,128)(2,1)S(1)} %copy-done.5, bf16[512,3072]{1,0:T(8,128)(2,1)} %collective-permute-done.10.refs_0_.refs_1_, bf16[512,3072]{1,0:T(8,128)(2,1)} %collective-permute-done.10.refs_0_.refs_1_, ...), custom_call_target="tpu_custom_call" | custom-call | tf_op jit(solution)/shard_map/pallas_call | solution.py:88
  144.1 2.6 %collective-permute-start.21 = (s16[272,512]{1,0:T(8,128)(2,1)S(1)}, s16[272,512]{1,0:T(8,128)(2,1)S(1)}, u32[]{:S(2)}, u32[]{:S(2)}) collective-permute-start(s16[272,512]{1,0:T(8,128)(2,1)S(1)} %get-tuple-element.108), channel_id=1, source_target_pairs={{0,4},{2,6},{4,0},{6,2},{8,12},{10,14},{12,8},{14,10},{1,5},{3,7},... | collective-permute-start | bytes 835592 | tf_op jit(solution)/shard_map/ppermute | solution.py:337
  149.6 9.1 %collective-permute-done.21.came.came1 = s16[272,512]{1,0:T(8,128)(2,1)S(1)} collective-permute-done((s16[272,512]{1,0:T(8,128)(2,1)S(1)}, s16[272,512]{1,0:T(8,128)(2,1)S(1)}, u32[]{:S(2)}, u32[]{:S(2)}) %collective-permute-start.21) | collective-permute-done | bytes 278560 | tf_op jit(solution)/shard_map/ppermute | solution.py:337
  159.1 4.4 %collective-permute-start.24 = (s16[80,512]{1,0:T(8,128)(2,1)S(1)}, s16[80,512]{1,0:T(8,128)(2,1)S(1)}, u32[]{:S(2)}, u32[]{:S(2)}) collective-permute-start(s16[80,512]{1,0:T(8,128)(2,1)S(1)} %get-tuple-element.116), channel_id=1, source_target_pairs={{0,2},{2,0},{4,6},{6,4},{8,10},{10,8},{12,14},{14,12},{1,3},{3,1},... | collective-permute-start | bytes 245768 | tf_op jit(solution)/shard_map/ppermute | solution.py:386
  164.1 2.7 %collective-permute-done.25.came2 = s16[144,512]{1,0:T(8,128)(2,1)S(1)} collective-permute-done((s16[144,512]{1,0:T(8,128)(2,1)S(1)}, s16[144,512]{1,0:T(8,128)(2,1)S(1)}, u32[]{:S(2)}, u32[]{:S(2)}) %collective-permute-start.25) | collective-permute-done | bytes 147488 | tf_op jit(solution)/shard_map/ppermute | solution.py:376
  169.4 2.0 %collective-permute-done.27 = s16[80,512]{1,0:T(8,128)(2,1)S(1)} collective-permute-done((s16[80,512]{1,0:T(8,128)(2,1)S(1)}, s16[80,512]{1,0:T(8,128)(2,1)S(1)}, u32[]{:S(2)}, u32[]{:S(2)}) %collective-permute-start.27) | collective-permute-done | bytes 81952 | tf_op jit(solution)/shard_map/ppermute | solution.py:386
  (180 shorter events, 53.6 us)
Async XLA Ops:
  0.6 14.3 %collective-permute-start.1 = (bf16[512,3072]{1,0:T(8,128)(2,1)}, bf16[512,3072]{1,0:T(8,128)(2,1)S(1)}, u32[]{:S(2)}, u32[]{:S(2)}) collective-permute-start(bf16[512,3072]{1,0:T(8,128)(2,1)} %refs_1_.3), channel_id=1, source_target_pairs={{0,1},{1,0},{2,3},{3,2},{4,5},{5,4},{6,7},{7,6},{8,9},{9,8},{10,11... | collective-permute-start | bytes 9437192 | tf_op jit(solution)/shard_map/ppermute | solution.py:467
  6.0 35.4 %collective-permute-start.3 = (bf16[512,1280]{1,0:T(8,128)(2,1)}, bf16[512,1280]{1,0:T(8,128)(2,1)}, u32[]{:S(2)}, u32[]{:S(2)}) collective-permute-start(bf16[512,1280]{1,0:T(8,128)(2,1)} %shard_map.65), channel_id=1, source_target_pairs={{0,2},{2,0},{4,6},{6,4},{8,10},{10,8},{12,14},{14,12},{1,3},{3,1},... | collective-permute-start | bytes 3932168 | tf_op jit(solution)/shard_map/ppermute | solution.py:469
  13.3 22.4 %collective-permute-start = (s16[272,1024]{1,0:T(8,128)(2,1)}, s16[272,1024]{1,0:T(8,128)(2,1)}, u32[]{:S(2)}, u32[]{:S(2)}) collective-permute-start(s16[272,1024]{1,0:T(8,128)(2,1)} %get-tuple-element.66), channel_id=1, source_target_pairs={{0,4},{2,6},{4,0},{6,2},{8,12},{10,14},{12,8},{14,10},{1,5},{3,7},... | collective-permute-start | bytes 1671176 | tf_op jit(solution)/shard_map/ppermute | solution.py:337
  18.4 21.8 %collective-permute-start.2 = (s16[272,1024]{1,0:T(8,128)(2,1)}, s16[272,1024]{1,0:T(8,128)(2,1)}, u32[]{:S(2)}, u32[]{:S(2)}) collective-permute-start(s16[272,1024]{1,0:T(8,128)(2,1)} %get-tuple-element.67), channel_id=1, source_target_pairs={{0,4},{2,6},{4,0},{6,2},{8,12},{10,14},{12,8},{14,10},{1,5},{3,7},... | collective-permute-start | bytes 1671176 | tf_op jit(solution)/shard_map/ppermute | solution.py:337
  40.2 70.6 %collective-permute-start.10 = (bf16[512,3072]{1,0:T(8,128)(2,1)S(1)}, bf16[512,3072]{1,0:T(8,128)(2,1)}, u32[]{:S(2)}, u32[]{:S(2)}) collective-permute-start(bf16[512,3072]{1,0:T(8,128)(2,1)S(1)} %shard_map.63.source.refs_0_.refs_1_), channel_id=1, source_target_pairs={{0,1},{1,0},{2,3},{3,2},{4,5},{5,4},{6,7},{7,6},{8,9},{9,8},{10,11... | collective-permute-start | bytes 9437192 | tf_op jit(solution)/shard_map/ppermute | solution.py:485
  41.4 19.4 %collective-permute-start.6 = (bf16[512,1280]{1,0:T(8,128)(2,1)}, bf16[512,1280]{1,0:T(8,128)(2,1)S(1)}, u32[]{:S(2)}, u32[]{:S(2)}) collective-permute-start(bf16[512,1280]{1,0:T(8,128)(2,1)} %collective-permute-done.3.source.refs_3_.refs_4_), channel_id=1, source_target_pairs={{0,1},{1,0},{2,3},{3,2},{4,5},{5,4},{6,7},{7,6},{8,9},{9,8},{10,11... | collective-permute-start | bytes 3932168 | tf_op jit(solution)/shard_map/ppermute | solution.py:523
  43.0 36.3 %collective-permute-start.4 = (bf16[512,1280]{1,0:T(8,128)(2,1)S(1)}, bf16[512,1280]{1,0:T(8,128)(2,1)}, u32[]{:S(2)}, u32[]{:S(2)}) collective-permute-start(bf16[512,1280]{1,0:T(8,128)(2,1)S(1)} %shard_map.69), channel_id=1, source_target_pairs={{0,2},{2,0},{4,6},{6,4},{8,10},{10,8},{12,14},{14,12},{1,3},{3,1},... | collective-permute-start | bytes 3932168 | tf_op jit(solution)/shard_map/ppermute | solution.py:484
  43.4 16.1 %collective-permute-start.7 = (s16[144,1024]{1,0:T(8,128)(2,1)S(1)}, s16[144,1024]{1,0:T(8,128)(2,1)S(1)}, u32[]{:S(2)}, u32[]{:S(2)}) collective-permute-start(s16[144,1024]{1,0:T(8,128)(2,1)S(1)} %shard_map.66), channel_id=1, source_target_pairs={{0,8},{2,10},{4,12},{6,14},{8,0},{10,2},{12,4},{14,6},{1,9},{3,11}... | collective-permute-start | bytes 884744 | tf_op jit(solution)/shard_map/ppermute | solution.py:376
  52.3 25.4 %collective-permute-start.5 = (s16[272,1024]{1,0:T(8,128)(2,1)S(1)}, s16[272,1024]{1,0:T(8,128)(2,1)S(1)}, u32[]{:S(2)}, u32[]{:S(2)}) collective-permute-start(s16[272,1024]{1,0:T(8,128)(2,1)S(1)} %get-tuple-element.74), channel_id=1, source_target_pairs={{0,4},{2,6},{4,0},{6,2},{8,12},{10,14},{12,8},{14,10},{1,5},{3,7},... | collective-permute-start | bytes 1671176 | tf_op jit(solution)/shard_map/ppermute | solution.py:337
  59.5 18.5 %collective-permute-start.8 = (s16[144,1024]{1,0:T(8,128)(2,1)S(1)}, s16[144,1024]{1,0:T(8,128)(2,1)S(1)}, u32[]{:S(2)}, u32[]{:S(2)}) collective-permute-start(s16[144,1024]{1,0:T(8,128)(2,1)S(1)} %shard_map.70), channel_id=1, source_target_pairs={{0,8},{2,10},{4,12},{6,14},{8,0},{10,2},{12,4},{14,6},{1,9},{3,11}... | collective-permute-start | bytes 884744 | tf_op jit(solution)/shard_map/ppermute | solution.py:376
  79.4 30.8 %collective-permute-start.11 = (bf16[512,1280]{1,0:T(8,128)(2,1)}, bf16[512,1280]{1,0:T(8,128)(2,1)}, u32[]{:S(2)}, u32[]{:S(2)}) collective-permute-start(bf16[512,1280]{1,0:T(8,128)(2,1)} %collective-permute-done.4.source.refs_3_.refs_4_), channel_id=1, source_target_pairs={{0,1},{1,0},{2,3},{3,2},{4,5},{5,4},{6,7},{7,6},{8,9},{9,8},{10,11... | collective-permute-start | bytes 3932168 | tf_op jit(solution)/shard_map/ppermute | solution.py:523
  79.4 21.8 %collective-permute-start.12 = (s16[272,1024]{1,0:T(8,128)(2,1)S(1)}, s16[272,1024]{1,0:T(8,128)(2,1)S(1)}, u32[]{:S(2)}, u32[]{:S(2)}) collective-permute-start(s16[272,1024]{1,0:T(8,128)(2,1)S(1)} %get-tuple-element.82), channel_id=1, source_target_pairs={{0,4},{2,6},{4,0},{6,2},{8,12},{10,14},{12,8},{14,10},{1,5},{3,7},... | collective-permute-start | bytes 1671176 | tf_op jit(solution)/shard_map/ppermute | solution.py:337
  79.5 6.6 %collective-permute-start.29 = (s16[80,1024]{1,0:T(8,128)(2,1)S(1)}, s16[80,1024]{1,0:T(8,128)(2,1)}, u32[]{:S(2)}, u32[]{:S(2)}) collective-permute-start(s16[80,1024]{1,0:T(8,128)(2,1)S(1)} %get-tuple-element.80), channel_id=1, source_target_pairs={{0,2},{2,0},{4,6},{6,4},{8,10},{10,8},{12,14},{14,12},{1,3},{3,1},... | collective-permute-start | bytes 491528 | tf_op jit(solution)/shard_map/ppermute | solution.py:386
  81.2 25.1 %collective-permute-start.13 = (s16[144,1024]{1,0:T(8,128)(2,1)S(1)}, s16[144,1024]{1,0:T(8,128)(2,1)}, u32[]{:S(2)}, u32[]{:S(2)}) collective-permute-start(s16[144,1024]{1,0:T(8,128)(2,1)S(1)} %shard_map.73), channel_id=1, source_target_pairs={{0,8},{2,10},{4,12},{6,14},{8,0},{10,2},{12,4},{14,6},{1,9},{3,11}... | collective-permute-start | bytes 884744 | tf_op jit(solution)/shard_map/ppermute | solution.py:376
  86.2 8.3 %collective-permute-start.31 = (s16[80,1024]{1,0:T(8,128)(2,1)S(1)}, s16[80,1024]{1,0:T(8,128)(2,1)S(1)}, u32[]{:S(2)}, u32[]{:S(2)}) collective-permute-start(s16[80,1024]{1,0:T(8,128)(2,1)S(1)} %get-tuple-element.85), channel_id=1, source_target_pairs={{0,2},{2,0},{4,6},{6,4},{8,10},{10,8},{12,14},{14,12},{1,3},{3,1},... | collective-permute-start | bytes 491528 | tf_op jit(solution)/shard_map/ppermute | solution.py:386
  94.5 23.6 %collective-permute-start.9 = (s16[272,1024]{1,0:T(8,128)(2,1)}, s16[272,1024]{1,0:T(8,128)(2,1)}, u32[]{:S(2)}, u32[]{:S(2)}) collective-permute-start(s16[272,1024]{1,0:T(8,128)(2,1)} %get-tuple-element.88), channel_id=1, source_target_pairs={{0,4},{2,6},{4,0},{6,2},{8,12},{10,14},{12,8},{14,10},{1,5},{3,7},... | collective-permute-start | bytes 1671176 | tf_op jit(solution)/shard_map/ppermute | solution.py:337
  102.1 20.5 %collective-permute-start.16 = (bf16[512,512]{1,0:T(8,128)(2,1)}, bf16[512,512]{1,0:T(8,128)(2,1)}, u32[]{:S(2)}, u32[]{:S(2)}) collective-permute-start(bf16[512,512]{1,0:T(8,128)(2,1)} %shard_map.81), channel_id=1, source_target_pairs={{0,2},{2,0},{4,6},{6,4},{8,10},{10,8},{12,14},{14,12},{1,3},{3,1},... | collective-permute-start | bytes 1572872 | tf_op jit(solution)/shard_map/ppermute | solution.py:484
  106.3 15.3 %collective-permute-start.17 = (s16[144,1024]{1,0:T(8,128)(2,1)S(1)}, s16[144,1024]{1,0:T(8,128)(2,1)S(1)}, u32[]{:S(2)}, u32[]{:S(2)}) collective-permute-start(s16[144,1024]{1,0:T(8,128)(2,1)S(1)} %shard_map.77), channel_id=1, source_target_pairs={{0,8},{2,10},{4,12},{6,14},{8,0},{10,2},{12,4},{14,6},{1,9},{3,11}... | collective-permute-start | bytes 884744 | tf_op jit(solution)/shard_map/ppermute | solution.py:376
  110.2 14.8 %collective-permute-start.28 = (s16[80,1024]{1,0:T(8,128)(2,1)S(1)}, s16[80,1024]{1,0:T(8,128)(2,1)S(1)}, u32[]{:S(2)}, u32[]{:S(2)}) collective-permute-start(s16[80,1024]{1,0:T(8,128)(2,1)S(1)} %get-tuple-element.92), channel_id=1, source_target_pairs={{0,2},{2,0},{4,6},{6,4},{8,10},{10,8},{12,14},{14,12},{1,3},{3,1},... | collective-permute-start | bytes 491528 | tf_op jit(solution)/shard_map/ppermute | solution.py:386
  114.3 23.9 %collective-permute-start.15 = (s16[272,1024]{1,0:T(8,128)(2,1)S(1)}, s16[272,1024]{1,0:T(8,128)(2,1)S(1)}, u32[]{:S(2)}, u32[]{:S(2)}) collective-permute-start(s16[272,1024]{1,0:T(8,128)(2,1)S(1)} %get-tuple-element.94), channel_id=1, source_target_pairs={{0,4},{2,6},{4,0},{6,2},{8,12},{10,14},{12,8},{14,10},{1,5},{3,7},... | collective-permute-start | bytes 1671176 | tf_op jit(solution)/shard_map/ppermute | solution.py:337
  119.3 20.2 %collective-permute-start.14 = (s16[144,1024]{1,0:T(8,128)(2,1)S(1)}, s16[144,1024]{1,0:T(8,128)(2,1)S(1)}, u32[]{:S(2)}, u32[]{:S(2)}) collective-permute-start(s16[144,1024]{1,0:T(8,128)(2,1)S(1)} %shard_map.80), channel_id=1, source_target_pairs={{0,8},{2,10},{4,12},{6,14},{8,0},{10,2},{12,4},{14,6},{1,9},{3,11}... | collective-permute-start | bytes 884744 | tf_op jit(solution)/shard_map/ppermute | solution.py:376
  122.0 19.7 %collective-permute-start.30 = (s16[80,1024]{1,0:T(8,128)(2,1)S(1)}, s16[80,1024]{1,0:T(8,128)(2,1)S(1)}, u32[]{:S(2)}, u32[]{:S(2)}) collective-permute-start(s16[80,1024]{1,0:T(8,128)(2,1)S(1)} %get-tuple-element.99), channel_id=1, source_target_pairs={{0,2},{2,0},{4,6},{6,4},{8,10},{10,8},{12,14},{14,12},{1,3},{3,1},... | collective-permute-start | bytes 491528 | tf_op jit(solution)/shard_map/ppermute | solution.py:386
  124.9 16.9 %collective-permute-start.19 = (bf16[512,512]{1,0:T(8,128)(2,1)}, bf16[512,512]{1,0:T(8,128)(2,1)S(1)}, u32[]{:S(2)}, u32[]{:S(2)}) collective-permute-start(bf16[512,512]{1,0:T(8,128)(2,1)} %collective-permute-done.16.refs_3_.refs_4_), channel_id=1, source_target_pairs={{0,1},{1,0},{2,3},{3,2},{4,5},{5,4},{6,7},{7,6},{8,9},{9,8},{10,11... | collective-permute-start | bytes 1572872 | tf_op jit(solution)/shard_map/ppermute | solution.py:523
  125.1 22.8 %collective-permute-start.18 = (s16[272,512]{1,0:T(8,128)(2,1)S(1)}, s16[272,512]{1,0:T(8,128)(2,1)S(1)}, u32[]{:S(2)}, u32[]{:S(2)}) collective-permute-start(s16[272,512]{1,0:T(8,128)(2,1)S(1)} %get-tuple-element.101), channel_id=1, source_target_pairs={{0,4},{2,6},{4,0},{6,2},{8,12},{10,14},{12,8},{14,10},{1,5},{3,7},... | collective-permute-start | bytes 835592 | tf_op jit(solution)/shard_map/ppermute | solution.py:337
  138.6 24.9 %collective-permute-start.23 = (s16[144,1024]{1,0:T(8,128)(2,1)S(1)}, s16[144,1024]{1,0:T(8,128)(2,1)S(1)}, u32[]{:S(2)}, u32[]{:S(2)}) collective-permute-start(s16[144,1024]{1,0:T(8,128)(2,1)S(1)} %shard_map.84), channel_id=1, source_target_pairs={{0,8},{2,10},{4,12},{6,14},{8,0},{10,2},{12,4},{14,6},{1,9},{3,11}... | collective-permute-start | bytes 884744 | tf_op jit(solution)/shard_map/ppermute | solution.py:376
  140.8 23.2 %collective-permute-start.22 = (s16[80,1024]{1,0:T(8,128)(2,1)S(1)}, s16[80,1024]{1,0:T(8,128)(2,1)S(1)}, u32[]{:S(2)}, u32[]{:S(2)}) collective-permute-start(s16[80,1024]{1,0:T(8,128)(2,1)S(1)} %get-tuple-element.106), channel_id=1, source_target_pairs={{0,2},{2,0},{4,6},{6,4},{8,10},{10,8},{12,14},{14,12},{1,3},{3,1},... | collective-permute-start | bytes 491528 | tf_op jit(solution)/shard_map/ppermute | solution.py:386
  144.1 14.6 %collective-permute-start.21 = (s16[272,512]{1,0:T(8,128)(2,1)S(1)}, s16[272,512]{1,0:T(8,128)(2,1)S(1)}, u32[]{:S(2)}, u32[]{:S(2)}) collective-permute-start(s16[272,512]{1,0:T(8,128)(2,1)S(1)} %get-tuple-element.108), channel_id=1, source_target_pairs={{0,4},{2,6},{4,0},{6,2},{8,12},{10,14},{12,8},{14,10},{1,5},{3,7},... | collective-permute-start | bytes 835592 | tf_op jit(solution)/shard_map/ppermute | solution.py:337
  148.1 10.9 %collective-permute-start.20 = (s16[144,512]{1,0:T(8,128)(2,1)S(1)}, s16[144,512]{1,0:T(8,128)(2,1)S(1)}, u32[]{:S(2)}, u32[]{:S(2)}) collective-permute-start(s16[144,512]{1,0:T(8,128)(2,1)S(1)} %shard_map.87), channel_id=1, source_target_pairs={{0,8},{2,10},{4,12},{6,14},{8,0},{10,2},{12,4},{14,6},{1,9},{3,11}... | collective-permute-start | bytes 442376 | tf_op jit(solution)/shard_map/ppermute | solution.py:376
  158.8 8.0 %collective-permute-start.25 = (s16[144,512]{1,0:T(8,128)(2,1)S(1)}, s16[144,512]{1,0:T(8,128)(2,1)S(1)}, u32[]{:S(2)}, u32[]{:S(2)}) collective-permute-start(s16[144,512]{1,0:T(8,128)(2,1)S(1)} %shard_map.88), channel_id=1, source_target_pairs={{0,8},{2,10},{4,12},{6,14},{8,0},{10,2},{12,4},{14,6},{1,9},{3,11}... | collective-permute-start | bytes 442376 | tf_op jit(solution)/shard_map/ppermute | solution.py:376
  159.1 9.0 %collective-permute-start.24 = (s16[80,512]{1,0:T(8,128)(2,1)S(1)}, s16[80,512]{1,0:T(8,128)(2,1)S(1)}, u32[]{:S(2)}, u32[]{:S(2)}) collective-permute-start(s16[80,512]{1,0:T(8,128)(2,1)S(1)} %get-tuple-element.116), channel_id=1, source_target_pairs={{0,2},{2,0},{4,6},{6,4},{8,10},{10,8},{12,14},{14,12},{1,3},{3,1},... | collective-permute-start | bytes 245768 | tf_op jit(solution)/shard_map/ppermute | solution.py:386
  163.9 5.4 %collective-permute-start.26 = (s16[80,1024]{1,0:T(8,128)(2,1)S(1)}, s16[80,1024]{1,0:T(8,128)(2,1)S(1)}, u32[]{:S(2)}, u32[]{:S(2)}) collective-permute-start(s16[80,1024]{1,0:T(8,128)(2,1)S(1)} %get-tuple-element.114), channel_id=1, source_target_pairs={{0,2},{2,0},{4,6},{6,4},{8,10},{10,8},{12,14},{14,12},{1,3},{3,1},... | collective-permute-start | bytes 491528 | tf_op jit(solution)/shard_map/ppermute | solution.py:386
  166.9 4.5 %collective-permute-start.27 = (s16[80,512]{1,0:T(8,128)(2,1)S(1)}, s16[80,512]{1,0:T(8,128)(2,1)S(1)}, u32[]{:S(2)}, u32[]{:S(2)}) collective-permute-start(s16[80,512]{1,0:T(8,128)(2,1)S(1)} %get-tuple-element.117), channel_id=1, source_target_pairs={{0,2},{2,0},{4,6},{6,4},{8,10},{10,8},{12,14},{14,12},{1,3},{3,1},... | collective-permute-start | bytes 245768 | tf_op jit(solution)/shard_map/ppermute | solution.py:386
  (36 other events, 212.0 us)

commit v4 on v3

--- a/solution.py
+++ b/solution.py
@@ -13,11 +13,12 @@
 
 epsilon = 1e-06
 VMEM = 16 << 20
-TAIL = 16
+TAIL = 8
 LAG = 1
 FIRST = False
 DOUBLES = (0,)
 COMMON = 4
+HOOK_LATE = 2
 PAIR = 2
 ROWS_AT = 1
 PICK_LATE = False
@@ -96,21 +97,35 @@
     )(indices, *operands)
 
 
-def pick_kernel(at, source, out):
-    out[...] = source[...]
-
-
-def pick(plan, source, first, count):
-    tokens = source.shape[0]
-    return gridded(
-        pick_kernel,
-        plan,
-        count,
-        [pl.BlockSpec((tokens, LANES), lambda i, at: (0, at[first + i]))],
-        pl.BlockSpec((tokens, LANES), lambda i, at: (0, i)),
-        jax.ShapeDtypeStruct((tokens, LANES * count), source.dtype),
-        source,
-    )
+def pick_kernel(first, runs, at, source, out, sems):
+    copies = []
+    start = 0
+    for index, length in enumerate(runs):
+        columns = pl.ds(pl.multiple_of(at[first + start] * LANES, LANES), length * LANES)
+        copy = pltpu.make_async_copy(
+            source.at[:, columns], out.at[:, start * LANES : (start + length) * LANES], sems.at[index]
+        )
+        copy.start()
+        copies.append(copy)
+        start += length
+    for copy in copies:
+        copy.wait()
+
+
+def pick(plan, source, first, runs):
+    return pl.pallas_call(
+        functools.partial(pick_kernel, first, runs),
+        grid_spec=pltpu.PrefetchScalarGridSpec(
+            num_scalar_prefetch=1,
+            grid=(1,),
+            in_specs=[pl.BlockSpec(memory_space=pl.ANY)],
+            out_specs=pl.BlockSpec(memory_space=pl.ANY),
+            scratch_shapes=[pltpu.SemaphoreType.DMA((len(runs),))],
+        ),
+        out_shape=jax.ShapeDtypeStruct((source.shape[0], LANES * sum(runs)), source.dtype),
+        cost_estimate=FREE,
+        compiler_params=pltpu.CompilerParams(vmem_limit_bytes=VMEM),
+    )(plan, source)
 
 
 def turn_kernel(at, source, out):
@@ -358,7 +373,7 @@
         if k in DOUBLES:
             wanted["next1"] = came1[k + 1]
         wanted = lax.optimization_barrier(wanted)
-        if k in hooks:
+        if k in hooks and not HOOK_LATE:
             hooks[k][1](wanted["more"])
         if k in extras:
             extras[k][1](wanted["extra"])
@@ -390,6 +405,9 @@
         if not EARLY and k + 2 < count and k + 2 in later:
             raw, _ = lax.optimization_barrier((stage(k + 2), tuple(ahead)))
             begin(k + 2, raw)
+        if k in hooks and HOOK_LATE:
+            more, _ = lax.optimization_barrier((wanted["more"], sent1[k + 2] if HOOK_LATE == 1 else tuple(ahead)))
+            hooks[k][1](more)
 
 
 def unpacked(message):
@@ -466,7 +484,7 @@
     attn = attn_out
     attn_far = lax.ppermute(attn, "tensor", core_swap)
     if not PICK_LATE:
-        store["attn_pair"] = lax.ppermute(pick(plan, attn, at_attn_theirs, 1 + len(attn_theirs)), "dp", swap(dp))
+        store["attn_pair"] = lax.ppermute(pick(plan, attn, at_attn_theirs, (1, 1, len(attn_theirs) - 1)), "dp", swap(dp))
 
     def qkv_input():
         values, _ = lax.optimization_barrier((hidden, sent1_gate[0]))
@@ -480,7 +498,7 @@
         for index in range(len(PIECES)):
             if index:
                 mod, _ = lax.optimization_barrier((mod, message))
-            message = pick(plan, mod, at_qkv_theirs + sum(PIECES[:index]), PIECES[index])
+            message = pick(plan, mod, at_qkv_theirs + sum(PIECES[:index]), (PIECES[index],) if index else (1, 1, PIECES[0] - 2))
             store["pieces"][index] = lax.ppermute(message, "dp", swap(dp))
         store["mod_far"] = lax.ppermute(store["mod"], "tensor", core_swap)
         store["rows"] = turn(plan, store["mod"], at_order)
@@ -554,7 +572,7 @@
         result = gram(plan, rows, columns, other_rows, others)
         if k == 0 and PICK_LATE:
             late, _ = lax.optimization_barrier((attn, result[1]))
-            store["attn_pair"] = lax.ppermute(pick(plan, late, at_attn_theirs, 1 + len(attn_theirs)), "dp", swap(dp))
+            store["attn_pair"] = lax.ppermute(pick(plan, late, at_attn_theirs, (1, 1, len(attn_theirs) - 1)), "dp", swap(dp))
         if k == GATE:
             sent1_gate.append(result[1])
         return result

time: 174 us -> 167 us (0.960)
  waiting for transfers between devices: 57.2 us -> 50.3 us
    ppermute x8, waiting for transfers between devices: 44 us -> 38.5 us  [begin(): came1[k] = lax.ppermute(sent1[k], 'dp', swap(8, 2))]
    pallas_call x16 -> x13, Pallas kernels: 41.7 us -> 36.4 us  [gridded(): pl.pallas_call(kernel, grid_spec=pltpu.PrefetchScalarGridSpec(num_scalar_...]
    pallas_call x0 -> x3, Pallas kernels: none -> 3.73 us  [pick(): pl.pallas_call(functools.partial(pick_kernel, first, runs), grid_spec=plt...]
    ppermute x8, starting transfers between devices: 7.51 us -> 10.2 us  [pipeline(): came2[k] = lax.ppermute(sent, 'dp', swap(8, 4))]
  transfers between devices with their start and end apart: 32 -> 32, of which waited for: 13 -> 11; matrix products, arithmetic and copies ran while one was open for 3% -> 3% of each run, Pallas kernels for 31% -> 32%
where the time goes in v4:
time: 167 us; the launch traced here: 166 us
  Pallas kernels  52.5 us (31%)
  waiting for transfers between devices  50.3 us (30%)
  starting transfers between devices  38.3 us (23%)
  local copies, waits for them, and re-layouts  14.4 us (9%)
  other arithmetic  5.12 us (3%)
  blocking collectives  4.06 us (2%)
    ppermute x8, waiting for transfers between devices, begin(): came1[k] = lax.ppermute(sent1[k], 'dp', swap(8, 2))  38.5 us
    pallas_call x13, Pallas kernels, gridded(): pl.pallas_call(kernel, grid_spec=pltpu.PrefetchScalarGridSpec(num_scalar_...  36.4 us
    ppermute x8, starting transfers between devices, begin(): came1[k] = lax.ppermute(sent1[k], 'dp', swap(8, 2))  13 us
    unnamed x80, local copies, waits for them, and re-layouts  12.9 us
    pallas_call x16, Pallas kernels, blocked(): pl.pallas_call(kernel, grid=(width // size,), in_specs=[pl.BlockSpec((row...  11.2 us
    ppermute x8, starting transfers between devices, pipeline(): came2[k] = lax.ppermute(sent, 'dp', swap(8, 4))  10.2 us
    ppermute x8, starting transfers between devices, pipeline(): came3[j] = lax.ppermute(sent, 'dp', swap(8))  9.1 us
    ppermute x8, waiting for transfers between devices, pipeline(): came2[k] = lax.ppermute(sent, 'dp', swap(8, 4))  7.78 us
  transfers between devices with their start and end apart: 32, of which 11 were waited for; matrix products, arithmetic and copies ran while one was open for 3% of the time, Pallas kernels for 32%

profile of v4, /device:TPU:0, one launch (start us, length us, event | category | flops | bytes accessed | tf_op | source)
XLA Modules:
  0.0 166.2 jit_solution(14286855157147207512)
XLA Ops:
  1.3 1.9 %copy-done = bf16[512,3072]{1,0:T(8,128)(2,1)S(1)} copy-done((bf16[512,3072]{1,0:T(8,128)(2,1)S(1)}, bf16[512,3072]{1,0:T(8,128)(2,1)}, u32[]{:S(2)}) %copy-start) | copy-done | bytes 3145752
  4.8 2.8 %collective-permute-start.3 = (bf16[512,1280]{1,0:T(8,128)(2,1)}, bf16[512,1280]{1,0:T(8,128)(2,1)}, u32[]{:S(2)}, u32[]{:S(2)}) collective-permute-start(bf16[512,1280]{1,0:T(8,128)(2,1)} %shard_map.66), channel_id=1, source_target_pairs={{0,2},{2,0},{4,6},{6,4},{8,10},{10,8},{12,14},{14,12},{1,3},{3,1},... | collective-permute-start | bytes 3932168 | tf_op jit(solution)/shard_map/ppermute | solution.py:487
  8.7 2.5 %shard_map.60 = (f32[256,1024]{1,0:T(8,128)S(1)}, s16[264,1024]{1,0:T(8,128)(2,1)}) custom-call(s32[35]{0:T(128)S(1)} %stack.115.at, bf16[512,512]{1,0:T(8,128)(2,1)S(1)} %shard_map.59.rows, bf16[512,3072]{1,0:T(8,128)(2,1)S(1)} %copy-done, bf16[512,3072]{1,0:T(8,128)(2,1)S(1)} %copy-done), custom_call_target="tpu_custom_call" | custom-call | tf_op jit(solution)/shard_map/pallas_call | solution.py:89
  13.8 2.5 %shard_map.61 = (f32[256,1024]{1,0:T(8,128)S(1)}, s16[264,1024]{1,0:T(8,128)(2,1)}) custom-call(s32[35]{0:T(128)S(1)} %stack.115.at, bf16[512,512]{1,0:T(8,128)(2,1)S(1)} %shard_map.59.rows, bf16[512,3072]{1,0:T(8,128)(2,1)S(1)} %collective-permute-done.1.refs_0_.refs_1_, bf16[512,3072]{1,0:T(8,128)(2,1)S(1)} %collective-permute-done.1.refs_0_.refs_1_), custom_call_target="tpu_custom_call" | custom-call | tf_op jit(solution)/shard_map/pallas_call | solution.py:89
  19.0 1.9 %copy-done.10 = bf16[512,3072]{1,0:T(8,128)(2,1)S(1)} copy-done((bf16[512,3072]{1,0:T(8,128)(2,1)S(1)}, bf16[512,3072]{1,0:T(8,128)(2,1)}, u32[]{:S(2)}) %copy-start.10) | copy-done | bytes 3145752
  22.1 4.1 %psum.7.moments = f32[8,512]{1,0:T(8,128)} all-reduce(f32[8,512]{1,0:T(8,128)S(1)} %shard_map.62), channel_id=1, replica_groups=mesh['groups'=2,'dp'=8,'tensor'=2] {'tensor'}, use_global_device_ids=true, to_apply=%region_0.1 | all-reduce | flops 4096 | bytes 32768 | tf_op jit(solution)/shard_map/psum | solution.py:491
  26.2 1.9 %copy-done.11 = bf16[512,3072]{1,0:T(8,128)(2,1)S(1)} copy-done((bf16[512,3072]{1,0:T(8,128)(2,1)S(1)}, bf16[512,3072]{1,0:T(8,128)(2,1)}, u32[]{:S(2)}) %copy-start.11) | copy-done | bytes 3145752
  28.8 5.8 %shard_map.63.source.refs_0_.refs_1_ = bf16[512,3072]{1,0:T(8,128)(2,1)S(1)} custom-call(s32[35]{0:T(128)S(1)} %stack.115.at, s32[1,512]{1,0:T(1,128)S(1)} %bitcast.36, f32[8,512]{1,0:T(8,128)S(1)} %copy-done.32, bf16[512,3072]{1,0:T(8,128)(2,1)S(1)} %copy-done.11, f32[16,6144]{1,0:T(8,128)S(1)} %reshape.11.table), custom_call_target="tpu_custom_call" | custom-call | tf_op jit(solution)/shard_map/pallas_call | solution.py:89
  34.6 3.7 %collective-permute-done.2.came.came1 = s16[264,1024]{1,0:T(8,128)(2,1)} collective-permute-done((s16[264,1024]{1,0:T(8,128)(2,1)}, s16[264,1024]{1,0:T(8,128)(2,1)}, u32[]{:S(2)}, u32[]{:S(2)}) %collective-permute-start.2) | collective-permute-done | bytes 540704 | tf_op jit(solution)/shard_map/ppermute | solution.py:352
  41.3 2.8 %collective-permute-start.7 = (s16[136,1024]{1,0:T(8,128)(2,1)S(1)}, s16[136,1024]{1,0:T(8,128)(2,1)S(1)}, u32[]{:S(2)}, u32[]{:S(2)}) collective-permute-start(s16[136,1024]{1,0:T(8,128)(2,1)S(1)} %shard_map.64), channel_id=1, source_target_pairs={{0,8},{2,10},{4,12},{6,14},{8,0},{10,2},{12,4},{14,6},{1,9},{3,11}... | collective-permute-start | bytes 835592 | tf_op jit(solution)/shard_map/ppermute | solution.py:391
  44.0 2.7 %shard_map.67.refs_2_ = bf16[512,512]{1,0:T(8,128)(2,1)S(1)} custom-call(s32[35]{0:T(128)S(1)} %stack.115.at, bf16[512,1280]{1,0:T(8,128)(2,1)} %collective-permute-done.3.source.refs_3_.refs_4_), custom_call_target="tpu_custom_call" | custom-call | tf_op jit(solution)/shard_map/pallas_call | solution.py:89
  46.7 3.4 %shard_map.68 = (f32[256,1024]{1,0:T(8,128)S(1)}, s16[264,1024]{1,0:T(8,128)(2,1)S(1)}) custom-call(s32[35]{0:T(128)S(1)} %stack.115.at, bf16[512,512]{1,0:T(8,128)(2,1)S(1)} %copy-done.9, bf16[512,3072]{1,0:T(8,128)(2,1)S(1)} %copy-done.1, bf16[512,3072]{1,0:T(8,128)(2,1)S(1)} %copy-done.1, bf16[512,512]{1,0:T(8,128)(2,1)S(1)} %shard_map.67.refs_2_, ...), custom_call_target="tpu_custom_call" | custom-call | tf_op jit(solution)/shard_map/pallas_call | solution.py:89
  50.1 1.6 collective-permute-start.5
  54.4 2.4 %collective-permute-done.7.came2 = s16[136,1024]{1,0:T(8,128)(2,1)S(1)} collective-permute-done((s16[136,1024]{1,0:T(8,128)(2,1)S(1)}, s16[136,1024]{1,0:T(8,128)(2,1)S(1)}, u32[]{:S(2)}, u32[]{:S(2)}) %collective-permute-start.7) | collective-permute-done | bytes 278560 | tf_op jit(solution)/shard_map/ppermute | solution.py:391
  58.1 2.5 %shard_map.72 = (f32[256,1024]{1,0:T(8,128)S(1)}, s16[264,1024]{1,0:T(8,128)(2,1)S(1)}) custom-call(s32[35]{0:T(128)S(1)} %stack.115.at, bf16[512,512]{1,0:T(8,128)(2,1)S(1)} %copy-done.9, bf16[512,3072]{1,0:T(8,128)(2,1)S(1)} %copy-done.3, bf16[512,3072]{1,0:T(8,128)(2,1)S(1)} %copy-done.3, bf16[512,512]{1,0:T(8,128)(2,1)S(1)} %shard_map.67.refs_2_, ...), custom_call_target="tpu_custom_call" | custom-call | tf_op jit(solution)/shard_map/pallas_call | solution.py:89
  60.6 13.6 %collective-permute-done.5.came.came1 = s16[264,1024]{1,0:T(8,128)(2,1)S(1)} collective-permute-done((s16[264,1024]{1,0:T(8,128)(2,1)S(1)}, s16[264,1024]{1,0:T(8,128)(2,1)S(1)}, u32[]{:S(2)}, u32[]{:S(2)}) %collective-permute-start.5) | collective-permute-done | bytes 540704 | tf_op jit(solution)/shard_map/ppermute | solution.py:352
  76.0 1.6 collective-permute-start.29
  77.7 3.3 %collective-permute-start.13 = (s16[136,1024]{1,0:T(8,128)(2,1)S(1)}, s16[136,1024]{1,0:T(8,128)(2,1)}, u32[]{:S(2)}, u32[]{:S(2)}) collective-permute-start(s16[136,1024]{1,0:T(8,128)(2,1)S(1)} %shard_map.73), channel_id=1, source_target_pairs={{0,8},{2,10},{4,12},{6,14},{8,0},{10,2},{12,4},{14,6},{1,9},{3,11}... | collective-permute-start | bytes 835592 | tf_op jit(solution)/shard_map/ppermute | solution.py:391
  83.9 2.7 %shard_map.75.refs_2_ = bf16[512,512]{1,0:T(8,128)(2,1)S(1)} custom-call(s32[35]{0:T(128)S(1)} %stack.115.at, bf16[512,1280]{1,0:T(8,128)(2,1)} %collective-permute-done.4.source.refs_3_.refs_4_), custom_call_target="tpu_custom_call" | custom-call | tf_op jit(solution)/shard_map/pallas_call | solution.py:89
  86.6 4.0 %shard_map.76 = (f32[256,1024]{1,0:T(8,128)S(1)}, s16[264,1024]{1,0:T(8,128)(2,1)}) custom-call(s32[35]{0:T(128)S(1)} %stack.115.at, bf16[512,512]{1,0:T(8,128)(2,1)S(1)} %shard_map.65.rows, bf16[512,3072]{1,0:T(8,128)(2,1)S(1)} %shard_map.63.source.refs_0_.refs_1_, bf16[512,3072]{1,0:T(8,128)(2,1)S(1)} %shard_map.63.source.refs_0_.refs_1_, ...), custom_call_target="tpu_custom_call" | custom-call | tf_op jit(solution)/shard_map/pallas_call | solution.py:89
  90.7 1.8 %collective-permute-start.9 = (s16[264,1024]{1,0:T(8,128)(2,1)}, s16[264,1024]{1,0:T(8,128)(2,1)}, u32[]{:S(2)}, u32[]{:S(2)}) collective-permute-start(s16[264,1024]{1,0:T(8,128)(2,1)} %get-tuple-element.90), channel_id=1, source_target_pairs={{0,4},{2,6},{4,0},{6,2},{8,12},{10,14},{12,8},{14,10},{1,5},{3,7},... | collective-permute-start | bytes 1622024 | tf_op jit(solution)/shard_map/ppermute | solution.py:352
  93.9 3.2 %collective-permute-done.12.came.came1 = s16[264,1024]{1,0:T(8,128)(2,1)S(1)} collective-permute-done((s16[264,1024]{1,0:T(8,128)(2,1)S(1)}, s16[264,1024]{1,0:T(8,128)(2,1)S(1)}, u32[]{:S(2)}, u32[]{:S(2)}) %collective-permute-start.12) | collective-permute-done | bytes 540704 | tf_op jit(solution)/shard_map/ppermute | solution.py:352
  107.0 3.5 %shard_map.79 = (f32[256,1024]{1,0:T(8,128)S(1)}, s16[264,1024]{1,0:T(8,128)(2,1)S(1)}) custom-call(s32[35]{0:T(128)S(1)} %stack.115.at, bf16[512,512]{1,0:T(8,128)(2,1)S(1)} %copy-done.5, bf16[512,3072]{1,0:T(8,128)(2,1)} %collective-permute-done.10.refs_0_.refs_1_, bf16[512,3072]{1,0:T(8,128)(2,1)} %collective-permute-done.10.refs_0_.refs_1_, ...), custom_call_target="tpu_custom_call" | custom-call | tf_op jit(solution)/shard_map/pallas_call | solution.py:89
  110.5 2.5 %collective-permute-start.15 = (s16[264,1024]{1,0:T(8,128)(2,1)S(1)}, s16[264,1024]{1,0:T(8,128)(2,1)S(1)}, u32[]{:S(2)}, u32[]{:S(2)}) collective-permute-start(s16[264,1024]{1,0:T(8,128)(2,1)S(1)} %get-tuple-element.96), channel_id=1, source_target_pairs={{0,4},{2,6},{4,0},{6,2},{8,12},{10,14},{12,8},{14,10},{1,5},{3,7},... | collective-permute-start | bytes 1622024 | tf_op jit(solution)/shard_map/ppermute | solution.py:352
  114.9 1.8 %collective-permute-done.17.came2 = s16[136,1024]{1,0:T(8,128)(2,1)S(1)} collective-permute-done((s16[136,1024]{1,0:T(8,128)(2,1)S(1)}, s16[136,1024]{1,0:T(8,128)(2,1)S(1)}, u32[]{:S(2)}, u32[]{:S(2)}) %collective-permute-start.17) | collective-permute-done | bytes 278560 | tf_op jit(solution)/shard_map/ppermute | solution.py:391
  118.0 2.3 %shard_map.83 = (f32[256,512]{1,0:T(8,128)S(1)}, s16[264,512]{1,0:T(8,128)(2,1)S(1)}) custom-call(s32[35]{0:T(128)S(1)} %stack.115.at, bf16[512,512]{1,0:T(8,128)(2,1)S(1)} %copy-done.5, bf16[512,3072]{1,0:T(8,128)(2,1)S(1)} %shard_map.63.source.refs_0_.refs_1_, bf16[512,3072]{1,0:T(8,128)(2,1)S(1)} %shard_map.63.source.refs_0_.refs_1_, ...), custom_call_target="tpu_custom_call" | custom-call | tf_op jit(solution)/shard_map/pallas_call | solution.py:89
  123.1 10.3 %collective-permute-done.15.came.came1 = s16[264,1024]{1,0:T(8,128)(2,1)S(1)} collective-permute-done((s16[264,1024]{1,0:T(8,128)(2,1)S(1)}, s16[264,1024]{1,0:T(8,128)(2,1)S(1)}, u32[]{:S(2)}, u32[]{:S(2)}) %collective-permute-start.15) | collective-permute-done | bytes 540704 | tf_op jit(solution)/shard_map/ppermute | solution.py:352
  137.2 2.3 %shard_map.86 = (f32[256,512]{1,0:T(8,128)S(1)}, s16[264,512]{1,0:T(8,128)(2,1)S(1)}) custom-call(s32[35]{0:T(128)S(1)} %stack.115.at, bf16[512,512]{1,0:T(8,128)(2,1)S(1)} %copy-done.5, bf16[512,3072]{1,0:T(8,128)(2,1)} %collective-permute-done.10.refs_0_.refs_1_, bf16[512,3072]{1,0:T(8,128)(2,1)} %collective-permute-done.10.refs_0_.refs_1_, ...), custom_call_target="tpu_custom_call" | custom-call | tf_op jit(solution)/shard_map/pallas_call | solution.py:89
  139.6 3.4 %collective-permute-start.21 = (s16[264,512]{1,0:T(8,128)(2,1)S(1)}, s16[264,512]{1,0:T(8,128)(2,1)S(1)}, u32[]{:S(2)}, u32[]{:S(2)}) collective-permute-start(s16[264,512]{1,0:T(8,128)(2,1)S(1)} %get-tuple-element.110), channel_id=1, source_target_pairs={{0,4},{2,6},{4,0},{6,2},{8,12},{10,14},{12,8},{14,10},{1,5},{3,7},... | collective-permute-start | bytes 811016 | tf_op jit(solution)/shard_map/ppermute | solution.py:352
  145.1 7.1 %collective-permute-done.21.came.came1 = s16[264,512]{1,0:T(8,128)(2,1)S(1)} collective-permute-done((s16[264,512]{1,0:T(8,128)(2,1)S(1)}, s16[264,512]{1,0:T(8,128)(2,1)S(1)}, u32[]{:S(2)}, u32[]{:S(2)}) %collective-permute-start.21) | collective-permute-done | bytes 270368 | tf_op jit(solution)/shard_map/ppermute | solution.py:352
  156.3 3.6 %collective-permute-done.25.came2 = s16[136,512]{1,0:T(8,128)(2,1)S(1)} collective-permute-done((s16[136,512]{1,0:T(8,128)(2,1)S(1)}, s16[136,512]{1,0:T(8,128)(2,1)S(1)}, u32[]{:S(2)}, u32[]{:S(2)}) %collective-permute-start.25) | collective-permute-done | bytes 139296 | tf_op jit(solution)/shard_map/ppermute | solution.py:391
  161.7 2.7 %collective-permute-done.27 = s16[72,512]{1,0:T(8,128)(2,1)S(1)} collective-permute-done((s16[72,512]{1,0:T(8,128)(2,1)S(1)}, s16[72,512]{1,0:T(8,128)(2,1)S(1)}, u32[]{:S(2)}, u32[]{:S(2)}) %collective-permute-start.27) | collective-permute-done | bytes 73760 | tf_op jit(solution)/shard_map/ppermute | solution.py:401
  (180 shorter events, 52.5 us)
Async XLA Ops:
  0.6 13.1 %collective-permute-start.1 = (bf16[512,3072]{1,0:T(8,128)(2,1)}, bf16[512,3072]{1,0:T(8,128)(2,1)S(1)}, u32[]{:S(2)}, u32[]{:S(2)}) collective-permute-start(bf16[512,3072]{1,0:T(8,128)(2,1)} %refs_1_.3), channel_id=1, source_target_pairs={{0,1},{1,0},{2,3},{3,2},{4,5},{5,4},{6,7},{7,6},{8,9},{9,8},{10,11... | collective-permute-start | bytes 9437192 | tf_op jit(solution)/shard_map/ppermute | solution.py:485
  4.8 34.8 %collective-permute-start.3 = (bf16[512,1280]{1,0:T(8,128)(2,1)}, bf16[512,1280]{1,0:T(8,128)(2,1)}, u32[]{:S(2)}, u32[]{:S(2)}) collective-permute-start(bf16[512,1280]{1,0:T(8,128)(2,1)} %shard_map.66), channel_id=1, source_target_pairs={{0,2},{2,0},{4,6},{6,4},{8,10},{10,8},{12,14},{14,12},{1,3},{3,1},... | collective-permute-start | bytes 3932168 | tf_op jit(solution)/shard_map/ppermute | solution.py:487
  12.2 22.4 %collective-permute-start = (s16[264,1024]{1,0:T(8,128)(2,1)}, s16[264,1024]{1,0:T(8,128)(2,1)}, u32[]{:S(2)}, u32[]{:S(2)}) collective-permute-start(s16[264,1024]{1,0:T(8,128)(2,1)} %get-tuple-element.67), channel_id=1, source_target_pairs={{0,4},{2,6},{4,0},{6,2},{8,12},{10,14},{12,8},{14,10},{1,5},{3,7},... | collective-permute-start | bytes 1622024 | tf_op jit(solution)/shard_map/ppermute | solution.py:352
  17.2 21.1 %collective-permute-start.2 = (s16[264,1024]{1,0:T(8,128)(2,1)}, s16[264,1024]{1,0:T(8,128)(2,1)}, u32[]{:S(2)}, u32[]{:S(2)}) collective-permute-start(s16[264,1024]{1,0:T(8,128)(2,1)} %get-tuple-element.68), channel_id=1, source_target_pairs={{0,4},{2,6},{4,0},{6,2},{8,12},{10,14},{12,8},{14,10},{1,5},{3,7},... | collective-permute-start | bytes 1622024 | tf_op jit(solution)/shard_map/ppermute | solution.py:352
  39.5 67.4 %collective-permute-start.10 = (bf16[512,3072]{1,0:T(8,128)(2,1)S(1)}, bf16[512,3072]{1,0:T(8,128)(2,1)}, u32[]{:S(2)}, u32[]{:S(2)}) collective-permute-start(bf16[512,3072]{1,0:T(8,128)(2,1)S(1)} %shard_map.63.source.refs_0_.refs_1_), channel_id=1, source_target_pairs={{0,1},{1,0},{2,3},{3,2},{4,5},{5,4},{6,7},{7,6},{8,9},{9,8},{10,11... | collective-permute-start | bytes 9437192 | tf_op jit(solution)/shard_map/ppermute | solution.py:503
  39.6 18.4 %collective-permute-start.6 = (bf16[512,1280]{1,0:T(8,128)(2,1)}, bf16[512,1280]{1,0:T(8,128)(2,1)S(1)}, u32[]{:S(2)}, u32[]{:S(2)}) collective-permute-start(bf16[512,1280]{1,0:T(8,128)(2,1)} %collective-permute-done.3.source.refs_3_.refs_4_), channel_id=1, source_target_pairs={{0,1},{1,0},{2,3},{3,2},{4,5},{5,4},{6,7},{7,6},{8,9},{9,8},{10,11... | collective-permute-start | bytes 3932168 | tf_op jit(solution)/shard_map/ppermute | solution.py:541
  40.9 35.0 %collective-permute-start.4 = (bf16[512,1280]{1,0:T(8,128)(2,1)S(1)}, bf16[512,1280]{1,0:T(8,128)(2,1)}, u32[]{:S(2)}, u32[]{:S(2)}) collective-permute-start(bf16[512,1280]{1,0:T(8,128)(2,1)S(1)} %shard_map.69), channel_id=1, source_target_pairs={{0,2},{2,0},{4,6},{6,4},{8,10},{10,8},{12,14},{14,12},{1,3},{3,1},... | collective-permute-start | bytes 3932168 | tf_op jit(solution)/shard_map/ppermute | solution.py:502
  41.3 15.5 %collective-permute-start.7 = (s16[136,1024]{1,0:T(8,128)(2,1)S(1)}, s16[136,1024]{1,0:T(8,128)(2,1)S(1)}, u32[]{:S(2)}, u32[]{:S(2)}) collective-permute-start(s16[136,1024]{1,0:T(8,128)(2,1)S(1)} %shard_map.64), channel_id=1, source_target_pairs={{0,8},{2,10},{4,12},{6,14},{8,0},{10,2},{12,4},{14,6},{1,9},{3,11}... | collective-permute-start | bytes 835592 | tf_op jit(solution)/shard_map/ppermute | solution.py:391
  50.1 24.1 %collective-permute-start.5 = (s16[264,1024]{1,0:T(8,128)(2,1)S(1)}, s16[264,1024]{1,0:T(8,128)(2,1)S(1)}, u32[]{:S(2)}, u32[]{:S(2)}) collective-permute-start(s16[264,1024]{1,0:T(8,128)(2,1)S(1)} %get-tuple-element.76), channel_id=1, source_target_pairs={{0,4},{2,6},{4,0},{6,2},{8,12},{10,14},{12,8},{14,10},{1,5},{3,7},... | collective-permute-start | bytes 1622024 | tf_op jit(solution)/shard_map/ppermute | solution.py:352
  56.7 17.8 %collective-permute-start.8 = (s16[136,1024]{1,0:T(8,128)(2,1)S(1)}, s16[136,1024]{1,0:T(8,128)(2,1)S(1)}, u32[]{:S(2)}, u32[]{:S(2)}) collective-permute-start(s16[136,1024]{1,0:T(8,128)(2,1)S(1)} %shard_map.70), channel_id=1, source_target_pairs={{0,8},{2,10},{4,12},{6,14},{8,0},{10,2},{12,4},{14,6},{1,9},{3,11}... | collective-permute-start | bytes 835592 | tf_op jit(solution)/shard_map/ppermute | solution.py:391
  75.9 30.4 %collective-permute-start.11 = (bf16[512,1280]{1,0:T(8,128)(2,1)}, bf16[512,1280]{1,0:T(8,128)(2,1)}, u32[]{:S(2)}, u32[]{:S(2)}) collective-permute-start(bf16[512,1280]{1,0:T(8,128)(2,1)} %collective-permute-done.4.source.refs_3_.refs_4_), channel_id=1, source_target_pairs={{0,1},{1,0},{2,3},{3,2},{4,5},{5,4},{6,7},{7,6},{8,9},{9,8},{10,11... | collective-permute-start | bytes 3932168 | tf_op jit(solution)/shard_map/ppermute | solution.py:541
  76.0 21.1 %collective-permute-start.12 = (s16[264,1024]{1,0:T(8,128)(2,1)S(1)}, s16[264,1024]{1,0:T(8,128)(2,1)S(1)}, u32[]{:S(2)}, u32[]{:S(2)}) collective-permute-start(s16[264,1024]{1,0:T(8,128)(2,1)S(1)} %get-tuple-element.84), channel_id=1, source_target_pairs={{0,4},{2,6},{4,0},{6,2},{8,12},{10,14},{12,8},{14,10},{1,5},{3,7},... | collective-permute-start | bytes 1622024 | tf_op jit(solution)/shard_map/ppermute | solution.py:352
  76.0 6.3 %collective-permute-start.29 = (s16[72,1024]{1,0:T(8,128)(2,1)S(1)}, s16[72,1024]{1,0:T(8,128)(2,1)}, u32[]{:S(2)}, u32[]{:S(2)}) collective-permute-start(s16[72,1024]{1,0:T(8,128)(2,1)S(1)} %get-tuple-element.82), channel_id=1, source_target_pairs={{0,2},{2,0},{4,6},{6,4},{8,10},{10,8},{12,14},{14,12},{1,3},{3,1},... | collective-permute-start | bytes 442376 | tf_op jit(solution)/shard_map/ppermute | solution.py:401
  77.7 24.4 %collective-permute-start.13 = (s16[136,1024]{1,0:T(8,128)(2,1)S(1)}, s16[136,1024]{1,0:T(8,128)(2,1)}, u32[]{:S(2)}, u32[]{:S(2)}) collective-permute-start(s16[136,1024]{1,0:T(8,128)(2,1)S(1)} %shard_map.73), channel_id=1, source_target_pairs={{0,8},{2,10},{4,12},{6,14},{8,0},{10,2},{12,4},{14,6},{1,9},{3,11}... | collective-permute-start | bytes 835592 | tf_op jit(solution)/shard_map/ppermute | solution.py:391
  82.3 8.3 %collective-permute-start.31 = (s16[72,1024]{1,0:T(8,128)(2,1)S(1)}, s16[72,1024]{1,0:T(8,128)(2,1)S(1)}, u32[]{:S(2)}, u32[]{:S(2)}) collective-permute-start(s16[72,1024]{1,0:T(8,128)(2,1)S(1)} %get-tuple-element.87), channel_id=1, source_target_pairs={{0,2},{2,0},{4,6},{6,4},{8,10},{10,8},{12,14},{14,12},{1,3},{3,1},... | collective-permute-start | bytes 442376 | tf_op jit(solution)/shard_map/ppermute | solution.py:401
  90.7 22.9 %collective-permute-start.9 = (s16[264,1024]{1,0:T(8,128)(2,1)}, s16[264,1024]{1,0:T(8,128)(2,1)}, u32[]{:S(2)}, u32[]{:S(2)}) collective-permute-start(s16[264,1024]{1,0:T(8,128)(2,1)} %get-tuple-element.90), channel_id=1, source_target_pairs={{0,4},{2,6},{4,0},{6,2},{8,12},{10,14},{12,8},{14,10},{1,5},{3,7},... | collective-permute-start | bytes 1622024 | tf_op jit(solution)/shard_map/ppermute | solution.py:352
  97.9 20.2 %collective-permute-start.16 = (bf16[512,512]{1,0:T(8,128)(2,1)}, bf16[512,512]{1,0:T(8,128)(2,1)}, u32[]{:S(2)}, u32[]{:S(2)}) collective-permute-start(bf16[512,512]{1,0:T(8,128)(2,1)} %shard_map.81), channel_id=1, source_target_pairs={{0,2},{2,0},{4,6},{6,4},{8,10},{10,8},{12,14},{14,12},{1,3},{3,1},... | collective-permute-start | bytes 1572872 | tf_op jit(solution)/shard_map/ppermute | solution.py:502
  102.1 14.6 %collective-permute-start.17 = (s16[136,1024]{1,0:T(8,128)(2,1)S(1)}, s16[136,1024]{1,0:T(8,128)(2,1)S(1)}, u32[]{:S(2)}, u32[]{:S(2)}) collective-permute-start(s16[136,1024]{1,0:T(8,128)(2,1)S(1)} %shard_map.77), channel_id=1, source_target_pairs={{0,8},{2,10},{4,12},{6,14},{8,0},{10,2},{12,4},{14,6},{1,9},{3,11}... | collective-permute-start | bytes 835592 | tf_op jit(solution)/shard_map/ppermute | solution.py:391
  106.3 14.1 %collective-permute-start.28 = (s16[72,1024]{1,0:T(8,128)(2,1)S(1)}, s16[72,1024]{1,0:T(8,128)(2,1)S(1)}, u32[]{:S(2)}, u32[]{:S(2)}) collective-permute-start(s16[72,1024]{1,0:T(8,128)(2,1)S(1)} %get-tuple-element.94), channel_id=1, source_target_pairs={{0,2},{2,0},{4,6},{6,4},{8,10},{10,8},{12,14},{14,12},{1,3},{3,1},... | collective-permute-start | bytes 442376 | tf_op jit(solution)/shard_map/ppermute | solution.py:401
  110.5 22.9 %collective-permute-start.15 = (s16[264,1024]{1,0:T(8,128)(2,1)S(1)}, s16[264,1024]{1,0:T(8,128)(2,1)S(1)}, u32[]{:S(2)}, u32[]{:S(2)}) collective-permute-start(s16[264,1024]{1,0:T(8,128)(2,1)S(1)} %get-tuple-element.96), channel_id=1, source_target_pairs={{0,4},{2,6},{4,0},{6,2},{8,12},{10,14},{12,8},{14,10},{1,5},{3,7},... | collective-permute-start | bytes 1622024 | tf_op jit(solution)/shard_map/ppermute | solution.py:352
  114.8 20.4 %collective-permute-start.14 = (s16[136,1024]{1,0:T(8,128)(2,1)S(1)}, s16[136,1024]{1,0:T(8,128)(2,1)S(1)}, u32[]{:S(2)}, u32[]{:S(2)}) collective-permute-start(s16[136,1024]{1,0:T(8,128)(2,1)S(1)} %shard_map.80), channel_id=1, source_target_pairs={{0,8},{2,10},{4,12},{6,14},{8,0},{10,2},{12,4},{14,6},{1,9},{3,11}... | collective-permute-start | bytes 835592 | tf_op jit(solution)/shard_map/ppermute | solution.py:391
  117.1 20.0 %collective-permute-start.30 = (s16[72,1024]{1,0:T(8,128)(2,1)S(1)}, s16[72,1024]{1,0:T(8,128)(2,1)S(1)}, u32[]{:S(2)}, u32[]{:S(2)}) collective-permute-start(s16[72,1024]{1,0:T(8,128)(2,1)S(1)} %get-tuple-element.101), channel_id=1, source_target_pairs={{0,2},{2,0},{4,6},{6,4},{8,10},{10,8},{12,14},{14,12},{1,3},{3,1},... | collective-permute-start | bytes 442376 | tf_op jit(solution)/shard_map/ppermute | solution.py:401
  120.4 16.9 %collective-permute-start.19 = (bf16[512,512]{1,0:T(8,128)(2,1)}, bf16[512,512]{1,0:T(8,128)(2,1)S(1)}, u32[]{:S(2)}, u32[]{:S(2)}) collective-permute-start(bf16[512,512]{1,0:T(8,128)(2,1)} %collective-permute-done.16.refs_3_.refs_4_), channel_id=1, source_target_pairs={{0,1},{1,0},{2,3},{3,2},{4,5},{5,4},{6,7},{7,6},{8,9},{9,8},{10,11... | collective-permute-start | bytes 1572872 | tf_op jit(solution)/shard_map/ppermute | solution.py:541
  120.6 22.5 %collective-permute-start.18 = (s16[264,512]{1,0:T(8,128)(2,1)S(1)}, s16[264,512]{1,0:T(8,128)(2,1)S(1)}, u32[]{:S(2)}, u32[]{:S(2)}) collective-permute-start(s16[264,512]{1,0:T(8,128)(2,1)S(1)} %get-tuple-element.103), channel_id=1, source_target_pairs={{0,4},{2,6},{4,0},{6,2},{8,12},{10,14},{12,8},{14,10},{1,5},{3,7},... | collective-permute-start | bytes 811016 | tf_op jit(solution)/shard_map/ppermute | solution.py:352
  133.7 21.5 %collective-permute-start.23 = (s16[136,1024]{1,0:T(8,128)(2,1)S(1)}, s16[136,1024]{1,0:T(8,128)(2,1)S(1)}, u32[]{:S(2)}, u32[]{:S(2)}) collective-permute-start(s16[136,1024]{1,0:T(8,128)(2,1)S(1)} %shard_map.84), channel_id=1, source_target_pairs={{0,8},{2,10},{4,12},{6,14},{8,0},{10,2},{12,4},{14,6},{1,9},{3,11}... | collective-permute-start | bytes 835592 | tf_op jit(solution)/shard_map/ppermute | solution.py:391
  136.5 19.7 %collective-permute-start.22 = (s16[72,1024]{1,0:T(8,128)(2,1)S(1)}, s16[72,1024]{1,0:T(8,128)(2,1)S(1)}, u32[]{:S(2)}, u32[]{:S(2)}) collective-permute-start(s16[72,1024]{1,0:T(8,128)(2,1)S(1)} %get-tuple-element.108), channel_id=1, source_target_pairs={{0,2},{2,0},{4,6},{6,4},{8,10},{10,8},{12,14},{14,12},{1,3},{3,1},... | collective-permute-start | bytes 442376 | tf_op jit(solution)/shard_map/ppermute | solution.py:401
  139.6 12.7 %collective-permute-start.21 = (s16[264,512]{1,0:T(8,128)(2,1)S(1)}, s16[264,512]{1,0:T(8,128)(2,1)S(1)}, u32[]{:S(2)}, u32[]{:S(2)}) collective-permute-start(s16[264,512]{1,0:T(8,128)(2,1)S(1)} %get-tuple-element.110), channel_id=1, source_target_pairs={{0,4},{2,6},{4,0},{6,2},{8,12},{10,14},{12,8},{14,10},{1,5},{3,7},... | collective-permute-start | bytes 811016 | tf_op jit(solution)/shard_map/ppermute | solution.py:352
  143.2 10.3 %collective-permute-start.20 = (s16[136,512]{1,0:T(8,128)(2,1)S(1)}, s16[136,512]{1,0:T(8,128)(2,1)S(1)}, u32[]{:S(2)}, u32[]{:S(2)}) collective-permute-start(s16[136,512]{1,0:T(8,128)(2,1)S(1)} %shard_map.87), channel_id=1, source_target_pairs={{0,8},{2,10},{4,12},{6,14},{8,0},{10,2},{12,4},{14,6},{1,9},{3,11}... | collective-permute-start | bytes 417800 | tf_op jit(solution)/shard_map/ppermute | solution.py:391
  152.4 7.5 %collective-permute-start.25 = (s16[136,512]{1,0:T(8,128)(2,1)S(1)}, s16[136,512]{1,0:T(8,128)(2,1)S(1)}, u32[]{:S(2)}, u32[]{:S(2)}) collective-permute-start(s16[136,512]{1,0:T(8,128)(2,1)S(1)} %shard_map.88), channel_id=1, source_target_pairs={{0,8},{2,10},{4,12},{6,14},{8,0},{10,2},{12,4},{14,6},{1,9},{3,11}... | collective-permute-start | bytes 417800 | tf_op jit(solution)/shard_map/ppermute | solution.py:391
  153.6 8.0 %collective-permute-start.24 = (s16[72,512]{1,0:T(8,128)(2,1)S(1)}, s16[72,512]{1,0:T(8,128)(2,1)S(1)}, u32[]{:S(2)}, u32[]{:S(2)}) collective-permute-start(s16[72,512]{1,0:T(8,128)(2,1)S(1)} %get-tuple-element.118), channel_id=1, source_target_pairs={{0,2},{2,0},{4,6},{6,4},{8,10},{10,8},{12,14},{14,12},{1,3},{3,1},... | collective-permute-start | bytes 221192 | tf_op jit(solution)/shard_map/ppermute | solution.py:401
  155.6 6.1 %collective-permute-start.26 = (s16[72,1024]{1,0:T(8,128)(2,1)S(1)}, s16[72,1024]{1,0:T(8,128)(2,1)S(1)}, u32[]{:S(2)}, u32[]{:S(2)}) collective-permute-start(s16[72,1024]{1,0:T(8,128)(2,1)S(1)} %get-tuple-element.116), channel_id=1, source_target_pairs={{0,2},{2,0},{4,6},{6,4},{8,10},{10,8},{12,14},{14,12},{1,3},{3,1},... | collective-permute-start | bytes 442376 | tf_op jit(solution)/shard_map/ppermute | solution.py:401
  160.0 4.4 %collective-permute-start.27 = (s16[72,512]{1,0:T(8,128)(2,1)S(1)}, s16[72,512]{1,0:T(8,128)(2,1)S(1)}, u32[]{:S(2)}, u32[]{:S(2)}) collective-permute-start(s16[72,512]{1,0:T(8,128)(2,1)S(1)} %get-tuple-element.119), channel_id=1, source_target_pairs={{0,2},{2,0},{4,6},{6,4},{8,10},{10,8},{12,14},{14,12},{1,3},{3,1},... | collective-permute-start | bytes 221192 | tf_op jit(solution)/shard_map/ppermute | solution.py:401
  (36 other events, 205.5 us)

commit v5 on v4

--- a/solution.py
+++ b/solution.py
@@ -128,19 +128,21 @@
     )(plan, source)
 
 
-def turn_kernel(at, source, out):
-    out[...] = source[...].T
+def turn_kernel(first, at, source, out):
+    size = out.shape[0] // 4
+    for index in range(4):
+        columns = pl.ds(pl.multiple_of(at[first + index] * size, size), size)
+        out[index * size : (index + 1) * size, :] = source[:, columns].T
 
 
 def turn(plan, source, first):
     tokens = source.shape[0]
-    size = ROW_DEV // 4
     return gridded(
-        turn_kernel,
+        functools.partial(turn_kernel, first),
         plan,
-        4,
-        [pl.BlockSpec((tokens, size), lambda i, at: (0, at[first + i]))],
-        pl.BlockSpec((size, tokens), lambda i, at: (i, 0)),
+        1,
+        [pl.BlockSpec((tokens, ROW_DEV), lambda i, at: (0, 0))],
+        pl.BlockSpec((ROW_DEV, tokens), lambda i, at: (0, 0)),
         jax.ShapeDtypeStruct((ROW_DEV, tokens), source.dtype),
         source,
     )

time: 167 us -> 166 us (level)
  waiting for transfers between devices: 50.3 us -> 53.8 us
  Pallas kernels: 52.5 us -> 50 us
  starting transfers between devices: 38.3 us -> 36.6 us
    pallas_call x13, Pallas kernels: 36.4 us -> 33.8 us  [gridded(): pl.pallas_call(kernel, grid_spec=pltpu.PrefetchScalarGridSpec(num_scalar_...]
  transfers between devices with their start and end apart: 32 -> 32, of which waited for: 11 -> 13; matrix products, arithmetic and copies ran while one was open for 3% -> 3% of each run, Pallas kernels for 32% -> 30%
where the time goes in v5:
time: 166 us
  waiting for transfers between devices  53.8 us (32%)
  Pallas kernels  50 us (30%)
  starting transfers between devices  36.6 us (22%)
  local copies, waits for them, and re-layouts  14.4 us (9%)
  other arithmetic  5.12 us (3%)
  blocking collectives  4.06 us (2%)
    ppermute x8, waiting for transfers between devices, begin(): came1[k] = lax.ppermute(sent1[k], 'dp', swap(8, 2))  40 us
    pallas_call x13, Pallas kernels, gridded(): pl.pallas_call(kernel, grid_spec=pltpu.PrefetchScalarGridSpec(num_scalar_...  33.8 us
    unnamed x80, local copies, waits for them, and re-layouts  12.9 us
    ppermute x8, starting transfers between devices, begin(): came1[k] = lax.ppermute(sent1[k], 'dp', swap(8, 2))  12.6 us
    pallas_call x16, Pallas kernels, blocked(): pl.pallas_call(kernel, grid=(width // size,), in_specs=[pl.BlockSpec((row...  11.2 us
    ppermute x8, starting transfers between devices, pipeline(): came3[j] = lax.ppermute(sent, 'dp', swap(8))  9.33 us
    ppermute x8, starting transfers between devices, pipeline(): came2[k] = lax.ppermute(sent, 'dp', swap(8, 4))  8.68 us
    ppermute x8, waiting for transfers between devices, pipeline(): came2[k] = lax.ppermute(sent, 'dp', swap(8, 4))  8.67 us
  transfers between devices with their start and end apart: 32, of which 13 were waited for; matrix products, arithmetic and copies ran while one was open for 3% of the time, Pallas kernels for 30%

profile of v5, /device:TPU:0, one launch (start us, length us, event | category | flops | bytes accessed | tf_op | source)
XLA Modules:
  0.0 165.6 jit_solution(6055704985230509406)
XLA Ops:
  1.3 1.9 %copy-done = bf16[512,3072]{1,0:T(8,128)(2,1)S(1)} copy-done((bf16[512,3072]{1,0:T(8,128)(2,1)S(1)}, bf16[512,3072]{1,0:T(8,128)(2,1)}, u32[]{:S(2)}) %copy-start) | copy-done | bytes 3145752
  4.8 2.8 %collective-permute-start.3 = (bf16[512,1280]{1,0:T(8,128)(2,1)}, bf16[512,1280]{1,0:T(8,128)(2,1)}, u32[]{:S(2)}, u32[]{:S(2)}) collective-permute-start(bf16[512,1280]{1,0:T(8,128)(2,1)} %shard_map.66), channel_id=1, source_target_pairs={{0,2},{2,0},{4,6},{6,4},{8,10},{10,8},{12,14},{14,12},{1,3},{3,1},... | collective-permute-start | bytes 3932168 | tf_op jit(solution)/shard_map/ppermute | solution.py:489
  8.3 2.5 %shard_map.60 = (f32[256,1024]{1,0:T(8,128)S(1)}, s16[264,1024]{1,0:T(8,128)(2,1)}) custom-call(s32[35]{0:T(128)S(1)} %stack.115.at, bf16[512,512]{1,0:T(8,128)(2,1)S(1)} %shard_map.59.rows, bf16[512,3072]{1,0:T(8,128)(2,1)S(1)} %copy-done, bf16[512,3072]{1,0:T(8,128)(2,1)S(1)} %copy-done), custom_call_target="tpu_custom_call" | custom-call | tf_op jit(solution)/shard_map/pallas_call | solution.py:89
  13.4 2.5 %shard_map.61 = (f32[256,1024]{1,0:T(8,128)S(1)}, s16[264,1024]{1,0:T(8,128)(2,1)}) custom-call(s32[35]{0:T(128)S(1)} %stack.115.at, bf16[512,512]{1,0:T(8,128)(2,1)S(1)} %shard_map.59.rows, bf16[512,3072]{1,0:T(8,128)(2,1)S(1)} %collective-permute-done.1.refs_0_.refs_1_, bf16[512,3072]{1,0:T(8,128)(2,1)S(1)} %collective-permute-done.1.refs_0_.refs_1_), custom_call_target="tpu_custom_call" | custom-call | tf_op jit(solution)/shard_map/pallas_call | solution.py:89
  18.6 1.9 %copy-done.10 = bf16[512,3072]{1,0:T(8,128)(2,1)S(1)} copy-done((bf16[512,3072]{1,0:T(8,128)(2,1)S(1)}, bf16[512,3072]{1,0:T(8,128)(2,1)}, u32[]{:S(2)}) %copy-start.10) | copy-done | bytes 3145752
  21.8 4.1 %psum.7.moments = f32[8,512]{1,0:T(8,128)} all-reduce(f32[8,512]{1,0:T(8,128)S(1)} %shard_map.62), channel_id=1, replica_groups=mesh['groups'=2,'dp'=8,'tensor'=2] {'tensor'}, use_global_device_ids=true, to_apply=%region_0.1 | all-reduce | flops 4096 | bytes 32768 | tf_op jit(solution)/shard_map/psum | solution.py:493
  25.8 1.9 %copy-done.11 = bf16[512,3072]{1,0:T(8,128)(2,1)S(1)} copy-done((bf16[512,3072]{1,0:T(8,128)(2,1)S(1)}, bf16[512,3072]{1,0:T(8,128)(2,1)}, u32[]{:S(2)}) %copy-start.11) | copy-done | bytes 3145752
  28.4 5.8 %shard_map.63.source.refs_0_.refs_1_ = bf16[512,3072]{1,0:T(8,128)(2,1)S(1)} custom-call(s32[35]{0:T(128)S(1)} %stack.115.at, s32[1,512]{1,0:T(1,128)S(1)} %bitcast.36, f32[8,512]{1,0:T(8,128)S(1)} %copy-done.32, bf16[512,3072]{1,0:T(8,128)(2,1)S(1)} %copy-done.11, f32[16,6144]{1,0:T(8,128)S(1)} %reshape.11.table), custom_call_target="tpu_custom_call" | custom-call | tf_op jit(solution)/shard_map/pallas_call | solution.py:89
  34.2 3.7 %collective-permute-done.2.came.came1 = s16[264,1024]{1,0:T(8,128)(2,1)} collective-permute-done((s16[264,1024]{1,0:T(8,128)(2,1)}, s16[264,1024]{1,0:T(8,128)(2,1)}, u32[]{:S(2)}, u32[]{:S(2)}) %collective-permute-start.2) | collective-permute-done | bytes 540704 | tf_op jit(solution)/shard_map/ppermute | solution.py:354
  40.9 2.8 %collective-permute-start.7 = (s16[136,1024]{1,0:T(8,128)(2,1)S(1)}, s16[136,1024]{1,0:T(8,128)(2,1)S(1)}, u32[]{:S(2)}, u32[]{:S(2)}) collective-permute-start(s16[136,1024]{1,0:T(8,128)(2,1)S(1)} %shard_map.64), channel_id=1, source_target_pairs={{0,8},{2,10},{4,12},{6,14},{8,0},{10,2},{12,4},{14,6},{1,9},{3,11}... | collective-permute-start | bytes 835592 | tf_op jit(solution)/shard_map/ppermute | solution.py:393
  43.7 1.8 %shard_map.67.refs_2_ = bf16[512,512]{1,0:T(8,128)(2,1)S(1)} custom-call(s32[35]{0:T(128)S(1)} %stack.115.at, bf16[512,1280]{1,0:T(8,128)(2,1)} %collective-permute-done.3.source.refs_3_.refs_4_), custom_call_target="tpu_custom_call" | custom-call | tf_op jit(solution)/shard_map/pallas_call | solution.py:89
  45.5 3.4 %shard_map.68 = (f32[256,1024]{1,0:T(8,128)S(1)}, s16[264,1024]{1,0:T(8,128)(2,1)S(1)}) custom-call(s32[35]{0:T(128)S(1)} %stack.115.at, bf16[512,512]{1,0:T(8,128)(2,1)S(1)} %copy-done.9, bf16[512,3072]{1,0:T(8,128)(2,1)S(1)} %copy-done.1, bf16[512,3072]{1,0:T(8,128)(2,1)S(1)} %copy-done.1, bf16[512,512]{1,0:T(8,128)(2,1)S(1)} %shard_map.67.refs_2_, ...), custom_call_target="tpu_custom_call" | custom-call | tf_op jit(solution)/shard_map/pallas_call | solution.py:89
  52.7 3.6 %collective-permute-done.7.came2 = s16[136,1024]{1,0:T(8,128)(2,1)S(1)} collective-permute-done((s16[136,1024]{1,0:T(8,128)(2,1)S(1)}, s16[136,1024]{1,0:T(8,128)(2,1)S(1)}, u32[]{:S(2)}, u32[]{:S(2)}) %collective-permute-start.7) | collective-permute-done | bytes 278560 | tf_op jit(solution)/shard_map/ppermute | solution.py:393
  57.7 2.5 %shard_map.72 = (f32[256,1024]{1,0:T(8,128)S(1)}, s16[264,1024]{1,0:T(8,128)(2,1)S(1)}) custom-call(s32[35]{0:T(128)S(1)} %stack.115.at, bf16[512,512]{1,0:T(8,128)(2,1)S(1)} %copy-done.9, bf16[512,3072]{1,0:T(8,128)(2,1)S(1)} %copy-done.3, bf16[512,3072]{1,0:T(8,128)(2,1)S(1)} %copy-done.3, bf16[512,512]{1,0:T(8,128)(2,1)S(1)} %shard_map.67.refs_2_, ...), custom_call_target="tpu_custom_call" | custom-call | tf_op jit(solution)/shard_map/pallas_call | solution.py:89
  60.2 13.1 %collective-permute-done.5.came.came1 = s16[264,1024]{1,0:T(8,128)(2,1)S(1)} collective-permute-done((s16[264,1024]{1,0:T(8,128)(2,1)S(1)}, s16[264,1024]{1,0:T(8,128)(2,1)S(1)}, u32[]{:S(2)}, u32[]{:S(2)}) %collective-permute-start.5) | collective-permute-done | bytes 540704 | tf_op jit(solution)/shard_map/ppermute | solution.py:354
  76.9 2.9 %collective-permute-start.13 = (s16[136,1024]{1,0:T(8,128)(2,1)S(1)}, s16[136,1024]{1,0:T(8,128)(2,1)}, u32[]{:S(2)}, u32[]{:S(2)}) collective-permute-start(s16[136,1024]{1,0:T(8,128)(2,1)S(1)} %shard_map.73), channel_id=1, source_target_pairs={{0,8},{2,10},{4,12},{6,14},{8,0},{10,2},{12,4},{14,6},{1,9},{3,11}... | collective-permute-start | bytes 835592 | tf_op jit(solution)/shard_map/ppermute | solution.py:393
  83.1 1.8 %shard_map.75.refs_2_ = bf16[512,512]{1,0:T(8,128)(2,1)S(1)} custom-call(s32[35]{0:T(128)S(1)} %stack.115.at, bf16[512,1280]{1,0:T(8,128)(2,1)} %collective-permute-done.4.source.refs_3_.refs_4_), custom_call_target="tpu_custom_call" | custom-call | tf_op jit(solution)/shard_map/pallas_call | solution.py:89
  84.9 4.0 %shard_map.76 = (f32[256,1024]{1,0:T(8,128)S(1)}, s16[264,1024]{1,0:T(8,128)(2,1)}) custom-call(s32[35]{0:T(128)S(1)} %stack.115.at, bf16[512,512]{1,0:T(8,128)(2,1)S(1)} %shard_map.65.rows, bf16[512,3072]{1,0:T(8,128)(2,1)S(1)} %shard_map.63.source.refs_0_.refs_1_, bf16[512,3072]{1,0:T(8,128)(2,1)S(1)} %shard_map.63.source.refs_0_.refs_1_, ...), custom_call_target="tpu_custom_call" | custom-call | tf_op jit(solution)/shard_map/pallas_call | solution.py:89
  88.9 1.8 %collective-permute-start.9 = (s16[264,1024]{1,0:T(8,128)(2,1)}, s16[264,1024]{1,0:T(8,128)(2,1)}, u32[]{:S(2)}, u32[]{:S(2)}) collective-permute-start(s16[264,1024]{1,0:T(8,128)(2,1)} %get-tuple-element.90), channel_id=1, source_target_pairs={{0,4},{2,6},{4,0},{6,2},{8,12},{10,14},{12,8},{14,10},{1,5},{3,7},... | collective-permute-start | bytes 1622024 | tf_op jit(solution)/shard_map/ppermute | solution.py:354
  92.1 4.1 %collective-permute-done.12.came.came1 = s16[264,1024]{1,0:T(8,128)(2,1)S(1)} collective-permute-done((s16[264,1024]{1,0:T(8,128)(2,1)S(1)}, s16[264,1024]{1,0:T(8,128)(2,1)S(1)}, u32[]{:S(2)}, u32[]{:S(2)}) %collective-permute-start.12) | collective-permute-done | bytes 540704 | tf_op jit(solution)/shard_map/ppermute | solution.py:354
  105.7 3.5 %shard_map.79 = (f32[256,1024]{1,0:T(8,128)S(1)}, s16[264,1024]{1,0:T(8,128)(2,1)S(1)}) custom-call(s32[35]{0:T(128)S(1)} %stack.115.at, bf16[512,512]{1,0:T(8,128)(2,1)S(1)} %copy-done.5, bf16[512,3072]{1,0:T(8,128)(2,1)} %collective-permute-done.10.refs_0_.refs_1_, bf16[512,3072]{1,0:T(8,128)(2,1)} %collective-permute-done.10.refs_0_.refs_1_, ...), custom_call_target="tpu_custom_call" | custom-call | tf_op jit(solution)/shard_map/pallas_call | solution.py:89
  109.2 2.5 %collective-permute-start.15 = (s16[264,1024]{1,0:T(8,128)(2,1)S(1)}, s16[264,1024]{1,0:T(8,128)(2,1)S(1)}, u32[]{:S(2)}, u32[]{:S(2)}) collective-permute-start(s16[264,1024]{1,0:T(8,128)(2,1)S(1)} %get-tuple-element.96), channel_id=1, source_target_pairs={{0,4},{2,6},{4,0},{6,2},{8,12},{10,14},{12,8},{14,10},{1,5},{3,7},... | collective-permute-start | bytes 1622024 | tf_op jit(solution)/shard_map/ppermute | solution.py:354
  113.6 2.3 %collective-permute-done.17.came2 = s16[136,1024]{1,0:T(8,128)(2,1)S(1)} collective-permute-done((s16[136,1024]{1,0:T(8,128)(2,1)S(1)}, s16[136,1024]{1,0:T(8,128)(2,1)S(1)}, u32[]{:S(2)}, u32[]{:S(2)}) %collective-permute-start.17) | collective-permute-done | bytes 278560 | tf_op jit(solution)/shard_map/ppermute | solution.py:393
  116.8 2.3 %shard_map.83 = (f32[256,512]{1,0:T(8,128)S(1)}, s16[264,512]{1,0:T(8,128)(2,1)S(1)}) custom-call(s32[35]{0:T(128)S(1)} %stack.115.at, bf16[512,512]{1,0:T(8,128)(2,1)S(1)} %copy-done.5, bf16[512,3072]{1,0:T(8,128)(2,1)S(1)} %shard_map.63.source.refs_0_.refs_1_, bf16[512,3072]{1,0:T(8,128)(2,1)S(1)} %shard_map.63.source.refs_0_.refs_1_, ...), custom_call_target="tpu_custom_call" | custom-call | tf_op jit(solution)/shard_map/pallas_call | solution.py:89
  119.3 2.0 %collective-permute-start.18 = (s16[264,512]{1,0:T(8,128)(2,1)S(1)}, s16[264,512]{1,0:T(8,128)(2,1)S(1)}, u32[]{:S(2)}, u32[]{:S(2)}) collective-permute-start(s16[264,512]{1,0:T(8,128)(2,1)S(1)} %get-tuple-element.103), channel_id=1, source_target_pairs={{0,4},{2,6},{4,0},{6,2},{8,12},{10,14},{12,8},{14,10},{1,5},{3,7},... | collective-permute-start | bytes 811016 | tf_op jit(solution)/shard_map/ppermute | solution.py:354
  122.3 10.3 %collective-permute-done.15.came.came1 = s16[264,1024]{1,0:T(8,128)(2,1)S(1)} collective-permute-done((s16[264,1024]{1,0:T(8,128)(2,1)S(1)}, s16[264,1024]{1,0:T(8,128)(2,1)S(1)}, u32[]{:S(2)}, u32[]{:S(2)}) %collective-permute-start.15) | collective-permute-done | bytes 540704 | tf_op jit(solution)/shard_map/ppermute | solution.py:354
  135.5 2.3 %shard_map.86 = (f32[256,512]{1,0:T(8,128)S(1)}, s16[264,512]{1,0:T(8,128)(2,1)S(1)}) custom-call(s32[35]{0:T(128)S(1)} %stack.115.at, bf16[512,512]{1,0:T(8,128)(2,1)S(1)} %copy-done.5, bf16[512,3072]{1,0:T(8,128)(2,1)} %collective-permute-done.10.refs_0_.refs_1_, bf16[512,3072]{1,0:T(8,128)(2,1)} %collective-permute-done.10.refs_0_.refs_1_, ...), custom_call_target="tpu_custom_call" | custom-call | tf_op jit(solution)/shard_map/pallas_call | solution.py:89
  137.8 2.6 %collective-permute-start.21 = (s16[264,512]{1,0:T(8,128)(2,1)S(1)}, s16[264,512]{1,0:T(8,128)(2,1)S(1)}, u32[]{:S(2)}, u32[]{:S(2)}) collective-permute-start(s16[264,512]{1,0:T(8,128)(2,1)S(1)} %get-tuple-element.110), channel_id=1, source_target_pairs={{0,4},{2,6},{4,0},{6,2},{8,12},{10,14},{12,8},{14,10},{1,5},{3,7},... | collective-permute-start | bytes 811016 | tf_op jit(solution)/shard_map/ppermute | solution.py:354
  143.3 8.1 %collective-permute-done.21.came.came1 = s16[264,512]{1,0:T(8,128)(2,1)S(1)} collective-permute-done((s16[264,512]{1,0:T(8,128)(2,1)S(1)}, s16[264,512]{1,0:T(8,128)(2,1)S(1)}, u32[]{:S(2)}, u32[]{:S(2)}) %collective-permute-start.21) | collective-permute-done | bytes 270368 | tf_op jit(solution)/shard_map/ppermute | solution.py:354
  152.3 3.6 %collective-permute-start.24 = (s16[72,512]{1,0:T(8,128)(2,1)S(1)}, s16[72,512]{1,0:T(8,128)(2,1)S(1)}, u32[]{:S(2)}, u32[]{:S(2)}) collective-permute-start(s16[72,512]{1,0:T(8,128)(2,1)S(1)} %get-tuple-element.118), channel_id=1, source_target_pairs={{0,2},{2,0},{4,6},{6,4},{8,10},{10,8},{12,14},{14,12},{1,3},{3,1},... | collective-permute-start | bytes 221192 | tf_op jit(solution)/shard_map/ppermute | solution.py:403
  156.5 2.7 %collective-permute-done.25.came2 = s16[136,512]{1,0:T(8,128)(2,1)S(1)} collective-permute-done((s16[136,512]{1,0:T(8,128)(2,1)S(1)}, s16[136,512]{1,0:T(8,128)(2,1)S(1)}, u32[]{:S(2)}, u32[]{:S(2)}) %collective-permute-start.25) | collective-permute-done | bytes 139296 | tf_op jit(solution)/shard_map/ppermute | solution.py:393
  161.9 1.9 %collective-permute-done.27 = s16[72,512]{1,0:T(8,128)(2,1)S(1)} collective-permute-done((s16[72,512]{1,0:T(8,128)(2,1)S(1)}, s16[72,512]{1,0:T(8,128)(2,1)S(1)}, u32[]{:S(2)}, u32[]{:S(2)}) %collective-permute-start.27) | collective-permute-done | bytes 73760 | tf_op jit(solution)/shard_map/ppermute | solution.py:403
  (180 shorter events, 51.3 us)
Async XLA Ops:
  0.6 12.8 %collective-permute-start.1 = (bf16[512,3072]{1,0:T(8,128)(2,1)}, bf16[512,3072]{1,0:T(8,128)(2,1)S(1)}, u32[]{:S(2)}, u32[]{:S(2)}) collective-permute-start(bf16[512,3072]{1,0:T(8,128)(2,1)} %refs_1_.3), channel_id=1, source_target_pairs={{0,1},{1,0},{2,3},{3,2},{4,5},{5,4},{6,7},{7,6},{8,9},{9,8},{10,11... | collective-permute-start | bytes 9437192 | tf_op jit(solution)/shard_map/ppermute | solution.py:487
  4.8 34.5 %collective-permute-start.3 = (bf16[512,1280]{1,0:T(8,128)(2,1)}, bf16[512,1280]{1,0:T(8,128)(2,1)}, u32[]{:S(2)}, u32[]{:S(2)}) collective-permute-start(bf16[512,1280]{1,0:T(8,128)(2,1)} %shard_map.66), channel_id=1, source_target_pairs={{0,2},{2,0},{4,6},{6,4},{8,10},{10,8},{12,14},{14,12},{1,3},{3,1},... | collective-permute-start | bytes 3932168 | tf_op jit(solution)/shard_map/ppermute | solution.py:489
  11.8 22.4 %collective-permute-start = (s16[264,1024]{1,0:T(8,128)(2,1)}, s16[264,1024]{1,0:T(8,128)(2,1)}, u32[]{:S(2)}, u32[]{:S(2)}) collective-permute-start(s16[264,1024]{1,0:T(8,128)(2,1)} %get-tuple-element.67), channel_id=1, source_target_pairs={{0,4},{2,6},{4,0},{6,2},{8,12},{10,14},{12,8},{14,10},{1,5},{3,7},... | collective-permute-start | bytes 1622024 | tf_op jit(solution)/shard_map/ppermute | solution.py:354
  16.9 21.1 %collective-permute-start.2 = (s16[264,1024]{1,0:T(8,128)(2,1)}, s16[264,1024]{1,0:T(8,128)(2,1)}, u32[]{:S(2)}, u32[]{:S(2)}) collective-permute-start(s16[264,1024]{1,0:T(8,128)(2,1)} %get-tuple-element.68), channel_id=1, source_target_pairs={{0,4},{2,6},{4,0},{6,2},{8,12},{10,14},{12,8},{14,10},{1,5},{3,7},... | collective-permute-start | bytes 1622024 | tf_op jit(solution)/shard_map/ppermute | solution.py:354
  39.2 66.5 %collective-permute-start.10 = (bf16[512,3072]{1,0:T(8,128)(2,1)S(1)}, bf16[512,3072]{1,0:T(8,128)(2,1)}, u32[]{:S(2)}, u32[]{:S(2)}) collective-permute-start(bf16[512,3072]{1,0:T(8,128)(2,1)S(1)} %shard_map.63.source.refs_0_.refs_1_), channel_id=1, source_target_pairs={{0,1},{1,0},{2,3},{3,2},{4,5},{5,4},{6,7},{7,6},{8,9},{9,8},{10,11... | collective-permute-start | bytes 9437192 | tf_op jit(solution)/shard_map/ppermute | solution.py:505
  39.3 18.4 %collective-permute-start.6 = (bf16[512,1280]{1,0:T(8,128)(2,1)}, bf16[512,1280]{1,0:T(8,128)(2,1)S(1)}, u32[]{:S(2)}, u32[]{:S(2)}) collective-permute-start(bf16[512,1280]{1,0:T(8,128)(2,1)} %collective-permute-done.3.source.refs_3_.refs_4_), channel_id=1, source_target_pairs={{0,1},{1,0},{2,3},{3,2},{4,5},{5,4},{6,7},{7,6},{8,9},{9,8},{10,11... | collective-permute-start | bytes 3932168 | tf_op jit(solution)/shard_map/ppermute | solution.py:543
  40.5 34.5 %collective-permute-start.4 = (bf16[512,1280]{1,0:T(8,128)(2,1)S(1)}, bf16[512,1280]{1,0:T(8,128)(2,1)}, u32[]{:S(2)}, u32[]{:S(2)}) collective-permute-start(bf16[512,1280]{1,0:T(8,128)(2,1)S(1)} %shard_map.69), channel_id=1, source_target_pairs={{0,2},{2,0},{4,6},{6,4},{8,10},{10,8},{12,14},{14,12},{1,3},{3,1},... | collective-permute-start | bytes 3932168 | tf_op jit(solution)/shard_map/ppermute | solution.py:504
  40.9 15.5 %collective-permute-start.7 = (s16[136,1024]{1,0:T(8,128)(2,1)S(1)}, s16[136,1024]{1,0:T(8,128)(2,1)S(1)}, u32[]{:S(2)}, u32[]{:S(2)}) collective-permute-start(s16[136,1024]{1,0:T(8,128)(2,1)S(1)} %shard_map.64), channel_id=1, source_target_pairs={{0,8},{2,10},{4,12},{6,14},{8,0},{10,2},{12,4},{14,6},{1,9},{3,11}... | collective-permute-start | bytes 835592 | tf_op jit(solution)/shard_map/ppermute | solution.py:393
  48.9 24.5 %collective-permute-start.5 = (s16[264,1024]{1,0:T(8,128)(2,1)S(1)}, s16[264,1024]{1,0:T(8,128)(2,1)S(1)}, u32[]{:S(2)}, u32[]{:S(2)}) collective-permute-start(s16[264,1024]{1,0:T(8,128)(2,1)S(1)} %get-tuple-element.76), channel_id=1, source_target_pairs={{0,4},{2,6},{4,0},{6,2},{8,12},{10,14},{12,8},{14,10},{1,5},{3,7},... | collective-permute-start | bytes 1622024 | tf_op jit(solution)/shard_map/ppermute | solution.py:354
  56.4 17.3 %collective-permute-start.8 = (s16[136,1024]{1,0:T(8,128)(2,1)S(1)}, s16[136,1024]{1,0:T(8,128)(2,1)S(1)}, u32[]{:S(2)}, u32[]{:S(2)}) collective-permute-start(s16[136,1024]{1,0:T(8,128)(2,1)S(1)} %shard_map.70), channel_id=1, source_target_pairs={{0,8},{2,10},{4,12},{6,14},{8,0},{10,2},{12,4},{14,6},{1,9},{3,11}... | collective-permute-start | bytes 835592 | tf_op jit(solution)/shard_map/ppermute | solution.py:393
  75.0 30.0 %collective-permute-start.11 = (bf16[512,1280]{1,0:T(8,128)(2,1)}, bf16[512,1280]{1,0:T(8,128)(2,1)}, u32[]{:S(2)}, u32[]{:S(2)}) collective-permute-start(bf16[512,1280]{1,0:T(8,128)(2,1)} %collective-permute-done.4.source.refs_3_.refs_4_), channel_id=1, source_target_pairs={{0,1},{1,0},{2,3},{3,2},{4,5},{5,4},{6,7},{7,6},{8,9},{9,8},{10,11... | collective-permute-start | bytes 3932168 | tf_op jit(solution)/shard_map/ppermute | solution.py:543
  75.1 21.1 %collective-permute-start.12 = (s16[264,1024]{1,0:T(8,128)(2,1)S(1)}, s16[264,1024]{1,0:T(8,128)(2,1)S(1)}, u32[]{:S(2)}, u32[]{:S(2)}) collective-permute-start(s16[264,1024]{1,0:T(8,128)(2,1)S(1)} %get-tuple-element.84), channel_id=1, source_target_pairs={{0,4},{2,6},{4,0},{6,2},{8,12},{10,14},{12,8},{14,10},{1,5},{3,7},... | collective-permute-start | bytes 1622024 | tf_op jit(solution)/shard_map/ppermute | solution.py:354
  75.2 6.3 %collective-permute-start.29 = (s16[72,1024]{1,0:T(8,128)(2,1)S(1)}, s16[72,1024]{1,0:T(8,128)(2,1)}, u32[]{:S(2)}, u32[]{:S(2)}) collective-permute-start(s16[72,1024]{1,0:T(8,128)(2,1)S(1)} %get-tuple-element.82), channel_id=1, source_target_pairs={{0,2},{2,0},{4,6},{6,4},{8,10},{10,8},{12,14},{14,12},{1,3},{3,1},... | collective-permute-start | bytes 442376 | tf_op jit(solution)/shard_map/ppermute | solution.py:403
  76.9 24.4 %collective-permute-start.13 = (s16[136,1024]{1,0:T(8,128)(2,1)S(1)}, s16[136,1024]{1,0:T(8,128)(2,1)}, u32[]{:S(2)}, u32[]{:S(2)}) collective-permute-start(s16[136,1024]{1,0:T(8,128)(2,1)S(1)} %shard_map.73), channel_id=1, source_target_pairs={{0,8},{2,10},{4,12},{6,14},{8,0},{10,2},{12,4},{14,6},{1,9},{3,11}... | collective-permute-start | bytes 835592 | tf_op jit(solution)/shard_map/ppermute | solution.py:393
  81.5 7.4 %collective-permute-start.31 = (s16[72,1024]{1,0:T(8,128)(2,1)S(1)}, s16[72,1024]{1,0:T(8,128)(2,1)S(1)}, u32[]{:S(2)}, u32[]{:S(2)}) collective-permute-start(s16[72,1024]{1,0:T(8,128)(2,1)S(1)} %get-tuple-element.87), channel_id=1, source_target_pairs={{0,2},{2,0},{4,6},{6,4},{8,10},{10,8},{12,14},{14,12},{1,3},{3,1},... | collective-permute-start | bytes 442376 | tf_op jit(solution)/shard_map/ppermute | solution.py:403
  88.9 23.3 %collective-permute-start.9 = (s16[264,1024]{1,0:T(8,128)(2,1)}, s16[264,1024]{1,0:T(8,128)(2,1)}, u32[]{:S(2)}, u32[]{:S(2)}) collective-permute-start(s16[264,1024]{1,0:T(8,128)(2,1)} %get-tuple-element.90), channel_id=1, source_target_pairs={{0,4},{2,6},{4,0},{6,2},{8,12},{10,14},{12,8},{14,10},{1,5},{3,7},... | collective-permute-start | bytes 1622024 | tf_op jit(solution)/shard_map/ppermute | solution.py:354
  97.1 19.8 %collective-permute-start.16 = (bf16[512,512]{1,0:T(8,128)(2,1)}, bf16[512,512]{1,0:T(8,128)(2,1)}, u32[]{:S(2)}, u32[]{:S(2)}) collective-permute-start(bf16[512,512]{1,0:T(8,128)(2,1)} %shard_map.81), channel_id=1, source_target_pairs={{0,2},{2,0},{4,6},{6,4},{8,10},{10,8},{12,14},{14,12},{1,3},{3,1},... | collective-permute-start | bytes 1572872 | tf_op jit(solution)/shard_map/ppermute | solution.py:504
  101.3 14.6 %collective-permute-start.17 = (s16[136,1024]{1,0:T(8,128)(2,1)S(1)}, s16[136,1024]{1,0:T(8,128)(2,1)S(1)}, u32[]{:S(2)}, u32[]{:S(2)}) collective-permute-start(s16[136,1024]{1,0:T(8,128)(2,1)S(1)} %shard_map.77), channel_id=1, source_target_pairs={{0,8},{2,10},{4,12},{6,14},{8,0},{10,2},{12,4},{14,6},{1,9},{3,11}... | collective-permute-start | bytes 835592 | tf_op jit(solution)/shard_map/ppermute | solution.py:393
  105.1 14.1 %collective-permute-start.28 = (s16[72,1024]{1,0:T(8,128)(2,1)S(1)}, s16[72,1024]{1,0:T(8,128)(2,1)S(1)}, u32[]{:S(2)}, u32[]{:S(2)}) collective-permute-start(s16[72,1024]{1,0:T(8,128)(2,1)S(1)} %get-tuple-element.94), channel_id=1, source_target_pairs={{0,2},{2,0},{4,6},{6,4},{8,10},{10,8},{12,14},{14,12},{1,3},{3,1},... | collective-permute-start | bytes 442376 | tf_op jit(solution)/shard_map/ppermute | solution.py:403
  109.2 23.3 %collective-permute-start.15 = (s16[264,1024]{1,0:T(8,128)(2,1)S(1)}, s16[264,1024]{1,0:T(8,128)(2,1)S(1)}, u32[]{:S(2)}, u32[]{:S(2)}) collective-permute-start(s16[264,1024]{1,0:T(8,128)(2,1)S(1)} %get-tuple-element.96), channel_id=1, source_target_pairs={{0,4},{2,6},{4,0},{6,2},{8,12},{10,14},{12,8},{14,10},{1,5},{3,7},... | collective-permute-start | bytes 1622024 | tf_op jit(solution)/shard_map/ppermute | solution.py:354
  113.5 20.1 %collective-permute-start.14 = (s16[136,1024]{1,0:T(8,128)(2,1)S(1)}, s16[136,1024]{1,0:T(8,128)(2,1)S(1)}, u32[]{:S(2)}, u32[]{:S(2)}) collective-permute-start(s16[136,1024]{1,0:T(8,128)(2,1)S(1)} %shard_map.80), channel_id=1, source_target_pairs={{0,8},{2,10},{4,12},{6,14},{8,0},{10,2},{12,4},{14,6},{1,9},{3,11}... | collective-permute-start | bytes 835592 | tf_op jit(solution)/shard_map/ppermute | solution.py:393
  116.3 19.1 %collective-permute-start.30 = (s16[72,1024]{1,0:T(8,128)(2,1)S(1)}, s16[72,1024]{1,0:T(8,128)(2,1)S(1)}, u32[]{:S(2)}, u32[]{:S(2)}) collective-permute-start(s16[72,1024]{1,0:T(8,128)(2,1)S(1)} %get-tuple-element.101), channel_id=1, source_target_pairs={{0,2},{2,0},{4,6},{6,4},{8,10},{10,8},{12,14},{14,12},{1,3},{3,1},... | collective-permute-start | bytes 442376 | tf_op jit(solution)/shard_map/ppermute | solution.py:403
  119.1 16.4 %collective-permute-start.19 = (bf16[512,512]{1,0:T(8,128)(2,1)}, bf16[512,512]{1,0:T(8,128)(2,1)S(1)}, u32[]{:S(2)}, u32[]{:S(2)}) collective-permute-start(bf16[512,512]{1,0:T(8,128)(2,1)} %collective-permute-done.16.refs_3_.refs_4_), channel_id=1, source_target_pairs={{0,1},{1,0},{2,3},{3,2},{4,5},{5,4},{6,7},{7,6},{8,9},{9,8},{10,11... | collective-permute-start | bytes 1572872 | tf_op jit(solution)/shard_map/ppermute | solution.py:543
  119.3 21.3 %collective-permute-start.18 = (s16[264,512]{1,0:T(8,128)(2,1)S(1)}, s16[264,512]{1,0:T(8,128)(2,1)S(1)}, u32[]{:S(2)}, u32[]{:S(2)}) collective-permute-start(s16[264,512]{1,0:T(8,128)(2,1)S(1)} %get-tuple-element.103), channel_id=1, source_target_pairs={{0,4},{2,6},{4,0},{6,2},{8,12},{10,14},{12,8},{14,10},{1,5},{3,7},... | collective-permute-start | bytes 811016 | tf_op jit(solution)/shard_map/ppermute | solution.py:354
  132.9 23.0 %collective-permute-start.23 = (s16[136,1024]{1,0:T(8,128)(2,1)S(1)}, s16[136,1024]{1,0:T(8,128)(2,1)S(1)}, u32[]{:S(2)}, u32[]{:S(2)}) collective-permute-start(s16[136,1024]{1,0:T(8,128)(2,1)S(1)} %shard_map.84), channel_id=1, source_target_pairs={{0,8},{2,10},{4,12},{6,14},{8,0},{10,2},{12,4},{14,6},{1,9},{3,11}... | collective-permute-start | bytes 835592 | tf_op jit(solution)/shard_map/ppermute | solution.py:393
  134.9 21.5 %collective-permute-start.22 = (s16[72,1024]{1,0:T(8,128)(2,1)S(1)}, s16[72,1024]{1,0:T(8,128)(2,1)S(1)}, u32[]{:S(2)}, u32[]{:S(2)}) collective-permute-start(s16[72,1024]{1,0:T(8,128)(2,1)S(1)} %get-tuple-element.108), channel_id=1, source_target_pairs={{0,2},{2,0},{4,6},{6,4},{8,10},{10,8},{12,14},{14,12},{1,3},{3,1},... | collective-permute-start | bytes 442376 | tf_op jit(solution)/shard_map/ppermute | solution.py:403
  137.8 13.6 %collective-permute-start.21 = (s16[264,512]{1,0:T(8,128)(2,1)S(1)}, s16[264,512]{1,0:T(8,128)(2,1)S(1)}, u32[]{:S(2)}, u32[]{:S(2)}) collective-permute-start(s16[264,512]{1,0:T(8,128)(2,1)S(1)} %get-tuple-element.110), channel_id=1, source_target_pairs={{0,4},{2,6},{4,0},{6,2},{8,12},{10,14},{12,8},{14,10},{1,5},{3,7},... | collective-permute-start | bytes 811016 | tf_op jit(solution)/shard_map/ppermute | solution.py:354
  140.8 11.4 %collective-permute-start.20 = (s16[136,512]{1,0:T(8,128)(2,1)S(1)}, s16[136,512]{1,0:T(8,128)(2,1)S(1)}, u32[]{:S(2)}, u32[]{:S(2)}) collective-permute-start(s16[136,512]{1,0:T(8,128)(2,1)S(1)} %shard_map.87), channel_id=1, source_target_pairs={{0,8},{2,10},{4,12},{6,14},{8,0},{10,2},{12,4},{14,6},{1,9},{3,11}... | collective-permute-start | bytes 417800 | tf_op jit(solution)/shard_map/ppermute | solution.py:393
  151.5 7.7 %collective-permute-start.25 = (s16[136,512]{1,0:T(8,128)(2,1)S(1)}, s16[136,512]{1,0:T(8,128)(2,1)S(1)}, u32[]{:S(2)}, u32[]{:S(2)}) collective-permute-start(s16[136,512]{1,0:T(8,128)(2,1)S(1)} %shard_map.88), channel_id=1, source_target_pairs={{0,8},{2,10},{4,12},{6,14},{8,0},{10,2},{12,4},{14,6},{1,9},{3,11}... | collective-permute-start | bytes 417800 | tf_op jit(solution)/shard_map/ppermute | solution.py:393
  152.3 7.9 %collective-permute-start.24 = (s16[72,512]{1,0:T(8,128)(2,1)S(1)}, s16[72,512]{1,0:T(8,128)(2,1)S(1)}, u32[]{:S(2)}, u32[]{:S(2)}) collective-permute-start(s16[72,512]{1,0:T(8,128)(2,1)S(1)} %get-tuple-element.118), channel_id=1, source_target_pairs={{0,2},{2,0},{4,6},{6,4},{8,10},{10,8},{12,14},{14,12},{1,3},{3,1},... | collective-permute-start | bytes 221192 | tf_op jit(solution)/shard_map/ppermute | solution.py:403
  156.3 5.5 %collective-permute-start.26 = (s16[72,1024]{1,0:T(8,128)(2,1)S(1)}, s16[72,1024]{1,0:T(8,128)(2,1)S(1)}, u32[]{:S(2)}, u32[]{:S(2)}) collective-permute-start(s16[72,1024]{1,0:T(8,128)(2,1)S(1)} %get-tuple-element.116), channel_id=1, source_target_pairs={{0,2},{2,0},{4,6},{6,4},{8,10},{10,8},{12,14},{14,12},{1,3},{3,1},... | collective-permute-start | bytes 442376 | tf_op jit(solution)/shard_map/ppermute | solution.py:403
  159.4 4.4 %collective-permute-start.27 = (s16[72,512]{1,0:T(8,128)(2,1)S(1)}, s16[72,512]{1,0:T(8,128)(2,1)S(1)}, u32[]{:S(2)}, u32[]{:S(2)}) collective-permute-start(s16[72,512]{1,0:T(8,128)(2,1)S(1)} %get-tuple-element.119), channel_id=1, source_target_pairs={{0,2},{2,0},{4,6},{6,4},{8,10},{10,8},{12,14},{14,12},{1,3},{3,1},... | collective-permute-start | bytes 221192 | tf_op jit(solution)/shard_map/ppermute | solution.py:403
  (36 other events, 201.7 us)
